TPU v7x, 32 devices: a whole 2x2x4 slice. The times are simulated.
32 devices in a mesh: mode: 4 (over y, x), cell: 8 (over z, core).
Axes of the slice: x: 2, y: 2, z: 4, core: 2. Of those that a mesh axis runs over, the one named last changes fastest.
Arguments:
- populations: float32 [2048, 1, 16, 128], P('mode', None, 'cell'), may hold values from -6 to 6
- contact_mask: int32 [1, 16, 128], P(None, 'cell'), may hold values 0 or 1
- octant: int32 [2048], P('mode'), may hold values from 0 to 7
- courant: float32 [3, 2048], P(None, 'mode'), may hold values from 0.03 to 0.3
- collision: bfloat16 [2048, 2048], P('mode'), as said below
Outputs:
- advanced: float32 [2048, 1, 16, 128], P('mode', None, 'cell')
Inputs may be any that keep to these rules, and one draw needn't show every extreme that they name: `collision`: diagonal entries between 0.1 and 0.6, off-diagonal ones small, all independent.
All inputs are finite; a program needn't handle non-finite values. No bound on the sum of `contact_mask` on one device may be relied on, other than what follows from the above.
Results may differ from a plain program's by a relative error of at most 0.0014.
Values may be sent and summed in bfloat16 or wider, within the bound.
No kernel may reach another device: no remote copies, remote signals or barrier semaphores. Data moves between devices by JAX's collectives and lax.ppermute only.
A program may use at most 64 MiB of HBM per device.

v0:
```python
import jax
import jax.numpy as jnp
from jax import lax
from jax.sharding import PartitionSpec as P


def with_halo(block, sides, width):
    for axis, dim in sides:
        count = lax.axis_size(axis)
        forward = [(i, i + 1) for i in range(count - 1)]
        backward = [(target, source) for source, target in forward]
        low = lax.ppermute(
            lax.slice_in_dim(block, block.shape[dim] - width, None, axis=dim), axis, forward
        )
        high = lax.ppermute(lax.slice_in_dim(block, 0, width, axis=dim), axis, backward)
        block = jnp.concatenate([low, block, high], axis=dim)
    return block


def velocities(octant, courant):
    bits = [octant % 2, octant // 2 % 2, octant // 4 % 2]
    return [(1.0 - 2.0 * bits[d].astype(jnp.float32)) * courant[d] for d in range(3)]


def advect(field, speeds):
    vx, vy, vz = [s[:, None, None, None] for s in speeds]
    back_x = jnp.roll(field, 1, axis=3)
    ahead_x = jnp.roll(field, -1, axis=3)
    padded_y = with_halo(field.astype(jnp.bfloat16), (("cell", 2),), 1).astype(field.dtype)
    padded_z = jnp.pad(field, ((0, 0), (1, 1), (0, 0), (0, 0)))
    total = jnp.maximum(vx, 0.0) * (field - back_x) + jnp.minimum(vx, 0.0) * (ahead_x - field)
    total = (
        total
        + jnp.maximum(vy, 0.0) * (field - padded_y[:, :, :-2])
        + jnp.minimum(vy, 0.0) * (padded_y[:, :, 2:] - field)
    )
    total = (
        total
        + jnp.maximum(vz, 0.0) * (field - padded_z[:, :-2])
        + jnp.minimum(vz, 0.0) * (padded_z[:, 2:] - field)
    )
    return total


def collide(field, collision):
    rounded = field.astype(jnp.bfloat16).reshape(field.shape[0], -1)
    result = jnp.dot(
        collision,
        lax.all_gather(rounded, "mode", axis=0, tiled=True),
        preferred_element_type=jnp.float32,
    )
    return result.reshape(field.shape)


def on_device(populations, contact_mask, octant, courant, collision):
    keep = (1 - contact_mask).astype(jnp.float32)[None]
    speeds = velocities(octant, courant)
    first = keep * populations
    second = keep * (first - advect(first, speeds) - collide(first, collision))
    final = second - advect(second, speeds) - collide(second, collision)
    return keep * (0.5 * first + 0.5 * final)


def solution(mesh):
    placed = (
        P("mode", None, "cell", None),
        P(None, "cell", None),
        P("mode"),
        P(None, "mode"),
        P("mode", None),
    )
    return jax.shard_map(
        on_device,
        mesh=mesh,
        in_specs=placed,
        out_specs=P("mode", None, "cell", None),
        check_vma=False,
    )
```

profile of v0, /device:TPU:1, one launch (start us, length us, event | category | flops | bytes accessed | tf_op | source)
XLA Modules:
  0.0 97.6 jit_solution(12619536808355774919)
XLA Ops:
  6.5 0.0 copy-start
  6.5 0.0 copy-start.1
  6.5 0.0 copy-start.3
  6.5 0.0 all-gather.3.cloned.1.call-start
  6.5 0.8 convert_bitcast_fusion
  7.4 1.3 %fusion.39 = (bf16[512,1,2,128]{3,2,1,0:T(2,128)(2,1)S(1)}, f32[512,1,2,128]{3,2,1,0:T(2,128)S(1)}) fusion(f32[512,1,2,128]{3,2,1,0:T(2,128)} %param.5, f32[2,128]{1,0:T(2,128)S(1)} %convert_bitcast_fusion), kind=kLoop, calls=%fused_computation.75 | loop fusion | flops 262144 | bytes 1311744 | tf_op jit(solution)/shard_map/convert_element_type | solution.py:29
  8.7 0.7 copy.13
  9.4 0.0 all-gather.3.cloned.1.call-update
  9.5 0.0 all-gather.5.cloned.1.call-start
  9.5 0.4 fusion.45
  9.9 2.0 %collective-permute-start.1 = (bf16[512,1,1,128]{3,2,1,0:T(2,128)(2,1)S(1)}, bf16[512,1,1,128]{3,2,1,0:T(2,128)(2,1)S(1)}, u32[]{:S(2)}, u32[]{:S(2)}) collective-permute-start(bf16[512,1,1,128]{3,2,1,0:T(2,128)(2,1)S(1)} %get-tuple-element.26), channel_id=1, source_target_pairs={{1,0},{2,1},{3,2},{4,3},{5,4},{6,5},{7,6},{9,8},{10,9},{11,10},{12... | collective-permute-start | bytes 393224 | tf_op jit(solution)/shard_map/ppermute | solution.py:15
  11.9 4.5 %collective-permute-start = (bf16[512,1,1,128]{3,2,1,0:T(2,128)(2,1)S(1)}, bf16[512,1,1,128]{3,2,1,0:T(2,128)(2,1)S(1)}, u32[]{:S(2)}, u32[]{:S(2)}) collective-permute-start(bf16[512,1,1,128]{3,2,1,0:T(2,128)(2,1)S(1)} %get-tuple-element.25), channel_id=1, source_target_pairs={{0,1},{1,2},{2,3},{3,4},{4,5},{5,6},{6,7},{8,9},{9,10},{10,11},{11... | collective-permute-start | bytes 393224 | tf_op jit(solution)/shard_map/ppermute | solution.py:12
  16.4 0.0 copy-done.1
  16.4 0.0 copy-done.3
  16.5 1.5 %fusion.42 = (f32[512,1,2,1]{3,2,1,0:T(2,128)}, f32[512,1,2,1]{3,2,1,0:T(2,128)}) fusion(f32[512,1,2,128]{3,2,1,0:T(2,128)S(1)} %get-tuple-element.14), kind=kLoop, calls=%fused_computation.78 | loop fusion | bytes 16384 | tf_op jit(solution)/shard_map/jit(_roll_static)/slice | solution.py:27
  18.0 1.5 %fusion.43 = (f32[512,1,2,127]{3,2,1,0:T(2,128)}, f32[512,1,2,127]{3,2,1,0:T(2,128)}) fusion(f32[512,1,2,128]{3,2,1,0:T(2,128)S(1)} %get-tuple-element.14), kind=kLoop, calls=%fused_computation.79 | loop fusion | bytes 2080768 | tf_op jit(solution)/shard_map/jit(_roll_static)/slice | solution.py:27
  19.6 0.0 collective-permute-done.1
  19.6 0.2 collective-permute-done
  19.7 1.8 %maximum_convert_fusion = f32[512,1,4,128]{3,2,1,0:T(4,128)} fusion(bf16[512,1,1,128]{3,2,1,0:T(2,128)(2,1)S(1)} %collective-permute-done.1, bf16[512,1,2,128]{3,2,1,0:T(2,128)(2,1)S(1)} %get-tuple-element.13, bf16[512,1,1,128]{3,2,1,0:T(2,128)(2,1)S(1)} %collective-permute-done), kind=kLoop, calls=%fused_computation.23 | loop fusion | flops 1572864 | bytes 1572864 | tf_op jit(solution)/shard_map/convert_element_type | solution.py:29
  21.5 16.8 %all-gather.3.cloned.1.call-done = bf16[2048,256]{1,0:T(8,128)(2,1)} async-done(((bf16[512,256]{1,0:T(8,128)(2,1)}), bf16[2048,256]{1,0:T(8,128)(2,1)}) %all-gather.3.cloned.1.call-update) | async-done | bytes 1048592 | tf_op jit(solution)/shard_map/all_gather | solution.py:49
  38.3 0.0 copy-done
  38.3 2.0 %fusion.47 = f32[256,512]{1,0:T(8,128)S(1)} fusion(bf16[2048,256]{1,0:T(8,128)(2,1)} %all-gather.3.cloned.1.call-done, bf16[512,2048]{1,0:T(8,128)(2,1)S(1)} %copy-done), kind=kOutput, calls=%fused_computation.83 | convolution fusion | flops 536870912 | bytes 3670016 | tf_op jit(solution)/shard_map/dot_general | solution.py:47
  40.3 1.0 %copy.6 = f32[512,1,2,128]{3,2,1,0:T(2,128)} copy(f32[512,1,2,128]{0,3,2,1:T(8,128)S(1)} %bitcast.31) | data formatting | bytes 1048576 | tf_op jit(solution)/shard_map/reshape | solution.py:52
  41.3 0.0 copy-start.2
  41.3 8.3 %fusion.35 = (bf16[512,1,2,128]{3,2,1,0:T(2,128)(2,1)S(1)}, f32[512,1,2,128]{3,2,1,0:T(2,128)S(1)}) fusion(f32[512,1,2,128]{3,2,1,0:T(2,128)} %copy.6, f32[512,1,2,128]{3,2,1,0:T(2,128)S(1)} %get-tuple-element.14, f32[512]{0:T(512)S(1)} %get-tuple-element.34, f32[512]{0:T(512)S(1)} %get-tuple-element.32, f32[512,1,4,128]{3,2,1,0:T(4,128)} %maximum_convert_fusion, ...), kind=kLoop, calls=%fused_computation.74 | loop fusion | flops 2883584 | bytes 3945472 | tf_op jit(solution)/shard_map/convert_element_type | solution.py:29
  49.6 0.7 copy.12
  50.4 0.0 all-gather.5.cloned.1.call-update
  50.4 0.0 copy-done.2
  50.4 0.4 fusion.44
  50.8 2.6 %collective-permute-start.3 = (bf16[512,1,1,128]{3,2,1,0:T(2,128)(2,1)S(1)}, bf16[512,1,1,128]{3,2,1,0:T(2,128)(2,1)S(1)}, u32[]{:S(2)}, u32[]{:S(2)}) collective-permute-start(bf16[512,1,1,128]{3,2,1,0:T(2,128)(2,1)S(1)} %get-tuple-element.24), channel_id=1, source_target_pairs={{1,0},{2,1},{3,2},{4,3},{5,4},{6,5},{7,6},{9,8},{10,9},{11,10},{12... | collective-permute-start | bytes 393224 | tf_op jit(solution)/shard_map/ppermute | solution.py:15
  53.4 3.0 %collective-permute-start.2 = (bf16[512,1,1,128]{3,2,1,0:T(2,128)(2,1)S(1)}, bf16[512,1,1,128]{3,2,1,0:T(2,128)(2,1)S(1)}, u32[]{:S(2)}, u32[]{:S(2)}) collective-permute-start(bf16[512,1,1,128]{3,2,1,0:T(2,128)(2,1)S(1)} %get-tuple-element.23), channel_id=1, source_target_pairs={{0,1},{1,2},{2,3},{3,4},{4,5},{5,6},{6,7},{8,9},{9,10},{10,11},{11... | collective-permute-start | bytes 393224 | tf_op jit(solution)/shard_map/ppermute | solution.py:12
  56.4 1.5 %fusion.40 = (f32[512,1,2,1]{3,2,1,0:T(2,128)}, f32[512,1,2,1]{3,2,1,0:T(2,128)}) fusion(f32[512,1,2,128]{3,2,1,0:T(2,128)S(1)} %get-tuple-element.6), kind=kLoop, calls=%fused_computation.76 | loop fusion | bytes 16384 | tf_op jit(solution)/shard_map/jit(_roll_static)/slice | solution.py:27
  57.9 1.5 %fusion.41 = (f32[512,1,2,127]{3,2,1,0:T(2,128)}, f32[512,1,2,127]{3,2,1,0:T(2,128)}) fusion(f32[512,1,2,128]{3,2,1,0:T(2,128)S(1)} %get-tuple-element.6), kind=kLoop, calls=%fused_computation.77 | loop fusion | bytes 2080768 | tf_op jit(solution)/shard_map/jit(_roll_static)/slice | solution.py:27
  59.5 0.0 collective-permute-done.3
  59.5 0.2 collective-permute-done.2
  59.7 1.8 %maximum_convert_fusion.1 = f32[512,1,4,128]{3,2,1,0:T(4,128)} fusion(bf16[512,1,1,128]{3,2,1,0:T(2,128)(2,1)S(1)} %collective-permute-done.3, bf16[512,1,2,128]{3,2,1,0:T(2,128)(2,1)S(1)} %get-tuple-element.5, bf16[512,1,1,128]{3,2,1,0:T(2,128)(2,1)S(1)} %collective-permute-done.2), kind=kLoop, calls=%fused_computation.29 | loop fusion | flops 1572864 | bytes 1572864 | tf_op jit(solution)/shard_map/convert_element_type | solution.py:29
  61.5 15.7 %all-gather.5.cloned.1.call-done = bf16[2048,256]{1,0:T(8,128)(2,1)} async-done(((bf16[512,256]{1,0:T(8,128)(2,1)}), bf16[2048,256]{1,0:T(8,128)(2,1)}) %all-gather.5.cloned.1.call-update) | async-done | bytes 1048592 | tf_op jit(solution)/shard_map/all_gather | solution.py:49
  77.2 2.8 %fusion.48 = f32[256,512]{1,0:T(8,128)} fusion(bf16[2048,256]{1,0:T(8,128)(2,1)} %all-gather.5.cloned.1.call-done, bf16[512,2048]{1,0:T(8,128)(2,1)S(1)} %copy-done), kind=kOutput, calls=%fused_computation.84 | convolution fusion | flops 536870912 | bytes 3670016 | tf_op jit(solution)/shard_map/dot_general | solution.py:47
  80.0 2.0 %copy.7 = f32[512,1,2,128]{3,2,1,0:T(2,128)} copy(f32[512,1,2,128]{0,3,2,1:T(8,128)} %bitcast.32) | data formatting | bytes 1048576 | tf_op jit(solution)/shard_map/reshape | solution.py:52
  82.0 8.8 %add_multiply_fusion = f32[512,1,2,128]{3,2,1,0:T(2,128)} fusion(f32[512,1,2,128]{3,2,1,0:T(2,128)S(1)} %get-tuple-element.14, f32[512,1,2,128]{3,2,1,0:T(2,128)} %copy.7, f32[512,1,2,128]{3,2,1,0:T(2,128)S(1)} %get-tuple-element.6, f32[512,1,4,128]{3,2,1,0:T(4,128)} %maximum_convert_fusion.1, f32[512,1,2,1]{3,2,1,0:T(2,128)} %get-tuple-element.16, ...), kind=kLoop, calls=%fused_computation.30 | loop fusion | flops 2883584 | bytes 4207616 | tf_op jit(solution)/shard_map/mul | solution.py:61
  (5 shorter events, 0.0 us)
Async XLA Ops:
  6.5 31.8 %copy-start = (bf16[512,2048]{1,0:T(8,128)(2,1)S(1)}, bf16[512,2048]{1,0:T(8,128)(2,1)}, u32[]{:S(2)}) copy-start(bf16[512,2048]{1,0:T(8,128)(2,1)} %param.9) | copy-start | bytes 6291460
  6.5 9.9 %copy-start.1 = (f32[3,512]{1,0:T(4,128)S(1)}, f32[3,512]{1,0:T(4,128)}, u32[]{:S(2)}) copy-start(f32[3,512]{1,0:T(4,128)} %param.8) | copy-start | bytes 18436
  6.5 9.9 %copy-start.3 = (s32[512]{0:T(512)S(1)}, s32[512]{0:T(512)}, u32[]{:S(2)}) copy-start(s32[512]{0:T(512)} %param.7) | copy-start | bytes 6148
  6.5 31.8 %all-gather.3.cloned.1.call-start = ((), (), s32[]{:S(2)}) async-start(), calls=%async_computation | async-start | bytes 1310720 | tf_op jit(solution)/shard_map/all_gather | solution.py:49
  9.5 67.7 %all-gather.5.cloned.1.call-start = ((), (), s32[]{:S(2)}) async-start(), calls=%async_computation.1 | async-start | bytes 1310720 | tf_op jit(solution)/shard_map/all_gather | solution.py:49
  9.9 9.7 %collective-permute-start.1 = (bf16[512,1,1,128]{3,2,1,0:T(2,128)(2,1)S(1)}, bf16[512,1,1,128]{3,2,1,0:T(2,128)(2,1)S(1)}, u32[]{:S(2)}, u32[]{:S(2)}) collective-permute-start(bf16[512,1,1,128]{3,2,1,0:T(2,128)(2,1)S(1)} %get-tuple-element.26), channel_id=1, source_target_pairs={{1,0},{2,1},{3,2},{4,3},{5,4},{6,5},{7,6},{9,8},{10,9},{11,10},{12... | collective-permute-start | bytes 393224 | tf_op jit(solution)/shard_map/ppermute | solution.py:15
  11.9 7.9 %collective-permute-start = (bf16[512,1,1,128]{3,2,1,0:T(2,128)(2,1)S(1)}, bf16[512,1,1,128]{3,2,1,0:T(2,128)(2,1)S(1)}, u32[]{:S(2)}, u32[]{:S(2)}) collective-permute-start(bf16[512,1,1,128]{3,2,1,0:T(2,128)(2,1)S(1)} %get-tuple-element.25), channel_id=1, source_target_pairs={{0,1},{1,2},{2,3},{3,4},{4,5},{5,6},{6,7},{8,9},{9,10},{10,11},{11... | collective-permute-start | bytes 393224 | tf_op jit(solution)/shard_map/ppermute | solution.py:12
  41.3 9.1 %copy-start.2 = (s32[1,2,128]{2,1,0:T(2,128)S(1)}, s32[1,2,128]{2,1,0:T(2,128)}, u32[]{:S(2)}) copy-start(s32[1,2,128]{2,1,0:T(2,128)} %param.6) | copy-start | bytes 3076
  50.8 8.7 %collective-permute-start.3 = (bf16[512,1,1,128]{3,2,1,0:T(2,128)(2,1)S(1)}, bf16[512,1,1,128]{3,2,1,0:T(2,128)(2,1)S(1)}, u32[]{:S(2)}, u32[]{:S(2)}) collective-permute-start(bf16[512,1,1,128]{3,2,1,0:T(2,128)(2,1)S(1)} %get-tuple-element.24), channel_id=1, source_target_pairs={{1,0},{2,1},{3,2},{4,3},{5,4},{6,5},{7,6},{9,8},{10,9},{11,10},{12... | collective-permute-start | bytes 393224 | tf_op jit(solution)/shard_map/ppermute | solution.py:15
  53.4 6.3 %collective-permute-start.2 = (bf16[512,1,1,128]{3,2,1,0:T(2,128)(2,1)S(1)}, bf16[512,1,1,128]{3,2,1,0:T(2,128)(2,1)S(1)}, u32[]{:S(2)}, u32[]{:S(2)}) collective-permute-start(bf16[512,1,1,128]{3,2,1,0:T(2,128)(2,1)S(1)} %get-tuple-element.23), channel_id=1, source_target_pairs={{0,1},{1,2},{2,3},{3,4},{4,5},{5,6},{6,7},{8,9},{9,10},{10,11},{11... | collective-permute-start | bytes 393224 | tf_op jit(solution)/shard_map/ppermute | solution.py:12
Sparse Core Ops, SparseCore 0:
  9.6 28.6 all-gather.2
  50.5 26.6 all-gather.4
where the time goes:
time: 99 us; the launch traced here: 97.6 us
  waiting for transfers between devices  32.9 us (33%)
  other arithmetic  22.9 us (23%)
  between operations  13.5 us (14%)
  starting transfers between devices  12.2 us (12%)
  local copies, waits for them, and re-layouts  11.4 us (12%)
  matrix products  4.74 us (5%)
    all_gather x2, waiting for transfers between devices, collide(): lax.all_gather(rounded, 'mode', axis=0, tiled=True)  32.5 us
    mul x3, other arithmetic, on_device(): return keep * (0.5 * first + 0.5 * final)  9.65 us
    convert_element_type x2, other arithmetic, advect(): field.astype(jnp.bfloat16)  9.65 us
    ppermute x2, starting transfers between devices, with_halo(): lax.ppermute(lax.slice_in_dim(block, block.shape[dim] - width, None, axis...  7.56 us
    slice x4, local copies, waits for them, and re-layouts, advect(): back_x = jnp.roll(field, 1, axis=3)  6.11 us
    dot_general x2, matrix products, collide(): jnp.dot(collision, lax.all_gather(rounded, 'mode', axis=0, tiled=True), p...  4.74 us
    ppermute x2, starting transfers between devices, with_halo(): lax.ppermute(lax.slice_in_dim(block, 0, width, axis=dim), axis, backward)  4.55 us
    convert_element_type x2, other arithmetic, advect(): with_halo(field.astype(jnp.bfloat16), (('cell', 2),), 1).astype(field.dtype)  3.59 us
  transfers between devices with their start and end apart: 6, of which 4 were waited for; matrix products, arithmetic and copies ran while one was open for 11% of the time, Pallas kernels for 0%

commit v1 on v0

v1 whole, which is shorter than its diff:
```python
import functools

import jax
import jax.numpy as jnp
from jax import lax
from jax.experimental import pallas as pl
from jax.experimental.pallas import tpu as pltpu
from jax.sharding import PartitionSpec as P

F32 = jnp.float32
BF16 = jnp.bfloat16
VMEM = pl.BlockSpec(memory_space=pltpu.VMEM)


def call(body, outs, args, flops=0):
    total = sum(a.size * a.dtype.itemsize for a in (*outs, *args))
    return pl.pallas_call(
        body,
        out_shape=outs,
        in_specs=[VMEM] * len(args),
        out_specs=[VMEM] * len(outs),
        compiler_params=pltpu.CompilerParams(vmem_limit_bytes=24 * 2**20),
        cost_estimate=pl.CostEstimate(flops=flops, bytes_accessed=total, transcendentals=0),
    )(*args)


def shape(dims, dtype):
    return jax.ShapeDtypeStruct(dims, dtype)


def masked_rows(pop_ref, mask_ref, rows):
    modes = pop_ref.shape[0] // rows
    keep = (1 - mask_ref[...]).astype(F32)
    return [keep[r : r + 1] * pop_ref[pl.ds(r, modes, stride=rows), :] for r in range(rows)]


def prepare(rows, pop_ref, mask_ref, octant_ref, courant_ref, *outs):
    *q_refs, coef_ref = outs
    for q_ref, row in zip(q_refs, masked_rows(pop_ref, mask_ref, rows)):
        q_ref[...] = row.astype(BF16)
    octant = octant_ref[...]
    signs = [1.0 - 2.0 * ((octant >> d) & 1).astype(F32) for d in range(3)]
    speeds = [signs[d] * courant_ref[d : d + 1] for d in range(3)]
    table = jnp.concatenate(
        [jnp.abs(v) for v in speeds] + [(v < 0).astype(F32) for v in speeds] + [speeds[0] * 0.0] * 2, axis=0
    )
    coef_ref[...] = table.T


def product(c_ref, offset, blocks):
    modes = blocks[0].shape[0]
    position = lax.axis_index("mode") ^ offset
    columns = pl.ds(pl.multiple_of(position * modes, modes), modes)
    return jnp.dot(c_ref[:, columns], jnp.concatenate(blocks, axis=1), preferred_element_type=F32)


def local_terms(rows, fields, q_refs, coef_ref, c_ref):
    width = fields[0].shape[1]
    ax, ay, az = (coef_ref[:, d : d + 1] for d in range(3))
    neg_x, neg_y = (coef_ref[:, d : d + 1] > 0 for d in (3, 4))
    own = product(c_ref, 0, [q[...] for q in q_refs])
    stay = 1.0 - (ax + ay + az)
    results = []
    for r, p in enumerate(fields):
        beside = jnp.where(neg_x, pltpu.roll(p, width - 1, 1), pltpu.roll(p, 1, 1))
        low = fields[r - 1] if r > 0 else jnp.zeros_like(p)
        high = fields[r + 1] if r < rows - 1 else jnp.zeros_like(p)
        results.append(stay * p + ax * beside + ay * jnp.where(neg_y, high, low) - own[:, r * width : (r + 1) * width])
    return results


def remote_terms(rows, offsets, width, received, halos, coef_ref, c_ref):
    ay = coef_ref[:, 1:2]
    neg_y = coef_ref[:, 4:5] > 0
    low, high = (h[...].astype(F32) for h in halos)
    total = None
    for i, offset in enumerate(offsets):
        term = product(c_ref, offset, [received[r][i][...] for r in range(rows)])
        total = term if total is None else total + term
    results = [-total[:, r * width : (r + 1) * width] for r in range(rows)]
    results[0] = results[0] + jnp.where(neg_y, 0.0, ay * low)
    results[-1] = results[-1] + jnp.where(neg_y, ay * high, 0.0)
    return results


def first_local(rows, *refs):
    pop_ref, mask_ref, coef_ref, c_ref, *rest = refs
    q_refs, base_ref = rest[:rows], rest[rows]
    fields = masked_rows(pop_ref, mask_ref, rows)
    for r, value in enumerate(local_terms(rows, fields, q_refs, coef_ref, c_ref)):
        base_ref[r] = value


def first_end(rows, offsets, *refs):
    base_ref, mask_ref, coef_ref, c_ref, low, high, *rest = refs
    n = len(offsets)
    received = [rest[r * n : (r + 1) * n] for r in range(rows)]
    *q_refs, p1_ref = rest[rows * n :]
    keep = (1 - mask_ref[...]).astype(F32)
    width = keep.shape[1]
    for r, term in enumerate(remote_terms(rows, offsets, width, received, (low, high), coef_ref, c_ref)):
        value = keep[r : r + 1] * (base_ref[r] + term)
        p1_ref[r] = value
        q_refs[r][...] = value.astype(BF16)


def second_local(rows, *refs):
    pop_ref, mask_ref, p1_ref, coef_ref, c_ref, *rest = refs
    q_refs, base_ref = rest[:rows], rest[rows]
    first = masked_rows(pop_ref, mask_ref, rows)
    fields = [p1_ref[r] for r in range(rows)]
    for r, value in enumerate(local_terms(rows, fields, q_refs, coef_ref, c_ref)):
        base_ref[r] = 0.5 * first[r] + 0.5 * value


def second_end(rows, offsets, *refs):
    base_ref, mask_ref, coef_ref, c_ref, low, high, *rest = refs
    n = len(offsets)
    received = [rest[r * n : (r + 1) * n] for r in range(rows)]
    out_ref = rest[rows * n]
    keep = (1 - mask_ref[...]).astype(F32)
    width = keep.shape[1]
    modes = out_ref.shape[0] // rows
    for r, term in enumerate(remote_terms(rows, offsets, width, received, (low, high), coef_ref, c_ref)):
        out_ref[pl.ds(r, modes, stride=rows), :] = keep[r : r + 1] * (base_ref[r] + 0.5 * term)


def exchange(q, count):
    bits = [1 << b for b in range(count.bit_length() - 1)]
    gathered = []
    for r, row in enumerate(q):
        held = {0: row}
        for bit in bits if r % 2 == 0 else bits[::-1]:
            pairs = [(i, i ^ bit) for i in range(count)]
            held |= {o ^ bit: lax.ppermute(b, "mode", pairs) for o, b in held.items()}
        gathered.append(held)
    return gathered


def halo(q):
    count = lax.axis_size("cell")
    forward = [(i, i + 1) for i in range(count - 1)]
    backward = [(target, source) for source, target in forward]
    return lax.ppermute(q[-1], "cell", forward), lax.ppermute(q[0], "cell", backward)


def on_device(populations, contact_mask, octant, courant, collision):
    modes, planes, rows, width = populations.shape
    assert planes == 1
    count = lax.axis_size("mode")
    offsets = list(range(1, count))
    pop = populations.reshape(modes * rows, width)
    mask = contact_mask.reshape(rows, width)
    row_bf16 = shape((modes, width), BF16)
    all_rows = shape((rows, modes, width), F32)
    flops = 2 * modes * modes * rows * width

    *q, coef = call(
        functools.partial(prepare, rows),
        [row_bf16] * rows + [shape((modes, 8), F32)],
        [pop, mask, octant.reshape(1, modes), courant],
    )
    low, high = halo(q)
    gathered = exchange(q, count)
    (base,) = call(
        functools.partial(first_local, rows), [all_rows], [pop, mask, coef, collision, *q], flops=flops
    )
    blocks = [g[o] for g in gathered for o in offsets]
    *q, p1 = call(
        functools.partial(first_end, rows, offsets),
        [row_bf16] * rows + [all_rows],
        [base, mask, coef, collision, low, high, *blocks],
        flops=flops * len(offsets),
    )
    low, high = halo(q)
    gathered = exchange(q, count)
    (base,) = call(
        functools.partial(second_local, rows), [all_rows], [pop, mask, p1, coef, collision, *q], flops=flops
    )
    blocks = [g[o] for g in gathered for o in offsets]
    (out,) = call(
        functools.partial(second_end, rows, offsets),
        [shape((modes * rows, width), F32)],
        [base, mask, coef, collision, low, high, *blocks],
        flops=flops * len(offsets),
    )
    return out.reshape(populations.shape)


def solution(mesh):
    placed = (
        P("mode", None, "cell", None),
        P(None, "cell", None),
        P("mode"),
        P(None, "mode"),
        P("mode", None),
    )
    return jax.shard_map(
        on_device,
        mesh=mesh,
        in_specs=placed,
        out_specs=P("mode", None, "cell", None),
        check_vma=False,
    )
```

time: 99 us -> 37.1 us (0.37)
  waiting for transfers between devices: 32.9 us -> 2.81 us
  other arithmetic: 22.9 us -> 0 us
  between operations: 13.5 us -> 0.18 us
  starting transfers between devices: 12.2 us -> 25 us
  local copies, waits for them, and re-layouts: 11.4 us -> 4.7 us
  matrix products: 4.74 us -> 0 us
  Pallas kernels: 0 us -> 4.08 us
    all_gather x2 -> x0, waiting for transfers between devices: 32.5 us -> none  [collide(): lax.all_gather(rounded, 'mode', axis=0, tiled=True)]
    convert_element_type x4 -> x0, other arithmetic: 13.2 us -> none  [the longest x2 9.65 us: advect(): field.astype(jnp.bfloat16)]
    ppermute x4 -> x16, starting transfers between devices: 12.1 us -> 25 us  [the longest x12 11.1 us: exchange(): held |= {o ^ bit: lax.ppermute(b, 'mode', pairs) for o, b in held.items()}]
    mul x3 -> x0, other arithmetic: 9.65 us -> none  [on_device(): return keep * (0.5 * first + 0.5 * final)]
    slice x7 -> x0, local copies, waits for them, and re-layouts: 6.85 us -> none  [the longest x4 6.11 us: advect(): back_x = jnp.roll(field, 1, axis=3)]
    dot_general x2 -> x0, matrix products: 4.74 us -> none  [collide(): jnp.dot(collision, lax.all_gather(rounded, 'mode', axis=0, tiled=True), p...]
    pallas_call x0 -> x5, Pallas kernels: none -> 4.08 us  [call(): pl.pallas_call(body, out_shape=outs, in_specs=[VMEM] * len(args), out_spe...]
    unnamed x10 -> x14, local copies, waits for them, and re-layouts: 1.49 us -> 4.7 us
  transfers between devices with their start and end apart: 6 -> 16, of which waited for: 4 -> 3; matrix products, arithmetic and copies ran while one was open for 11% -> 0% of each run, Pallas kernels for 0% -> 5%
where the time goes in v1:
time: 37.1 us; the launch traced here: 36.7 us
  starting transfers between devices  25 us (67%)
  local copies, waits for them, and re-layouts  4.7 us (13%)
  Pallas kernels  4.08 us (11%)
  waiting for transfers between devices  2.81 us (8%)
    ppermute x12, starting transfers between devices, exchange(): held |= {o ^ bit: lax.ppermute(b, 'mode', pairs) for o, b in held.items()}  11.1 us
    ppermute x2, starting transfers between devices, halo(): lax.ppermute(q[-1], 'cell', forward)  7.57 us
    ppermute x2, starting transfers between devices, halo(): lax.ppermute(q[0], 'cell', backward)  6.33 us
    unnamed x14, local copies, waits for them, and re-layouts  4.7 us
    pallas_call x5, Pallas kernels, call(): pl.pallas_call(body, out_shape=outs, in_specs=[VMEM] * len(args), out_spe...  4.08 us
    ppermute x12, waiting for transfers between devices, exchange(): held |= {o ^ bit: lax.ppermute(b, 'mode', pairs) for o, b in held.items()}  2.8 us
  transfers between devices with their start and end apart: 16, of which 3 were waited for; matrix products, arithmetic and copies ran while one was open for 0% of the time, Pallas kernels for 5%

profile of v1, /device:TPU:1, one launch (start us, length us, event | category | flops | bytes accessed | tf_op | source)
XLA Modules:
  0.0 36.7 jit_solution(15535042311882416496)
XLA Ops:
  0.0 0.0 copy-start.2
  0.0 1.0 %copy-done.2 = f32[512,1,2,128]{3,2,1,0:T(2,128)S(1)} copy-done((f32[512,1,2,128]{3,2,1,0:T(2,128)S(1)}, f32[512,1,2,128]{3,2,1,0:T(2,128)}, u32[]{:S(2)}) %copy-start.2) | copy-done | bytes 524312
  1.0 0.0 copy-start.4
  1.0 0.7 %copy-done.4 = s32[1,2,128]{2,1,0:T(2,128)S(1)} copy-done((s32[1,2,128]{2,1,0:T(2,128)S(1)}, s32[1,2,128]{2,1,0:T(2,128)}, u32[]{:S(2)}) %copy-start.4) | copy-done | bytes 1048
  1.7 0.0 copy-start.5
  1.7 0.7 %copy-done.5 = f32[3,512]{1,0:T(4,128)S(1)} copy-done((f32[3,512]{1,0:T(4,128)S(1)}, f32[3,512]{1,0:T(4,128)}, u32[]{:S(2)}) %copy-start.5) | copy-done | bytes 6168
  2.4 0.0 copy-start.6
  2.4 0.7 %copy-done.6 = s32[512]{0:T(512)S(1)} copy-done((s32[512]{0:T(512)S(1)}, s32[512]{0:T(512)}, u32[]{:S(2)}) %copy-start.6) | copy-done | bytes 2072
  3.1 0.1 shard_map.55
  3.2 2.1 %collective-permute-start.3 = (bf16[512,128]{1,0:T(8,128)(2,1)S(1)}, bf16[512,128]{1,0:T(8,128)(2,1)S(1)}, u32[]{:S(2)}, u32[]{:S(2)}) collective-permute-start(bf16[512,128]{1,0:T(8,128)(2,1)S(1)} %get-tuple-element.12.refs_4_), channel_id=1, source_target_pairs={{0,16},{8,24},{16,0},{24,8},{1,17},{9,25},{17,1},{25,9},{2,18},{10... | collective-permute-start | bytes 393224 | tf_op jit(solution)/shard_map/ppermute | solution.py:135
  5.4 1.2 %collective-permute-start.2 = (bf16[512,128]{1,0:T(8,128)(2,1)S(1)}, bf16[512,128]{1,0:T(8,128)(2,1)S(1)}, u32[]{:S(2)}, u32[]{:S(2)}) collective-permute-start(bf16[512,128]{1,0:T(8,128)(2,1)S(1)} %get-tuple-element.12.refs_4_), channel_id=1, source_target_pairs={{0,8},{8,0},{16,24},{24,16},{1,9},{9,1},{17,25},{25,17},{2,10},{10... | collective-permute-start | bytes 393224 | tf_op jit(solution)/shard_map/ppermute | solution.py:135
  6.6 0.2 collective-permute-start.6
  6.8 3.4 %collective-permute-start.1 = (bf16[512,128]{1,0:T(8,128)(2,1)S(1)}, bf16[512,128]{1,0:T(8,128)(2,1)S(1)}, u32[]{:S(2)}, u32[]{:S(2)}) collective-permute-start(bf16[512,128]{1,0:T(8,128)(2,1)S(1)} %get-tuple-element.12.refs_4_), channel_id=1, source_target_pairs={{1,0},{2,1},{3,2},{4,3},{5,4},{6,5},{7,6},{9,8},{10,9},{11,10},{12... | collective-permute-start | bytes 393224 | tf_op jit(solution)/shard_map/ppermute | solution.py:144
  10.2 0.1 collective-permute-start.5
  10.3 0.0 collective-permute-done.3.refs_7_
  10.3 3.6 %collective-permute-start = (bf16[512,128]{1,0:T(8,128)(2,1)S(1)}, bf16[512,128]{1,0:T(8,128)(2,1)S(1)}, u32[]{:S(2)}, u32[]{:S(2)}) collective-permute-start(bf16[512,128]{1,0:T(8,128)(2,1)S(1)} %get-tuple-element.13.refs_5_), channel_id=1, source_target_pairs={{0,1},{1,2},{2,3},{3,4},{4,5},{5,6},{6,7},{8,9},{9,10},{10,11},{11... | collective-permute-start | bytes 393224 | tf_op jit(solution)/shard_map/ppermute | solution.py:144
  13.9 0.0 collective-permute-done.2.refs_6_
  14.0 1.6 %collective-permute-start.4 = (bf16[512,128]{1,0:T(8,128)(2,1)S(1)}, bf16[512,128]{1,0:T(8,128)(2,1)S(1)}, u32[]{:S(2)}, u32[]{:S(2)}) collective-permute-start(bf16[512,128]{1,0:T(8,128)(2,1)S(1)} %collective-permute-done.2.refs_6_), channel_id=1, source_target_pairs={{0,16},{8,24},{16,0},{24,8},{1,17},{9,25},{17,1},{25,9},{2,18},{10... | collective-permute-start | bytes 393224 | tf_op jit(solution)/shard_map/ppermute | solution.py:135
  15.6 0.0 collective-permute-done.6.refs_10_
  15.6 1.2 %collective-permute-start.7 = (bf16[512,128]{1,0:T(8,128)(2,1)S(1)}, bf16[512,128]{1,0:T(8,128)(2,1)S(1)}, u32[]{:S(2)}, u32[]{:S(2)}) collective-permute-start(bf16[512,128]{1,0:T(8,128)(2,1)S(1)} %collective-permute-done.6.refs_10_), channel_id=1, source_target_pairs={{0,8},{8,0},{16,24},{24,16},{1,9},{9,1},{17,25},{25,17},{2,10},{10... | collective-permute-start | bytes 393224 | tf_op jit(solution)/shard_map/ppermute | solution.py:135
  16.8 0.0 copy-start
  16.8 1.6 %copy-done = bf16[512,2048]{1,0:T(8,128)(2,1)S(1)} copy-done((bf16[512,2048]{1,0:T(8,128)(2,1)S(1)}, bf16[512,2048]{1,0:T(8,128)(2,1)}, u32[]{:S(2)}) %copy-start) | copy-done | bytes 2097176
  18.4 0.0 copy-start.1
  18.4 0.9 %shard_map.56.refs_0_ = f32[2,512,128]{2,1,0:T(8,128)S(1)} custom-call(f32[1024,128]{1,0:T(8,128)S(1)} %bitcast.7, s32[2,128]{1,0:T(2,128)S(1)} %bitcast.10, f32[512,8]{1,0:T(8,128)S(1)} %get-tuple-element.11.refs_2_.refs_3_, bf16[512,2048]{1,0:T(8,128)(2,1)S(1)} %copy-done, bf16[512,128]{1,0:T(8,128)(2,1)S(1)} %get-tuple-element.12.refs_4_, ...), custom_call_target="tpu_custom_call" | custom-call | flops 134217728 | bytes 3425280 | tf_op jit(solution)/shard_map/pallas_call | solution.py:17
  19.4 0.0 copy-start.3
  19.4 0.0 collective-permute-done.1.refs_5_
  19.4 0.0 collective-permute-done.5.refs_9_
  19.4 0.0 collective-permute-done.refs_4_
  19.4 0.0 collective-permute-done.4.refs_8_
  19.4 0.9 %collective-permute-done.7.refs_11_ = bf16[512,128]{1,0:T(8,128)(2,1)S(1)} collective-permute-done((bf16[512,128]{1,0:T(8,128)(2,1)S(1)}, bf16[512,128]{1,0:T(8,128)(2,1)S(1)}, u32[]{:S(2)}, u32[]{:S(2)}) %collective-permute-start.7) | collective-permute-done | bytes 131104 | tf_op jit(solution)/shard_map/ppermute | solution.py:135
  20.3 0.0 copy-done.1
  20.3 0.6 %shard_map.57 = (bf16[512,128]{1,0:T(8,128)(2,1)S(1)}, bf16[512,128]{1,0:T(8,128)(2,1)S(1)}, f32[2,512,128]{2,1,0:T(8,128)S(1)}) custom-call(f32[2,512,128]{2,1,0:T(8,128)S(1)} %shard_map.56.refs_0_, s32[2,128]{1,0:T(2,128)S(1)} %bitcast.11, f32[512,8]{1,0:T(8,128)S(1)} %get-tuple-element.11.refs_2_.refs_3_, bf16[512,2048]{1,0:T(8,128)(2,1)S(1)} %copy-done.1, ...), custom_call_target="tpu_custom_call" | custom-call | flops 402653184 | bytes 4473856 | tf_op jit(solution)/shard_map/pallas_call | solution.py:17
  20.9 0.1 collective-permute-start.11
  21.0 1.4 %collective-permute-start.10 = (bf16[512,128]{1,0:T(8,128)(2,1)S(1)}, bf16[512,128]{1,0:T(8,128)(2,1)S(1)}, u32[]{:S(2)}, u32[]{:S(2)}) collective-permute-start(bf16[512,128]{1,0:T(8,128)(2,1)S(1)} %get-tuple-element.15.refs_5_), channel_id=1, source_target_pairs={{0,8},{8,0},{16,24},{24,16},{1,9},{9,1},{17,25},{25,17},{2,10},{10... | collective-permute-start | bytes 393224 | tf_op jit(solution)/shard_map/ppermute | solution.py:135
  22.4 1.2 %collective-permute-start.14 = (bf16[512,128]{1,0:T(8,128)(2,1)S(1)}, bf16[512,128]{1,0:T(8,128)(2,1)S(1)}, u32[]{:S(2)}, u32[]{:S(2)}) collective-permute-start(bf16[512,128]{1,0:T(8,128)(2,1)S(1)} %get-tuple-element.16.refs_6_), channel_id=1, source_target_pairs={{0,16},{8,24},{16,0},{24,8},{1,17},{9,25},{17,1},{25,9},{2,18},{10... | collective-permute-start | bytes 393224 | tf_op jit(solution)/shard_map/ppermute | solution.py:135
  23.6 2.9 %collective-permute-start.9 = (bf16[512,128]{1,0:T(8,128)(2,1)S(1)}, bf16[512,128]{1,0:T(8,128)(2,1)S(1)}, u32[]{:S(2)}, u32[]{:S(2)}) collective-permute-start(bf16[512,128]{1,0:T(8,128)(2,1)S(1)} %get-tuple-element.15.refs_5_), channel_id=1, source_target_pairs={{1,0},{2,1},{3,2},{4,3},{5,4},{6,5},{7,6},{9,8},{10,9},{11,10},{12... | collective-permute-start | bytes 393224 | tf_op jit(solution)/shard_map/ppermute | solution.py:144
  26.5 0.3 collective-permute-start.13
  26.9 0.0 collective-permute-done.11.refs_7_
  26.9 4.0 %collective-permute-start.8 = (bf16[512,128]{1,0:T(8,128)(2,1)S(1)}, bf16[512,128]{1,0:T(8,128)(2,1)S(1)}, u32[]{:S(2)}, u32[]{:S(2)}) collective-permute-start(bf16[512,128]{1,0:T(8,128)(2,1)S(1)} %get-tuple-element.16.refs_6_), channel_id=1, source_target_pairs={{0,1},{1,2},{2,3},{3,4},{4,5},{5,6},{6,7},{8,9},{9,10},{10,11},{11... | collective-permute-start | bytes 393224 | tf_op jit(solution)/shard_map/ppermute | solution.py:144
  30.8 0.0 collective-permute-done.10.refs_6_
  30.8 0.1 collective-permute-start.12
  30.9 0.0 collective-permute-done.14.refs_10_
  30.9 1.4 %collective-permute-start.15 = (bf16[512,128]{1,0:T(8,128)(2,1)S(1)}, bf16[512,128]{1,0:T(8,128)(2,1)S(1)}, u32[]{:S(2)}, u32[]{:S(2)}) collective-permute-start(bf16[512,128]{1,0:T(8,128)(2,1)S(1)} %collective-permute-done.14.refs_10_), channel_id=1, source_target_pairs={{0,8},{8,0},{16,24},{24,16},{1,9},{9,1},{17,25},{25,17},{2,10},{10... | collective-permute-start | bytes 393224 | tf_op jit(solution)/shard_map/ppermute | solution.py:135
  32.4 0.0 copy-done.3
  32.4 1.0 %shard_map.58.refs_0_ = f32[2,512,128]{2,1,0:T(8,128)S(1)} custom-call(f32[1024,128]{1,0:T(8,128)S(1)} %bitcast.8, s32[2,128]{1,0:T(2,128)S(1)} %bitcast.12, f32[2,512,128]{2,1,0:T(8,128)S(1)} %get-tuple-element.14.refs_2_, f32[512,8]{1,0:T(8,128)S(1)} %get-tuple-element.11.refs_2_.refs_3_, bf16[512,2048]{1,0:T(8,128)(2,1)S(1)} %copy-done.1, ...), custom_call_target="tpu_custom_call" | custom-call | flops 134217728 | bytes 3949568 | tf_op jit(solution)/shard_map/pallas_call | solution.py:17
  33.4 0.0 collective-permute-done.9.refs_5_
  33.4 0.0 collective-permute-done.13.refs_9_
  33.4 0.0 collective-permute-done.8.refs_4_
  33.4 1.6 %collective-permute-done.12.refs_8_ = bf16[512,128]{1,0:T(8,128)(2,1)S(1)} collective-permute-done((bf16[512,128]{1,0:T(8,128)(2,1)S(1)}, bf16[512,128]{1,0:T(8,128)(2,1)S(1)}, u32[]{:S(2)}, u32[]{:S(2)}) %collective-permute-start.12) | collective-permute-done | bytes 131104 | tf_op jit(solution)/shard_map/ppermute | solution.py:135
  35.0 0.3 collective-permute-done.15.refs_11_
  35.3 1.4 %shard_map.59 = f32[1024,128]{1,0:T(8,128)} custom-call(f32[2,512,128]{2,1,0:T(8,128)S(1)} %shard_map.58.refs_0_, s32[2,128]{1,0:T(2,128)S(1)} %bitcast.13, f32[512,8]{1,0:T(8,128)S(1)} %get-tuple-element.11.refs_2_.refs_3_, bf16[512,2048]{1,0:T(8,128)(2,1)S(1)} %copy-done.1, bf16[512,128]{1,0:T(8,128)(2,1)S(1)} %collective-permute-done.8.refs_4_, ...), custom_call_target="tpu_custom_call" | custom-call | flops 402653184 | bytes 4211712 | tf_op jit(solution)/shard_map/pallas_call | solution.py:17
Async XLA Ops:
  0.0 1.0 %copy-start.2 = (f32[512,1,2,128]{3,2,1,0:T(2,128)S(1)}, f32[512,1,2,128]{3,2,1,0:T(2,128)}, u32[]{:S(2)}) copy-start(f32[512,1,2,128]{3,2,1,0:T(2,128)} %param.5) | copy-start | bytes 1572868
  1.0 0.7 %copy-start.4 = (s32[1,2,128]{2,1,0:T(2,128)S(1)}, s32[1,2,128]{2,1,0:T(2,128)}, u32[]{:S(2)}) copy-start(s32[1,2,128]{2,1,0:T(2,128)} %param.6) | copy-start | bytes 3076
  1.7 0.7 %copy-start.5 = (f32[3,512]{1,0:T(4,128)S(1)}, f32[3,512]{1,0:T(4,128)}, u32[]{:S(2)}) copy-start(f32[3,512]{1,0:T(4,128)} %courant_ref.1) | copy-start | bytes 18436
  2.4 0.7 %copy-start.6 = (s32[512]{0:T(512)S(1)}, s32[512]{0:T(512)}, u32[]{:S(2)}) copy-start(s32[512]{0:T(512)} %param.7) | copy-start | bytes 6148
  3.2 7.1 %collective-permute-start.3 = (bf16[512,128]{1,0:T(8,128)(2,1)S(1)}, bf16[512,128]{1,0:T(8,128)(2,1)S(1)}, u32[]{:S(2)}, u32[]{:S(2)}) collective-permute-start(bf16[512,128]{1,0:T(8,128)(2,1)S(1)} %get-tuple-element.12.refs_4_), channel_id=1, source_target_pairs={{0,16},{8,24},{16,0},{24,8},{1,17},{9,25},{17,1},{25,9},{2,18},{10... | collective-permute-start | bytes 393224 | tf_op jit(solution)/shard_map/ppermute | solution.py:135
  5.4 8.6 %collective-permute-start.2 = (bf16[512,128]{1,0:T(8,128)(2,1)S(1)}, bf16[512,128]{1,0:T(8,128)(2,1)S(1)}, u32[]{:S(2)}, u32[]{:S(2)}) collective-permute-start(bf16[512,128]{1,0:T(8,128)(2,1)S(1)} %get-tuple-element.12.refs_4_), channel_id=1, source_target_pairs={{0,8},{8,0},{16,24},{24,16},{1,9},{9,1},{17,25},{25,17},{2,10},{10... | collective-permute-start | bytes 393224 | tf_op jit(solution)/shard_map/ppermute | solution.py:135
  6.6 9.0 %collective-permute-start.6 = (bf16[512,128]{1,0:T(8,128)(2,1)S(1)}, bf16[512,128]{1,0:T(8,128)(2,1)S(1)}, u32[]{:S(2)}, u32[]{:S(2)}) collective-permute-start(bf16[512,128]{1,0:T(8,128)(2,1)S(1)} %get-tuple-element.13.refs_5_), channel_id=1, source_target_pairs={{0,16},{8,24},{16,0},{24,8},{1,17},{9,25},{17,1},{25,9},{2,18},{10... | collective-permute-start | bytes 393224 | tf_op jit(solution)/shard_map/ppermute | solution.py:135
  6.8 12.6 %collective-permute-start.1 = (bf16[512,128]{1,0:T(8,128)(2,1)S(1)}, bf16[512,128]{1,0:T(8,128)(2,1)S(1)}, u32[]{:S(2)}, u32[]{:S(2)}) collective-permute-start(bf16[512,128]{1,0:T(8,128)(2,1)S(1)} %get-tuple-element.12.refs_4_), channel_id=1, source_target_pairs={{1,0},{2,1},{3,2},{4,3},{5,4},{6,5},{7,6},{9,8},{10,9},{11,10},{12... | collective-permute-start | bytes 393224 | tf_op jit(solution)/shard_map/ppermute | solution.py:144
  10.2 9.1 %collective-permute-start.5 = (bf16[512,128]{1,0:T(8,128)(2,1)S(1)}, bf16[512,128]{1,0:T(8,128)(2,1)S(1)}, u32[]{:S(2)}, u32[]{:S(2)}) collective-permute-start(bf16[512,128]{1,0:T(8,128)(2,1)S(1)} %get-tuple-element.13.refs_5_), channel_id=1, source_target_pairs={{0,8},{8,0},{16,24},{24,16},{1,9},{9,1},{17,25},{25,17},{2,10},{10... | collective-permute-start | bytes 393224 | tf_op jit(solution)/shard_map/ppermute | solution.py:135
  10.3 9.1 %collective-permute-start = (bf16[512,128]{1,0:T(8,128)(2,1)S(1)}, bf16[512,128]{1,0:T(8,128)(2,1)S(1)}, u32[]{:S(2)}, u32[]{:S(2)}) collective-permute-start(bf16[512,128]{1,0:T(8,128)(2,1)S(1)} %get-tuple-element.13.refs_5_), channel_id=1, source_target_pairs={{0,1},{1,2},{2,3},{3,4},{4,5},{5,6},{6,7},{8,9},{9,10},{10,11},{11... | collective-permute-start | bytes 393224 | tf_op jit(solution)/shard_map/ppermute | solution.py:144
  14.0 5.5 %collective-permute-start.4 = (bf16[512,128]{1,0:T(8,128)(2,1)S(1)}, bf16[512,128]{1,0:T(8,128)(2,1)S(1)}, u32[]{:S(2)}, u32[]{:S(2)}) collective-permute-start(bf16[512,128]{1,0:T(8,128)(2,1)S(1)} %collective-permute-done.2.refs_6_), channel_id=1, source_target_pairs={{0,16},{8,24},{16,0},{24,8},{1,17},{9,25},{17,1},{25,9},{2,18},{10... | collective-permute-start | bytes 393224 | tf_op jit(solution)/shard_map/ppermute | solution.py:135
  15.6 4.7 %collective-permute-start.7 = (bf16[512,128]{1,0:T(8,128)(2,1)S(1)}, bf16[512,128]{1,0:T(8,128)(2,1)S(1)}, u32[]{:S(2)}, u32[]{:S(2)}) collective-permute-start(bf16[512,128]{1,0:T(8,128)(2,1)S(1)} %collective-permute-done.6.refs_10_), channel_id=1, source_target_pairs={{0,8},{8,0},{16,24},{24,16},{1,9},{9,1},{17,25},{25,17},{2,10},{10... | collective-permute-start | bytes 393224 | tf_op jit(solution)/shard_map/ppermute | solution.py:135
  16.8 1.6 %copy-start = (bf16[512,2048]{1,0:T(8,128)(2,1)S(1)}, bf16[512,2048]{1,0:T(8,128)(2,1)}, u32[]{:S(2)}) copy-start(bf16[512,2048]{1,0:T(8,128)(2,1)} %refs_3_.5) | copy-start | bytes 6291460
  18.4 1.9 %copy-start.1 = (bf16[512,2048]{1,0:T(8,128)(2,1)S(1)}, bf16[512,2048]{1,0:T(8,128)(2,1)}, u32[]{:S(2)}) copy-start(bf16[512,2048]{1,0:T(8,128)(2,1)} %refs_3_.5) | copy-start | bytes 6291460
  19.4 13.0 %copy-start.3 = (f32[512,1,2,128]{3,2,1,0:T(2,128)S(1)}, f32[512,1,2,128]{3,2,1,0:T(2,128)}, u32[]{:S(2)}) copy-start(f32[512,1,2,128]{3,2,1,0:T(2,128)} %param.5) | copy-start | bytes 1572868
  20.9 6.0 %collective-permute-start.11 = (bf16[512,128]{1,0:T(8,128)(2,1)S(1)}, bf16[512,128]{1,0:T(8,128)(2,1)S(1)}, u32[]{:S(2)}, u32[]{:S(2)}) collective-permute-start(bf16[512,128]{1,0:T(8,128)(2,1)S(1)} %get-tuple-element.15.refs_5_), channel_id=1, source_target_pairs={{0,16},{8,24},{16,0},{24,8},{1,17},{9,25},{17,1},{25,9},{2,18},{10... | collective-permute-start | bytes 393224 | tf_op jit(solution)/shard_map/ppermute | solution.py:135
  21.0 9.9 %collective-permute-start.10 = (bf16[512,128]{1,0:T(8,128)(2,1)S(1)}, bf16[512,128]{1,0:T(8,128)(2,1)S(1)}, u32[]{:S(2)}, u32[]{:S(2)}) collective-permute-start(bf16[512,128]{1,0:T(8,128)(2,1)S(1)} %get-tuple-element.15.refs_5_), channel_id=1, source_target_pairs={{0,8},{8,0},{16,24},{24,16},{1,9},{9,1},{17,25},{25,17},{2,10},{10... | collective-permute-start | bytes 393224 | tf_op jit(solution)/shard_map/ppermute | solution.py:135
  22.4 8.5 %collective-permute-start.14 = (bf16[512,128]{1,0:T(8,128)(2,1)S(1)}, bf16[512,128]{1,0:T(8,128)(2,1)S(1)}, u32[]{:S(2)}, u32[]{:S(2)}) collective-permute-start(bf16[512,128]{1,0:T(8,128)(2,1)S(1)} %get-tuple-element.16.refs_6_), channel_id=1, source_target_pairs={{0,16},{8,24},{16,0},{24,8},{1,17},{9,25},{17,1},{25,9},{2,18},{10... | collective-permute-start | bytes 393224 | tf_op jit(solution)/shard_map/ppermute | solution.py:135
  23.6 9.8 %collective-permute-start.9 = (bf16[512,128]{1,0:T(8,128)(2,1)S(1)}, bf16[512,128]{1,0:T(8,128)(2,1)S(1)}, u32[]{:S(2)}, u32[]{:S(2)}) collective-permute-start(bf16[512,128]{1,0:T(8,128)(2,1)S(1)} %get-tuple-element.15.refs_5_), channel_id=1, source_target_pairs={{1,0},{2,1},{3,2},{4,3},{5,4},{6,5},{7,6},{9,8},{10,9},{11,10},{12... | collective-permute-start | bytes 393224 | tf_op jit(solution)/shard_map/ppermute | solution.py:144
  26.5 6.9 %collective-permute-start.13 = (bf16[512,128]{1,0:T(8,128)(2,1)S(1)}, bf16[512,128]{1,0:T(8,128)(2,1)S(1)}, u32[]{:S(2)}, u32[]{:S(2)}) collective-permute-start(bf16[512,128]{1,0:T(8,128)(2,1)S(1)} %get-tuple-element.16.refs_6_), channel_id=1, source_target_pairs={{0,8},{8,0},{16,24},{24,16},{1,9},{9,1},{17,25},{25,17},{2,10},{10... | collective-permute-start | bytes 393224 | tf_op jit(solution)/shard_map/ppermute | solution.py:135
  26.9 6.5 %collective-permute-start.8 = (bf16[512,128]{1,0:T(8,128)(2,1)S(1)}, bf16[512,128]{1,0:T(8,128)(2,1)S(1)}, u32[]{:S(2)}, u32[]{:S(2)}) collective-permute-start(bf16[512,128]{1,0:T(8,128)(2,1)S(1)} %get-tuple-element.16.refs_6_), channel_id=1, source_target_pairs={{0,1},{1,2},{2,3},{3,4},{4,5},{5,6},{6,7},{8,9},{9,10},{10,11},{11... | collective-permute-start | bytes 393224 | tf_op jit(solution)/shard_map/ppermute | solution.py:144
  30.8 4.2 %collective-permute-start.12 = (bf16[512,128]{1,0:T(8,128)(2,1)S(1)}, bf16[512,128]{1,0:T(8,128)(2,1)S(1)}, u32[]{:S(2)}, u32[]{:S(2)}) collective-permute-start(bf16[512,128]{1,0:T(8,128)(2,1)S(1)} %collective-permute-done.10.refs_6_), channel_id=1, source_target_pairs={{0,16},{8,24},{16,0},{24,8},{1,17},{9,25},{17,1},{25,9},{2,18},{10... | collective-permute-start | bytes 393224 | tf_op jit(solution)/shard_map/ppermute | solution.py:135
  30.9 4.4 %collective-permute-start.15 = (bf16[512,128]{1,0:T(8,128)(2,1)S(1)}, bf16[512,128]{1,0:T(8,128)(2,1)S(1)}, u32[]{:S(2)}, u32[]{:S(2)}) collective-permute-start(bf16[512,128]{1,0:T(8,128)(2,1)S(1)} %collective-permute-done.14.refs_10_), channel_id=1, source_target_pairs={{0,8},{8,0},{16,24},{24,16},{1,9},{9,1},{17,25},{25,17},{2,10},{10... | collective-permute-start | bytes 393224 | tf_op jit(solution)/shard_map/ppermute | solution.py:135

commit v2 on v0

v2 whole, which is shorter than its diff:
```python
import functools

import jax
import jax.numpy as jnp
from jax import lax
from jax.experimental import pallas as pl
from jax.experimental.pallas import tpu as pltpu
from jax.sharding import PartitionSpec as P

F32 = jnp.float32
BF16 = jnp.bfloat16
VMEM = pl.BlockSpec(memory_space=pltpu.VMEM)
HBM = pl.BlockSpec(memory_space=pltpu.HBM)


def call(body, outs, args, in_specs=None, out_specs=None, scratch=(), flops=0):
    total = sum(a.size * a.dtype.itemsize for a in (*outs, *args))
    return pl.pallas_call(
        body,
        out_shape=outs,
        in_specs=in_specs or [VMEM] * len(args),
        out_specs=out_specs or [VMEM] * len(outs),
        scratch_shapes=list(scratch),
        compiler_params=pltpu.CompilerParams(vmem_limit_bytes=24 * 2**20),
        cost_estimate=pl.CostEstimate(flops=flops, bytes_accessed=total, transcendentals=0),
    )(*args)


def shape(dims, dtype):
    return jax.ShapeDtypeStruct(dims, dtype)


def is_first():
    return 1 - lax.axis_index("cell") % 2


def source_row(r, rows):
    return r + is_first() * (rows - 1 - 2 * r)


def prepare(rows, pop_hbm, mask_hbm, octant_hbm, courant_hbm, *refs):
    q_refs, (p0_ref, keep_ref, coef_ref) = refs[:rows], refs[rows : rows + 3]
    pop_ref, mask_ref, octant_ref, courant_ref, sems = refs[rows + 3 :]
    pairs = (mask_hbm, mask_ref), (pop_hbm, pop_ref), (octant_hbm, octant_ref), (courant_hbm, courant_ref)
    copies = [pltpu.make_async_copy(*pair, sems.at[i]) for i, pair in enumerate(pairs)]
    for copy in copies:
        copy.start()
    modes = p0_ref.shape[1]
    copies[0].wait()
    copies[1].wait()
    for r in range(rows):
        source = source_row(r, rows)
        keep = (1 - mask_ref[pl.ds(source, 1), :]).astype(F32)
        row = keep * pop_ref[pl.ds(source, modes, stride=rows), :]
        keep_ref[r : r + 1, :] = keep
        p0_ref[r] = row
        q_refs[r][...] = row.astype(BF16)
    copies[2].wait()
    copies[3].wait()
    octant = octant_ref[...]
    speeds = [(1.0 - 2.0 * ((octant >> d) & 1).astype(F32)) * courant_ref[d : d + 1] for d in range(3)]
    flags = [(v < 0).astype(F32) for v in speeds]
    table = jnp.concatenate([jnp.abs(v) for v in speeds] + flags + flags[:2], axis=0)
    coef_ref[...] = table.T


def columns(offset, modes):
    position = lax.axis_index("mode") ^ offset
    return pl.ds(pl.multiple_of(position * modes, modes), modes)


def product(c_ref, offset, blocks):
    cols = columns(offset, blocks[0].shape[0])
    return jnp.dot(c_ref[:, cols], jnp.concatenate(blocks, axis=1), preferred_element_type=F32)


def backward_y(coef_ref):
    return (coef_ref[:, 4:5] > 0) == (is_first() == 0)


def near_terms(fields, q_refs, early, blocks, coef_ref, c_ref):
    rows = len(fields)
    modes, width = fields[0].shape
    ax, ay, az = (coef_ref[:, d : d + 1] for d in range(3))
    neg_x = coef_ref[:, 3:4] > 0
    after = backward_y(coef_ref)
    stay = 1.0 - (ax + ay + az)
    results = []
    for r, p in enumerate(fields):
        beside = jnp.where(neg_x, pltpu.roll(p, width - 1, 1), pltpu.roll(p, 1, 1))
        prior = fields[r - 1] if r > 0 else jnp.zeros_like(p)
        later = fields[r + 1] if r < rows - 1 else jnp.zeros_like(p)
        results.append(stay * p + ax * beside + ay * jnp.where(after, later, prior))
    total = product(c_ref, 0, [q[...] for q in q_refs])
    for i, offset in enumerate(early):
        total = total + product(c_ref, offset, [b[...] for b in blocks[i * rows : (i + 1) * rows]])
    return [v - total[:, r * width : (r + 1) * width] for r, v in enumerate(results)]


def far_terms(rows, late, blocks, inner, outer, coef_ref, c_ref):
    width = inner.shape[1]
    ay = coef_ref[:, 1:2]
    after = backward_y(coef_ref)
    results = [None] * rows
    if late:
        total = sum(
            product(c_ref, offset, [b[...] for b in blocks[i * rows : (i + 1) * rows]]) for i, offset in enumerate(late)
        )
        results = [-total[:, r * width : (r + 1) * width] for r in range(rows)]
    else:
        results = [jnp.zeros(inner.shape, F32)] * rows
    results[0] = results[0] + jnp.where(after, 0.0, ay * inner[...].astype(F32))
    results[-1] = results[-1] + jnp.where(after, ay * outer[...].astype(F32), 0.0)
    return results


def first_near(rows, early, *refs):
    p0_ref, coef_ref, c_hbm, *rest = refs
    q_refs, blocks = rest[:rows], rest[rows : rows * (1 + len(early))]
    base_ref, c_ref, sem = rest[rows * (1 + len(early)) :]
    copy = pltpu.make_async_copy(c_hbm, c_ref, sem)
    copy.start()
    copy.wait()
    for r, value in enumerate(near_terms([p0_ref[r] for r in range(rows)], q_refs, early, blocks, coef_ref, c_ref)):
        base_ref[r] = value


def first_end(rows, late, *refs):
    base_ref, keep_ref, coef_ref, c_ref, inner, outer, *rest = refs
    blocks, (*q_refs, p1_ref) = rest[: rows * len(late)], rest[rows * len(late) :]
    for r, term in enumerate(far_terms(rows, late, blocks, inner, outer, coef_ref, c_ref)):
        value = keep_ref[r : r + 1] * (base_ref[r] + term)
        p1_ref[r] = value
        q_refs[r][...] = value.astype(BF16)


def second_near(rows, early, *refs):
    p0_ref, p1_ref, coef_ref, c_ref, *rest = refs
    q_refs, blocks, base_ref = rest[:rows], rest[rows:-1], rest[-1]
    for r, value in enumerate(near_terms([p1_ref[r] for r in range(rows)], q_refs, early, blocks, coef_ref, c_ref)):
        base_ref[r] = 0.5 * p0_ref[r] + 0.5 * value


def second_end(rows, late, *refs):
    base_ref, keep_ref, coef_ref, c_ref, inner, outer, *rest = refs
    blocks, out_ref = rest[:-1], rest[-1]
    modes = out_ref.shape[0] // rows
    for r, term in enumerate(far_terms(rows, late, blocks, inner, outer, coef_ref, c_ref)):
        out_ref[pl.ds(source_row(r, rows), modes, stride=rows), :] = keep_ref[r : r + 1] * (base_ref[r] + 0.5 * term)


def exchange(q, count):
    bits = [1 << b for b in range(count.bit_length() - 1)]
    gathered = [{0: row} for row in q]
    orders = [bits if r % 2 == 0 else bits[::-1] for r in range(len(q))]
    for step in range(len(bits)):
        for held, order in zip(gathered, orders):
            bit = order[step]
            pairs = [(i, i ^ bit) for i in range(count)]
            held |= {o ^ bit: lax.ppermute(b, "mode", pairs) for o, b in held.items()}
    return gathered


def halo(q):
    count = lax.axis_size("cell")
    within = [(i, i ^ 1) for i in range(count)]
    between = [(i, i + 1) for i in range(1, count - 1, 2)]
    between += [(target, source) for source, target in between]
    return lax.ppermute(q[0], "cell", within), lax.ppermute(q[-1], "cell", between)


def on_device(populations, contact_mask, octant, courant, collision):
    modes, planes, rows, width = populations.shape
    count = lax.axis_size("mode")
    assert planes == 1 and lax.axis_size("cell") % 2 == 0 and count & (count - 1) == 0
    early = [1 << b for b in range(count.bit_length() - 1)]
    late = [o for o in range(1, count) if o not in early]
    pop = populations.reshape(modes * rows, width)
    mask = contact_mask.reshape(rows, width)
    octant = octant.reshape(1, modes)
    row_bf16 = shape((modes, width), BF16)
    all_rows = shape((rows, modes, width), F32)
    flops = 2 * modes * modes * rows * width
    near = flops * (1 + len(early))
    far = flops * len(late)

    *q, p0, keep, coef = call(
        functools.partial(prepare, rows),
        [row_bf16] * rows + [all_rows, shape((rows, width), F32), shape((modes, 8), F32)],
        [pop, mask, octant, courant],
        in_specs=[HBM] * 4,
        scratch=[pltpu.VMEM(a.shape, a.dtype) for a in (pop, mask, octant, courant)] + [pltpu.SemaphoreType.DMA((4,))],
    )
    gathered = exchange(q, count)
    inner, outer = halo(q)
    args = [p0, coef, collision, *q, *(g[o] for o in early for g in gathered)]
    base, c = call(
        functools.partial(first_near, rows, early),
        [all_rows, shape(collision.shape, collision.dtype)],
        args,
        in_specs=[VMEM, VMEM, HBM] + [VMEM] * (len(args) - 3),
        scratch=[pltpu.SemaphoreType.DMA],
        flops=near,
    )
    *q, p1 = call(
        functools.partial(first_end, rows, late),
        [row_bf16] * rows + [all_rows],
        [base, keep, coef, c, inner, outer, *(g[o] for o in late for g in gathered)],
        flops=far,
    )
    gathered = exchange(q, count)
    inner, outer = halo(q)
    (base,) = call(
        functools.partial(second_near, rows, early),
        [all_rows],
        [p0, p1, coef, c, *q, *(g[o] for o in early for g in gathered)],
        flops=near,
    )
    (out,) = call(
        functools.partial(second_end, rows, late),
        [shape((modes * rows, width), F32)],
        [base, keep, coef, c, inner, outer, *(g[o] for o in late for g in gathered)],
        flops=far,
    )
    return out.reshape(populations.shape)


def solution(mesh):
    placed = (
        P("mode", None, "cell", None),
        P(None, "cell", None),
        P("mode"),
        P(None, "mode"),
        P("mode", None),
    )
    return jax.shard_map(
        on_device,
        mesh=mesh,
        in_specs=placed,
        out_specs=P("mode", None, "cell", None),
        check_vma=False,
    )
```

time: 99 us -> 36.5 us (0.37)
  waiting for transfers between devices: 32.9 us -> 3.64 us
  other arithmetic: 22.9 us -> 0 us
  between operations: 13.5 us -> 0.13 us
  starting transfers between devices: 12.2 us -> 23.7 us
  local copies, waits for them, and re-layouts: 11.4 us -> 4.69 us
  matrix products: 4.74 us -> 0 us
  Pallas kernels: 0 us -> 3.83 us
    all_gather x2 -> x0, waiting for transfers between devices: 32.5 us -> none  [collide(): lax.all_gather(rounded, 'mode', axis=0, tiled=True)]
    convert_element_type x4 -> x0, other arithmetic: 13.2 us -> none  [the longest x2 9.65 us: advect(): field.astype(jnp.bfloat16)]
    ppermute x4 -> x16, starting transfers between devices: 12.1 us -> 23.7 us  [the longest x12 11.5 us: exchange(): held |= {o ^ bit: lax.ppermute(b, 'mode', pairs) for o, b in held.items()}]
    mul x3 -> x0, other arithmetic: 9.65 us -> none  [on_device(): return keep * (0.5 * first + 0.5 * final)]
    slice x7 -> x0, local copies, waits for them, and re-layouts: 6.85 us -> none  [the longest x4 6.11 us: advect(): back_x = jnp.roll(field, 1, axis=3)]
    dot_general x2 -> x0, matrix products: 4.74 us -> none  [collide(): jnp.dot(collision, lax.all_gather(rounded, 'mode', axis=0, tiled=True), p...]
    pallas_call x0 -> x5, Pallas kernels: none -> 3.83 us  [call(): pl.pallas_call(body, out_shape=outs, in_specs=in_specs or [VMEM] * len(ar...]
    ppermute x4 -> x16, waiting for transfers between devices: 0.4 us -> 3.64 us  [the longest x12 3.24 us: exchange(): held |= {o ^ bit: lax.ppermute(b, 'mode', pairs) for o, b in held.items()}]
  transfers between devices with their start and end apart: 6 -> 16, of which waited for: 4 -> 6; matrix products, arithmetic and copies ran while one was open for 11% -> 0% of each run, Pallas kernels for 0% -> 6%
where the time goes in v2:
time: 36.5 us; the launch traced here: 36 us
  starting transfers between devices  23.7 us (65%)
  local copies, waits for them, and re-layouts  4.69 us (13%)
  Pallas kernels  3.83 us (10%)
  waiting for transfers between devices  3.64 us (10%)
    ppermute x12, starting transfers between devices, exchange(): held |= {o ^ bit: lax.ppermute(b, 'mode', pairs) for o, b in held.items()}  11.5 us
    ppermute x2, starting transfers between devices, halo(): lax.ppermute(q[-1], 'cell', between)  9.84 us
    unnamed x10, local copies, waits for them, and re-layouts  4.69 us
    pallas_call x5, Pallas kernels, call(): pl.pallas_call(body, out_shape=outs, in_specs=in_specs or [VMEM] * len(ar...  3.83 us
    ppermute x12, waiting for transfers between devices, exchange(): held |= {o ^ bit: lax.ppermute(b, 'mode', pairs) for o, b in held.items()}  3.24 us
    ppermute x2, starting transfers between devices, halo(): lax.ppermute(q[0], 'cell', within)  2.38 us
  transfers between devices with their start and end apart: 16, of which 6 were waited for; matrix products, arithmetic and copies ran while one was open for 0% of the time, Pallas kernels for 6%

profile of v2, /device:TPU:1, one launch (start us, length us, event | category | flops | bytes accessed | tf_op | source)
XLA Modules:
  0.0 36.0 jit_solution(5074759601783447382)
XLA Ops:
  0.0 0.0 copy-start.1
  0.0 1.0 %copy-done.1 = f32[512,1,2,128]{3,2,1,0:T(2,128)S(1)} copy-done((f32[512,1,2,128]{3,2,1,0:T(2,128)S(1)}, f32[512,1,2,128]{3,2,1,0:T(2,128)}, u32[]{:S(2)}) %copy-start.1) | copy-done | bytes 524312
  1.0 0.0 copy-start.2
  1.0 0.7 %copy-done.2 = f32[3,512]{1,0:T(4,128)S(1)} copy-done((f32[3,512]{1,0:T(4,128)S(1)}, f32[3,512]{1,0:T(4,128)}, u32[]{:S(2)}) %copy-start.2) | copy-done | bytes 6168
  1.7 0.0 copy-start.3
  1.7 0.7 %copy-done.3 = s32[512]{0:T(512)S(1)} copy-done((s32[512]{0:T(512)S(1)}, s32[512]{0:T(512)}, u32[]{:S(2)}) %copy-start.3) | copy-done | bytes 2072
  2.4 0.0 copy-start.4
  2.4 0.7 %copy-done.4 = s32[1,2,128]{2,1,0:T(2,128)S(1)} copy-done((s32[1,2,128]{2,1,0:T(2,128)S(1)}, s32[1,2,128]{2,1,0:T(2,128)}, u32[]{:S(2)}) %copy-start.4) | copy-done | bytes 1048
  3.1 0.3 shard_map.55
  3.4 2.1 %collective-permute-start = (bf16[512,128]{1,0:T(8,128)(2,1)S(1)}, bf16[512,128]{1,0:T(8,128)(2,1)S(1)}, u32[]{:S(2)}, u32[]{:S(2)}) collective-permute-start(bf16[512,128]{1,0:T(8,128)(2,1)S(1)} %get-tuple-element.17.refs_3_), channel_id=1, source_target_pairs={{0,8},{8,0},{16,24},{24,16},{1,9},{9,1},{17,25},{25,17},{2,10},{10... | collective-permute-start | bytes 393224 | tf_op jit(solution)/shard_map/ppermute | solution.py:160
  5.5 1.2 %collective-permute-start.3 = (bf16[512,128]{1,0:T(8,128)(2,1)S(1)}, bf16[512,128]{1,0:T(8,128)(2,1)S(1)}, u32[]{:S(2)}, u32[]{:S(2)}) collective-permute-start(bf16[512,128]{1,0:T(8,128)(2,1)S(1)} %get-tuple-element.18.refs_4_), channel_id=1, source_target_pairs={{0,16},{8,24},{16,0},{24,8},{1,17},{9,25},{17,1},{25,9},{2,18},{10... | collective-permute-start | bytes 393224 | tf_op jit(solution)/shard_map/ppermute | solution.py:160
  6.8 0.3 collective-permute-start.1
  7.0 0.1 collective-permute-start.2
  7.1 1.5 %collective-permute-start.4 = (bf16[512,128]{1,0:T(8,128)(2,1)S(1)}, bf16[512,128]{1,0:T(8,128)(2,1)S(1)}, u32[]{:S(2)}, u32[]{:S(2)}) collective-permute-start(bf16[512,128]{1,0:T(8,128)(2,1)S(1)} %get-tuple-element.17.refs_3_), channel_id=1, source_target_pairs={{0,1},{1,0},{2,3},{3,2},{4,5},{5,4},{6,7},{7,6},{8,9},{9,8},{10,11... | collective-permute-start | bytes 393224 | tf_op jit(solution)/shard_map/ppermute | solution.py:169
  8.6 0.2 collective-permute-done.refs_5_
  8.7 4.9 %collective-permute-start.5 = (bf16[512,128]{1,0:T(8,128)(2,1)S(1)}, bf16[512,128]{1,0:T(8,128)(2,1)S(1)}, u32[]{:S(2)}, u32[]{:S(2)}) collective-permute-start(bf16[512,128]{1,0:T(8,128)(2,1)S(1)} %get-tuple-element.18.refs_4_), channel_id=1, source_target_pairs={{1,2},{3,4},{5,6},{2,1},{4,3},{6,5},{9,10},{11,12},{13,14},{10,9},... | collective-permute-start | bytes 393224 | tf_op jit(solution)/shard_map/ppermute | solution.py:169
  13.6 0.0 collective-permute-done.3.refs_8_
  13.6 2.1 %collective-permute-start.6 = (bf16[512,128]{1,0:T(8,128)(2,1)S(1)}, bf16[512,128]{1,0:T(8,128)(2,1)S(1)}, u32[]{:S(2)}, u32[]{:S(2)}) collective-permute-start(bf16[512,128]{1,0:T(8,128)(2,1)S(1)} %collective-permute-done.refs_5_), channel_id=1, source_target_pairs={{0,16},{8,24},{16,0},{24,8},{1,17},{9,25},{17,1},{25,9},{2,18},{10... | collective-permute-start | bytes 393224 | tf_op jit(solution)/shard_map/ppermute | solution.py:160
  15.8 0.0 collective-permute-done.1.refs_6_
  15.8 1.2 %collective-permute-start.7 = (bf16[512,128]{1,0:T(8,128)(2,1)S(1)}, bf16[512,128]{1,0:T(8,128)(2,1)S(1)}, u32[]{:S(2)}, u32[]{:S(2)}) collective-permute-start(bf16[512,128]{1,0:T(8,128)(2,1)S(1)} %collective-permute-done.3.refs_8_), channel_id=1, source_target_pairs={{0,8},{8,0},{16,24},{24,16},{1,9},{9,1},{17,25},{25,17},{2,10},{10... | collective-permute-start | bytes 393224 | tf_op jit(solution)/shard_map/ppermute | solution.py:160
  17.0 0.0 collective-permute-done.2.refs_7_
  17.0 0.0 copy-start
  17.0 1.6 %copy-done = bf16[512,2048]{1,0:T(8,128)(2,1)S(1)} copy-done((bf16[512,2048]{1,0:T(8,128)(2,1)S(1)}, bf16[512,2048]{1,0:T(8,128)(2,1)}, u32[]{:S(2)}) %copy-start) | copy-done | bytes 2097176
  18.6 1.1 %shard_map.56 = (f32[2,512,128]{2,1,0:T(8,128)S(1)}, bf16[512,2048]{1,0:T(8,128)(2,1)S(1)}) custom-call(f32[2,512,128]{2,1,0:T(8,128)S(1)} %get-tuple-element.15.refs_0_, f32[512,8]{1,0:T(8,128)S(1)} %get-tuple-element.16.refs_1_.refs_2_, bf16[512,2048]{1,0:T(8,128)(2,1)S(1)} %copy-done, bf16[512,128]{1,0:T(8,128)(2,1)S(1)} %get-tuple-element.17.refs_3_, ...), custom_call_target="tpu_custom_call" | custom-call | flops 402653184 | bytes 6045696 | tf_op jit(solution)/shard_map/pallas_call | solution.py:18
  19.6 0.0 collective-permute-done.4.refs_4_
  19.7 0.0 collective-permute-done.5.refs_5_
  19.7 0.0 collective-permute-done.6.refs_6_
  19.7 0.4 %collective-permute-done.7.refs_7_ = bf16[512,128]{1,0:T(8,128)(2,1)S(1)} collective-permute-done((bf16[512,128]{1,0:T(8,128)(2,1)S(1)}, bf16[512,128]{1,0:T(8,128)(2,1)S(1)}, u32[]{:S(2)}, u32[]{:S(2)}) %collective-permute-start.7) | collective-permute-done | bytes 131104 | tf_op jit(solution)/shard_map/ppermute | solution.py:160
  20.0 0.3 shard_map.57
  20.4 0.2 collective-permute-start.10
  20.6 1.0 %collective-permute-start.8 = (bf16[512,128]{1,0:T(8,128)(2,1)S(1)}, bf16[512,128]{1,0:T(8,128)(2,1)S(1)}, u32[]{:S(2)}, u32[]{:S(2)}) collective-permute-start(bf16[512,128]{1,0:T(8,128)(2,1)S(1)} %get-tuple-element.23.refs_4_), channel_id=1, source_target_pairs={{0,8},{8,0},{16,24},{24,16},{1,9},{9,1},{17,25},{25,17},{2,10},{10... | collective-permute-start | bytes 393224 | tf_op jit(solution)/shard_map/ppermute | solution.py:160
  21.6 1.1 %collective-permute-start.11 = (bf16[512,128]{1,0:T(8,128)(2,1)S(1)}, bf16[512,128]{1,0:T(8,128)(2,1)S(1)}, u32[]{:S(2)}, u32[]{:S(2)}) collective-permute-start(bf16[512,128]{1,0:T(8,128)(2,1)S(1)} %get-tuple-element.24.refs_5_), channel_id=1, source_target_pairs={{0,16},{8,24},{16,0},{24,8},{1,17},{9,25},{17,1},{25,9},{2,18},{10... | collective-permute-start | bytes 393224 | tf_op jit(solution)/shard_map/ppermute | solution.py:160
  22.7 0.7 %collective-permute-start.9 = (bf16[512,128]{1,0:T(8,128)(2,1)S(1)}, bf16[512,128]{1,0:T(8,128)(2,1)S(1)}, u32[]{:S(2)}, u32[]{:S(2)}) collective-permute-start(bf16[512,128]{1,0:T(8,128)(2,1)S(1)} %get-tuple-element.24.refs_5_), channel_id=1, source_target_pairs={{0,8},{8,0},{16,24},{24,16},{1,9},{9,1},{17,25},{25,17},{2,10},{10... | collective-permute-start | bytes 393224 | tf_op jit(solution)/shard_map/ppermute | solution.py:160
  23.4 0.9 %collective-permute-start.12 = (bf16[512,128]{1,0:T(8,128)(2,1)S(1)}, bf16[512,128]{1,0:T(8,128)(2,1)S(1)}, u32[]{:S(2)}, u32[]{:S(2)}) collective-permute-start(bf16[512,128]{1,0:T(8,128)(2,1)S(1)} %get-tuple-element.23.refs_4_), channel_id=1, source_target_pairs={{0,1},{1,0},{2,3},{3,2},{4,5},{5,4},{6,7},{7,6},{8,9},{9,8},{10,11... | collective-permute-start | bytes 393224 | tf_op jit(solution)/shard_map/ppermute | solution.py:169
  24.3 1.5 %collective-permute-done.10.refs_8_ = bf16[512,128]{1,0:T(8,128)(2,1)S(1)} collective-permute-done((bf16[512,128]{1,0:T(8,128)(2,1)S(1)}, bf16[512,128]{1,0:T(8,128)(2,1)S(1)}, u32[]{:S(2)}, u32[]{:S(2)}) %collective-permute-start.10) | collective-permute-done | bytes 131104 | tf_op jit(solution)/shard_map/ppermute | solution.py:160
  25.8 5.0 %collective-permute-start.13 = (bf16[512,128]{1,0:T(8,128)(2,1)S(1)}, bf16[512,128]{1,0:T(8,128)(2,1)S(1)}, u32[]{:S(2)}, u32[]{:S(2)}) collective-permute-start(bf16[512,128]{1,0:T(8,128)(2,1)S(1)} %get-tuple-element.24.refs_5_), channel_id=1, source_target_pairs={{1,2},{3,4},{5,6},{2,1},{4,3},{6,5},{9,10},{11,12},{13,14},{10,9},... | collective-permute-start | bytes 393224 | tf_op jit(solution)/shard_map/ppermute | solution.py:169
  30.7 0.0 collective-permute-done.8.refs_6_
  30.8 0.1 collective-permute-start.14
  30.8 0.0 collective-permute-done.11.refs_9_
  30.8 1.4 %collective-permute-start.15 = (bf16[512,128]{1,0:T(8,128)(2,1)S(1)}, bf16[512,128]{1,0:T(8,128)(2,1)S(1)}, u32[]{:S(2)}, u32[]{:S(2)}) collective-permute-start(bf16[512,128]{1,0:T(8,128)(2,1)S(1)} %collective-permute-done.11.refs_9_), channel_id=1, source_target_pairs={{0,8},{8,0},{16,24},{24,16},{1,9},{9,1},{17,25},{25,17},{2,10},{10... | collective-permute-start | bytes 393224 | tf_op jit(solution)/shard_map/ppermute | solution.py:160
  32.3 0.0 collective-permute-done.9.refs_7_
  32.3 1.0 %shard_map.58.refs_0_ = f32[2,512,128]{2,1,0:T(8,128)S(1)} custom-call(f32[2,512,128]{2,1,0:T(8,128)S(1)} %get-tuple-element.15.refs_0_, f32[2,512,128]{2,1,0:T(8,128)S(1)} %get-tuple-element.22.refs_1_, f32[512,8]{1,0:T(8,128)S(1)} %get-tuple-element.16.refs_1_.refs_2_, bf16[512,2048]{1,0:T(8,128)(2,1)S(1)} %get-tuple-element.21.refs_3_, ...), custom_call_target="tpu_custom_call" | custom-call | flops 402653184 | bytes 4472832 | tf_op jit(solution)/shard_map/pallas_call | solution.py:18
  33.3 0.0 collective-permute-done.12.refs_4_
  33.3 0.4 %collective-permute-done.13.refs_5_ = bf16[512,128]{1,0:T(8,128)(2,1)S(1)} collective-permute-done((bf16[512,128]{1,0:T(8,128)(2,1)S(1)}, bf16[512,128]{1,0:T(8,128)(2,1)S(1)}, u32[]{:S(2)}, u32[]{:S(2)}) %collective-permute-start.13) | collective-permute-done | bytes 131104 | tf_op jit(solution)/shard_map/ppermute | solution.py:169
  33.7 1.0 %collective-permute-done.14.refs_6_ = bf16[512,128]{1,0:T(8,128)(2,1)S(1)} collective-permute-done((bf16[512,128]{1,0:T(8,128)(2,1)S(1)}, bf16[512,128]{1,0:T(8,128)(2,1)S(1)}, u32[]{:S(2)}, u32[]{:S(2)}) %collective-permute-start.14) | collective-permute-done | bytes 131104 | tf_op jit(solution)/shard_map/ppermute | solution.py:160
  34.6 0.2 collective-permute-done.15.refs_7_
  34.9 1.1 %shard_map.59 = f32[1024,128]{1,0:T(8,128)} custom-call(f32[2,512,128]{2,1,0:T(8,128)S(1)} %shard_map.58.refs_0_, f32[2,128]{1,0:T(2,128)S(1)} %get-tuple-element.20.refs_1_, f32[512,8]{1,0:T(8,128)S(1)} %get-tuple-element.16.refs_1_.refs_2_, bf16[512,2048]{1,0:T(8,128)(2,1)S(1)} %get-tuple-element.21.refs_3_, ...), custom_call_target="tpu_custom_call" | custom-call | flops 134217728 | bytes 3687424 | tf_op jit(solution)/shard_map/pallas_call | solution.py:18
Async XLA Ops:
  0.0 1.0 %copy-start.1 = (f32[512,1,2,128]{3,2,1,0:T(2,128)S(1)}, f32[512,1,2,128]{3,2,1,0:T(2,128)}, u32[]{:S(2)}) copy-start(f32[512,1,2,128]{3,2,1,0:T(2,128)} %param.5) | copy-start | bytes 1572868
  1.0 0.7 %copy-start.2 = (f32[3,512]{1,0:T(4,128)S(1)}, f32[3,512]{1,0:T(4,128)}, u32[]{:S(2)}) copy-start(f32[3,512]{1,0:T(4,128)} %courant_hbm.1) | copy-start | bytes 18436
  1.7 0.7 %copy-start.3 = (s32[512]{0:T(512)S(1)}, s32[512]{0:T(512)}, u32[]{:S(2)}) copy-start(s32[512]{0:T(512)} %param.7) | copy-start | bytes 6148
  2.4 0.7 %copy-start.4 = (s32[1,2,128]{2,1,0:T(2,128)S(1)}, s32[1,2,128]{2,1,0:T(2,128)}, u32[]{:S(2)}) copy-start(s32[1,2,128]{2,1,0:T(2,128)} %param.6) | copy-start | bytes 3076
  3.4 5.3 %collective-permute-start = (bf16[512,128]{1,0:T(8,128)(2,1)S(1)}, bf16[512,128]{1,0:T(8,128)(2,1)S(1)}, u32[]{:S(2)}, u32[]{:S(2)}) collective-permute-start(bf16[512,128]{1,0:T(8,128)(2,1)S(1)} %get-tuple-element.17.refs_3_), channel_id=1, source_target_pairs={{0,8},{8,0},{16,24},{24,16},{1,9},{9,1},{17,25},{25,17},{2,10},{10... | collective-permute-start | bytes 393224 | tf_op jit(solution)/shard_map/ppermute | solution.py:160
  5.5 8.1 %collective-permute-start.3 = (bf16[512,128]{1,0:T(8,128)(2,1)S(1)}, bf16[512,128]{1,0:T(8,128)(2,1)S(1)}, u32[]{:S(2)}, u32[]{:S(2)}) collective-permute-start(bf16[512,128]{1,0:T(8,128)(2,1)S(1)} %get-tuple-element.18.refs_4_), channel_id=1, source_target_pairs={{0,16},{8,24},{16,0},{24,8},{1,17},{9,25},{17,1},{25,9},{2,18},{10... | collective-permute-start | bytes 393224 | tf_op jit(solution)/shard_map/ppermute | solution.py:160
  6.8 9.0 %collective-permute-start.1 = (bf16[512,128]{1,0:T(8,128)(2,1)S(1)}, bf16[512,128]{1,0:T(8,128)(2,1)S(1)}, u32[]{:S(2)}, u32[]{:S(2)}) collective-permute-start(bf16[512,128]{1,0:T(8,128)(2,1)S(1)} %get-tuple-element.18.refs_4_), channel_id=1, source_target_pairs={{0,8},{8,0},{16,24},{24,16},{1,9},{9,1},{17,25},{25,17},{2,10},{10... | collective-permute-start | bytes 393224 | tf_op jit(solution)/shard_map/ppermute | solution.py:160
  7.0 10.0 %collective-permute-start.2 = (bf16[512,128]{1,0:T(8,128)(2,1)S(1)}, bf16[512,128]{1,0:T(8,128)(2,1)S(1)}, u32[]{:S(2)}, u32[]{:S(2)}) collective-permute-start(bf16[512,128]{1,0:T(8,128)(2,1)S(1)} %get-tuple-element.17.refs_3_), channel_id=1, source_target_pairs={{0,16},{8,24},{16,0},{24,8},{1,17},{9,25},{17,1},{25,9},{2,18},{10... | collective-permute-start | bytes 393224 | tf_op jit(solution)/shard_map/ppermute | solution.py:160
  7.1 12.6 %collective-permute-start.4 = (bf16[512,128]{1,0:T(8,128)(2,1)S(1)}, bf16[512,128]{1,0:T(8,128)(2,1)S(1)}, u32[]{:S(2)}, u32[]{:S(2)}) collective-permute-start(bf16[512,128]{1,0:T(8,128)(2,1)S(1)} %get-tuple-element.17.refs_3_), channel_id=1, source_target_pairs={{0,1},{1,0},{2,3},{3,2},{4,5},{5,4},{6,7},{7,6},{8,9},{9,8},{10,11... | collective-permute-start | bytes 393224 | tf_op jit(solution)/shard_map/ppermute | solution.py:169
  8.7 10.9 %collective-permute-start.5 = (bf16[512,128]{1,0:T(8,128)(2,1)S(1)}, bf16[512,128]{1,0:T(8,128)(2,1)S(1)}, u32[]{:S(2)}, u32[]{:S(2)}) collective-permute-start(bf16[512,128]{1,0:T(8,128)(2,1)S(1)} %get-tuple-element.18.refs_4_), channel_id=1, source_target_pairs={{1,2},{3,4},{5,6},{2,1},{4,3},{6,5},{9,10},{11,12},{13,14},{10,9},... | collective-permute-start | bytes 393224 | tf_op jit(solution)/shard_map/ppermute | solution.py:169
  13.6 6.0 %collective-permute-start.6 = (bf16[512,128]{1,0:T(8,128)(2,1)S(1)}, bf16[512,128]{1,0:T(8,128)(2,1)S(1)}, u32[]{:S(2)}, u32[]{:S(2)}) collective-permute-start(bf16[512,128]{1,0:T(8,128)(2,1)S(1)} %collective-permute-done.refs_5_), channel_id=1, source_target_pairs={{0,16},{8,24},{16,0},{24,8},{1,17},{9,25},{17,1},{25,9},{2,18},{10... | collective-permute-start | bytes 393224 | tf_op jit(solution)/shard_map/ppermute | solution.py:160
  15.8 4.3 %collective-permute-start.7 = (bf16[512,128]{1,0:T(8,128)(2,1)S(1)}, bf16[512,128]{1,0:T(8,128)(2,1)S(1)}, u32[]{:S(2)}, u32[]{:S(2)}) collective-permute-start(bf16[512,128]{1,0:T(8,128)(2,1)S(1)} %collective-permute-done.3.refs_8_), channel_id=1, source_target_pairs={{0,8},{8,0},{16,24},{24,16},{1,9},{9,1},{17,25},{25,17},{2,10},{10... | collective-permute-start | bytes 393224 | tf_op jit(solution)/shard_map/ppermute | solution.py:160
  17.0 1.6 %copy-start = (bf16[512,2048]{1,0:T(8,128)(2,1)S(1)}, bf16[512,2048]{1,0:T(8,128)(2,1)}, u32[]{:S(2)}) copy-start(bf16[512,2048]{1,0:T(8,128)(2,1)} %refs_2_.1) | copy-start | bytes 6291460
  20.4 5.4 %collective-permute-start.10 = (bf16[512,128]{1,0:T(8,128)(2,1)S(1)}, bf16[512,128]{1,0:T(8,128)(2,1)S(1)}, u32[]{:S(2)}, u32[]{:S(2)}) collective-permute-start(bf16[512,128]{1,0:T(8,128)(2,1)S(1)} %get-tuple-element.23.refs_4_), channel_id=1, source_target_pairs={{0,16},{8,24},{16,0},{24,8},{1,17},{9,25},{17,1},{25,9},{2,18},{10... | collective-permute-start | bytes 393224 | tf_op jit(solution)/shard_map/ppermute | solution.py:160
  20.6 10.1 %collective-permute-start.8 = (bf16[512,128]{1,0:T(8,128)(2,1)S(1)}, bf16[512,128]{1,0:T(8,128)(2,1)S(1)}, u32[]{:S(2)}, u32[]{:S(2)}) collective-permute-start(bf16[512,128]{1,0:T(8,128)(2,1)S(1)} %get-tuple-element.23.refs_4_), channel_id=1, source_target_pairs={{0,8},{8,0},{16,24},{24,16},{1,9},{9,1},{17,25},{25,17},{2,10},{10... | collective-permute-start | bytes 393224 | tf_op jit(solution)/shard_map/ppermute | solution.py:160
  21.6 9.3 %collective-permute-start.11 = (bf16[512,128]{1,0:T(8,128)(2,1)S(1)}, bf16[512,128]{1,0:T(8,128)(2,1)S(1)}, u32[]{:S(2)}, u32[]{:S(2)}) collective-permute-start(bf16[512,128]{1,0:T(8,128)(2,1)S(1)} %get-tuple-element.24.refs_5_), channel_id=1, source_target_pairs={{0,16},{8,24},{16,0},{24,8},{1,17},{9,25},{17,1},{25,9},{2,18},{10... | collective-permute-start | bytes 393224 | tf_op jit(solution)/shard_map/ppermute | solution.py:160
  22.7 9.6 %collective-permute-start.9 = (bf16[512,128]{1,0:T(8,128)(2,1)S(1)}, bf16[512,128]{1,0:T(8,128)(2,1)S(1)}, u32[]{:S(2)}, u32[]{:S(2)}) collective-permute-start(bf16[512,128]{1,0:T(8,128)(2,1)S(1)} %get-tuple-element.24.refs_5_), channel_id=1, source_target_pairs={{0,8},{8,0},{16,24},{24,16},{1,9},{9,1},{17,25},{25,17},{2,10},{10... | collective-permute-start | bytes 393224 | tf_op jit(solution)/shard_map/ppermute | solution.py:160
  23.4 9.9 %collective-permute-start.12 = (bf16[512,128]{1,0:T(8,128)(2,1)S(1)}, bf16[512,128]{1,0:T(8,128)(2,1)S(1)}, u32[]{:S(2)}, u32[]{:S(2)}) collective-permute-start(bf16[512,128]{1,0:T(8,128)(2,1)S(1)} %get-tuple-element.23.refs_4_), channel_id=1, source_target_pairs={{0,1},{1,0},{2,3},{3,2},{4,5},{5,4},{6,7},{7,6},{8,9},{9,8},{10,11... | collective-permute-start | bytes 393224 | tf_op jit(solution)/shard_map/ppermute | solution.py:169
  25.8 7.9 %collective-permute-start.13 = (bf16[512,128]{1,0:T(8,128)(2,1)S(1)}, bf16[512,128]{1,0:T(8,128)(2,1)S(1)}, u32[]{:S(2)}, u32[]{:S(2)}) collective-permute-start(bf16[512,128]{1,0:T(8,128)(2,1)S(1)} %get-tuple-element.24.refs_5_), channel_id=1, source_target_pairs={{1,2},{3,4},{5,6},{2,1},{4,3},{6,5},{9,10},{11,12},{13,14},{10,9},... | collective-permute-start | bytes 393224 | tf_op jit(solution)/shard_map/ppermute | solution.py:169
  30.8 3.9 %collective-permute-start.14 = (bf16[512,128]{1,0:T(8,128)(2,1)S(1)}, bf16[512,128]{1,0:T(8,128)(2,1)S(1)}, u32[]{:S(2)}, u32[]{:S(2)}) collective-permute-start(bf16[512,128]{1,0:T(8,128)(2,1)S(1)} %collective-permute-done.8.refs_6_), channel_id=1, source_target_pairs={{0,16},{8,24},{16,0},{24,8},{1,17},{9,25},{17,1},{25,9},{2,18},{10... | collective-permute-start | bytes 393224 | tf_op jit(solution)/shard_map/ppermute | solution.py:160
  30.8 4.0 %collective-permute-start.15 = (bf16[512,128]{1,0:T(8,128)(2,1)S(1)}, bf16[512,128]{1,0:T(8,128)(2,1)S(1)}, u32[]{:S(2)}, u32[]{:S(2)}) collective-permute-start(bf16[512,128]{1,0:T(8,128)(2,1)S(1)} %collective-permute-done.11.refs_9_), channel_id=1, source_target_pairs={{0,8},{8,0},{16,24},{24,16},{1,9},{9,1},{17,25},{25,17},{2,10},{10... | collective-permute-start | bytes 393224 | tf_op jit(solution)/shard_map/ppermute | solution.py:160

commit v3 on v2

--- a/solution.py
+++ b/solution.py
@@ -15,6 +15,8 @@
 
 def call(body, outs, args, in_specs=None, out_specs=None, scratch=(), flops=0):
     total = sum(a.size * a.dtype.itemsize for a in (*outs, *args))
+    if in_specs:
+        args = [pltpu.with_memory_space_constraint(a, pltpu.HBM) if s is HBM else a for a, s in zip(args, in_specs)]
     return pl.pallas_call(
         body,
         out_shape=outs,
@@ -149,6 +151,14 @@
         out_ref[pl.ds(source_row(r, rows), modes, stride=rows), :] = keep_ref[r : r + 1] * (base_ref[r] + 0.5 * term)
 
 
+def later(row, other):
+    def body(row_ref, _, out_ref):
+        out_ref[...] = row_ref[...]
+
+    (copied,) = call(body, [shape(row.shape, row.dtype)], [row, other], in_specs=[VMEM, pl.BlockSpec(memory_space=pl.ANY)])
+    return copied
+
+
 def exchange(q, count):
     bits = [1 << b for b in range(count.bit_length() - 1)]
     gathered = [{0: row} for row in q]
@@ -161,12 +171,12 @@
     return gathered
 
 
-def halo(q):
+def halo(q, block):
     count = lax.axis_size("cell")
     within = [(i, i ^ 1) for i in range(count)]
     between = [(i, i + 1) for i in range(1, count - 1, 2)]
     between += [(target, source) for source, target in between]
-    return lax.ppermute(q[0], "cell", within), lax.ppermute(q[-1], "cell", between)
+    return lax.ppermute(later(q[0], block), "cell", within), lax.ppermute(q[-1], "cell", between)
 
 
 def on_device(populations, contact_mask, octant, courant, collision):
@@ -192,7 +202,7 @@
         scratch=[pltpu.VMEM(a.shape, a.dtype) for a in (pop, mask, octant, courant)] + [pltpu.SemaphoreType.DMA((4,))],
     )
     gathered = exchange(q, count)
-    inner, outer = halo(q)
+    inner, outer = halo(q, gathered[-1][early[0]])
     args = [p0, coef, collision, *q, *(g[o] for o in early for g in gathered)]
     base, c = call(
         functools.partial(first_near, rows, early),
@@ -209,7 +219,7 @@
         flops=far,
     )
     gathered = exchange(q, count)
-    inner, outer = halo(q)
+    inner, outer = halo(q, gathered[-1][early[0]])
     (base,) = call(
         functools.partial(second_near, rows, early),
         [all_rows],

time: 36.5 us -> 32.5 us (0.89)
  the two profiles are of different devices: /device:TPU:1 before, /device:TPU:0 now
where the time goes in v3:
time: 32.5 us; the launch traced here: 32.4 us
  starting transfers between devices  20 us (62%)
  Pallas kernels  6.3 us (19%)
  waiting for transfers between devices  5.98 us (18%)
    ppermute x12, starting transfers between devices, exchange(): held |= {o ^ bit: lax.ppermute(b, 'mode', pairs) for o, b in held.items()}  14.5 us
    pallas_call x7, Pallas kernels, call(): pl.pallas_call(body, out_shape=outs, in_specs=in_specs or [VMEM] * len(ar...  6.3 us
    ppermute x12, waiting for transfers between devices, exchange(): held |= {o ^ bit: lax.ppermute(b, 'mode', pairs) for o, b in held.items()}  5.97 us
    ppermute x2, starting transfers between devices, halo(): lax.ppermute(later(q[0], block), 'cell', within)  4.19 us
    ppermute x2, starting transfers between devices, halo(): lax.ppermute(q[-1], 'cell', between)  1.31 us
  transfers between devices with their start and end apart: 16, of which 6 were waited for; matrix products, arithmetic and copies ran while one was open for 0% of the time, Pallas kernels for 11%

profile of v3, /device:TPU:0, one launch (start us, length us, event | category | flops | bytes accessed | tf_op | source)
XLA Modules:
  0.0 32.4 jit_solution(17389154823064533723)
XLA Ops:
  0.0 1.3 %shard_map.55 = (bf16[512,128]{1,0:T(8,128)(2,1)S(1)}, bf16[512,128]{1,0:T(8,128)(2,1)S(1)}, f32[2,512,128]{2,1,0:T(8,128)S(1)}, f32[2,128]{1,0:T(2,128)S(1)}, f32[512,8]{1,0:T(8,128)S(1)}) custom-call(f32[1024,128]{1,0:T(8,128)} %bitcast.6, s32[2,128]{1,0:T(2,128)} %bitcast.8, s32[1,512]{1,0:T(1,128)} %bitcast.7, f32[3,512]{1,0:T(4,128)} %courant_hbm.1), custom_call_target="tpu_custom_call" | custom-call | bytes 1337344 | tf_op jit(solution)/shard_map/pallas_call | solution.py:20
  1.3 3.0 %collective-permute-start.1 = (bf16[512,128]{1,0:T(8,128)(2,1)S(1)}, bf16[512,128]{1,0:T(8,128)(2,1)S(1)}, u32[]{:S(2)}, u32[]{:S(2)}) collective-permute-start(bf16[512,128]{1,0:T(8,128)(2,1)S(1)} %get-tuple-element.18.refs_4_), channel_id=1, source_target_pairs={{0,8},{8,0},{16,24},{24,16},{1,9},{9,1},{17,25},{25,17},{2,10},{10... | collective-permute-start | bytes 393224 | tf_op jit(solution)/shard_map/ppermute | solution.py:170
  4.3 0.1 collective-permute-start
  4.4 2.0 %collective-permute-start.3 = (bf16[512,128]{1,0:T(8,128)(2,1)S(1)}, bf16[512,128]{1,0:T(8,128)(2,1)S(1)}, u32[]{:S(2)}, u32[]{:S(2)}) collective-permute-start(bf16[512,128]{1,0:T(8,128)(2,1)S(1)} %get-tuple-element.18.refs_4_), channel_id=1, source_target_pairs={{0,16},{8,24},{16,0},{24,8},{1,17},{9,25},{17,1},{25,9},{2,18},{10... | collective-permute-start | bytes 393224 | tf_op jit(solution)/shard_map/ppermute | solution.py:170
  6.4 0.1 collective-permute-start.2
  6.4 0.7 %collective-permute-start.5 = (bf16[512,128]{1,0:T(8,128)(2,1)S(1)}, bf16[512,128]{1,0:T(8,128)(2,1)S(1)}, u32[]{:S(2)}, u32[]{:S(2)}) collective-permute-start(bf16[512,128]{1,0:T(8,128)(2,1)S(1)} %get-tuple-element.18.refs_4_), channel_id=1, source_target_pairs={{1,2},{3,4},{5,6},{2,1},{4,3},{6,5},{9,10},{11,12},{13,14},{10,9},... | collective-permute-start | bytes 393224 | tf_op jit(solution)/shard_map/ppermute | solution.py:179
  7.1 1.6 %collective-permute-done.1.refs_6_._ = bf16[512,128]{1,0:T(8,128)(2,1)S(1)} collective-permute-done((bf16[512,128]{1,0:T(8,128)(2,1)S(1)}, bf16[512,128]{1,0:T(8,128)(2,1)S(1)}, u32[]{:S(2)}, u32[]{:S(2)}) %collective-permute-start.1) | collective-permute-done | bytes 131104 | tf_op jit(solution)/shard_map/ppermute | solution.py:170
  8.7 1.9 %collective-permute-start.4 = (bf16[512,128]{1,0:T(8,128)(2,1)S(1)}, bf16[512,128]{1,0:T(8,128)(2,1)S(1)}, u32[]{:S(2)}, u32[]{:S(2)}) collective-permute-start(bf16[512,128]{1,0:T(8,128)(2,1)S(1)} %shard_map.57), channel_id=1, source_target_pairs={{0,1},{1,0},{2,3},{3,2},{4,5},{5,4},{6,7},{7,6},{8,9},{9,8},{10,11... | collective-permute-start | bytes 393224 | tf_op jit(solution)/shard_map/ppermute | solution.py:179
  10.6 0.1 collective-permute-done.refs_5_
  10.6 1.8 %collective-permute-start.6 = (bf16[512,128]{1,0:T(8,128)(2,1)S(1)}, bf16[512,128]{1,0:T(8,128)(2,1)S(1)}, u32[]{:S(2)}, u32[]{:S(2)}) collective-permute-start(bf16[512,128]{1,0:T(8,128)(2,1)S(1)} %collective-permute-done.refs_5_), channel_id=1, source_target_pairs={{0,16},{8,24},{16,0},{24,8},{1,17},{9,25},{17,1},{25,9},{2,18},{10... | collective-permute-start | bytes 393224 | tf_op jit(solution)/shard_map/ppermute | solution.py:170
  12.4 0.0 collective-permute-done.3.refs_8_
  12.4 1.5 %collective-permute-start.7 = (bf16[512,128]{1,0:T(8,128)(2,1)S(1)}, bf16[512,128]{1,0:T(8,128)(2,1)S(1)}, u32[]{:S(2)}, u32[]{:S(2)}) collective-permute-start(bf16[512,128]{1,0:T(8,128)(2,1)S(1)} %collective-permute-done.3.refs_8_), channel_id=1, source_target_pairs={{0,8},{8,0},{16,24},{24,16},{1,9},{9,1},{17,25},{25,17},{2,10},{10... | collective-permute-start | bytes 393224 | tf_op jit(solution)/shard_map/ppermute | solution.py:170
  13.9 0.0 collective-permute-done.2.refs_7_
  13.9 2.5 %shard_map.56 = (f32[2,512,128]{2,1,0:T(8,128)S(1)}, bf16[512,2048]{1,0:T(8,128)(2,1)S(1)}) custom-call(f32[2,512,128]{2,1,0:T(8,128)S(1)} %get-tuple-element.15.refs_0_, f32[512,8]{1,0:T(8,128)S(1)} %get-tuple-element.16.refs_1_.refs_2_, bf16[512,2048]{1,0:T(8,128)(2,1)} %refs_2_.1, bf16[512,128]{1,0:T(8,128)(2,1)S(1)} %get-tuple-element.17.refs_3_.row_ref, ...), custom_call_target="tpu_custom_call" | custom-call | flops 402653184 | bytes 6045696 | tf_op jit(solution)/shard_map/pallas_call | solution.py:20
  16.4 0.0 collective-permute-done.5.refs_5_
  16.4 0.0 collective-permute-done.4.refs_4_
  16.4 0.0 collective-permute-done.6.refs_6_
  16.4 0.9 %collective-permute-done.7.refs_7_ = bf16[512,128]{1,0:T(8,128)(2,1)S(1)} collective-permute-done((bf16[512,128]{1,0:T(8,128)(2,1)S(1)}, bf16[512,128]{1,0:T(8,128)(2,1)S(1)}, u32[]{:S(2)}, u32[]{:S(2)}) %collective-permute-start.7) | collective-permute-done | bytes 131104 | tf_op jit(solution)/shard_map/ppermute | solution.py:170
  17.4 0.3 %shard_map.58 = (bf16[512,128]{1,0:T(8,128)(2,1)S(1)}, bf16[512,128]{1,0:T(8,128)(2,1)S(1)}, f32[2,512,128]{2,1,0:T(8,128)S(1)}) custom-call(f32[2,512,128]{2,1,0:T(8,128)S(1)} %get-tuple-element.19.refs_0_, f32[2,128]{1,0:T(2,128)S(1)} %get-tuple-element.20.refs_1_, f32[512,8]{1,0:T(8,128)S(1)} %get-tuple-element.16.refs_1_.refs_2_, ...), custom_call_target="tpu_custom_call" | custom-call | flops 134217728 | bytes 3949568 | tf_op jit(solution)/shard_map/pallas_call | solution.py:20
  17.7 1.6 %collective-permute-start.9 = (bf16[512,128]{1,0:T(8,128)(2,1)S(1)}, bf16[512,128]{1,0:T(8,128)(2,1)S(1)}, u32[]{:S(2)}, u32[]{:S(2)}) collective-permute-start(bf16[512,128]{1,0:T(8,128)(2,1)S(1)} %get-tuple-element.24.refs_5_), channel_id=1, source_target_pairs={{0,8},{8,0},{16,24},{24,16},{1,9},{9,1},{17,25},{25,17},{2,10},{10... | collective-permute-start | bytes 393224 | tf_op jit(solution)/shard_map/ppermute | solution.py:170
  19.3 0.5 %collective-permute-start.8 = (bf16[512,128]{1,0:T(8,128)(2,1)S(1)}, bf16[512,128]{1,0:T(8,128)(2,1)S(1)}, u32[]{:S(2)}, u32[]{:S(2)}) collective-permute-start(bf16[512,128]{1,0:T(8,128)(2,1)S(1)} %get-tuple-element.23.refs_4_.row_ref), channel_id=1, source_target_pairs={{0,8},{8,0},{16,24},{24,16},{1,9},{9,1},{17,25},{25,17},{2,10},{10... | collective-permute-start | bytes 393224 | tf_op jit(solution)/shard_map/ppermute | solution.py:170
  19.8 0.4 %collective-permute-start.11 = (bf16[512,128]{1,0:T(8,128)(2,1)S(1)}, bf16[512,128]{1,0:T(8,128)(2,1)S(1)}, u32[]{:S(2)}, u32[]{:S(2)}) collective-permute-start(bf16[512,128]{1,0:T(8,128)(2,1)S(1)} %get-tuple-element.24.refs_5_), channel_id=1, source_target_pairs={{0,16},{8,24},{16,0},{24,8},{1,17},{9,25},{17,1},{25,9},{2,18},{10... | collective-permute-start | bytes 393224 | tf_op jit(solution)/shard_map/ppermute | solution.py:170
  20.2 1.6 %collective-permute-start.10 = (bf16[512,128]{1,0:T(8,128)(2,1)S(1)}, bf16[512,128]{1,0:T(8,128)(2,1)S(1)}, u32[]{:S(2)}, u32[]{:S(2)}) collective-permute-start(bf16[512,128]{1,0:T(8,128)(2,1)S(1)} %get-tuple-element.23.refs_4_.row_ref), channel_id=1, source_target_pairs={{0,16},{8,24},{16,0},{24,8},{1,17},{9,25},{17,1},{25,9},{2,18},{10... | collective-permute-start | bytes 393224 | tf_op jit(solution)/shard_map/ppermute | solution.py:170
  21.8 0.7 %collective-permute-start.13 = (bf16[512,128]{1,0:T(8,128)(2,1)S(1)}, bf16[512,128]{1,0:T(8,128)(2,1)S(1)}, u32[]{:S(2)}, u32[]{:S(2)}) collective-permute-start(bf16[512,128]{1,0:T(8,128)(2,1)S(1)} %get-tuple-element.24.refs_5_), channel_id=1, source_target_pairs={{1,2},{3,4},{5,6},{2,1},{4,3},{6,5},{9,10},{11,12},{13,14},{10,9},... | collective-permute-start | bytes 393224 | tf_op jit(solution)/shard_map/ppermute | solution.py:179
  22.5 0.7 %collective-permute-done.9.refs_7_._ = bf16[512,128]{1,0:T(8,128)(2,1)S(1)} collective-permute-done((bf16[512,128]{1,0:T(8,128)(2,1)S(1)}, bf16[512,128]{1,0:T(8,128)(2,1)S(1)}, u32[]{:S(2)}, u32[]{:S(2)}) %collective-permute-start.9) | collective-permute-done | bytes 131104 | tf_op jit(solution)/shard_map/ppermute | solution.py:170
  23.2 2.3 %collective-permute-start.12 = (bf16[512,128]{1,0:T(8,128)(2,1)S(1)}, bf16[512,128]{1,0:T(8,128)(2,1)S(1)}, u32[]{:S(2)}, u32[]{:S(2)}) collective-permute-start(bf16[512,128]{1,0:T(8,128)(2,1)S(1)} %shard_map.60), channel_id=1, source_target_pairs={{0,1},{1,0},{2,3},{3,2},{4,5},{5,4},{6,7},{7,6},{8,9},{9,8},{10,11... | collective-permute-start | bytes 393224 | tf_op jit(solution)/shard_map/ppermute | solution.py:179
  25.5 0.0 collective-permute-done.8.refs_6_
  25.5 0.5 %collective-permute-start.14 = (bf16[512,128]{1,0:T(8,128)(2,1)S(1)}, bf16[512,128]{1,0:T(8,128)(2,1)S(1)}, u32[]{:S(2)}, u32[]{:S(2)}) collective-permute-start(bf16[512,128]{1,0:T(8,128)(2,1)S(1)} %collective-permute-done.8.refs_6_), channel_id=1, source_target_pairs={{0,16},{8,24},{16,0},{24,8},{1,17},{9,25},{17,1},{25,9},{2,18},{10... | collective-permute-start | bytes 393224 | tf_op jit(solution)/shard_map/ppermute | solution.py:170
  26.0 0.0 collective-permute-done.11.refs_9_
  26.0 1.5 %collective-permute-start.15 = (bf16[512,128]{1,0:T(8,128)(2,1)S(1)}, bf16[512,128]{1,0:T(8,128)(2,1)S(1)}, u32[]{:S(2)}, u32[]{:S(2)}) collective-permute-start(bf16[512,128]{1,0:T(8,128)(2,1)S(1)} %collective-permute-done.11.refs_9_), channel_id=1, source_target_pairs={{0,8},{8,0},{16,24},{24,16},{1,9},{9,1},{17,25},{25,17},{2,10},{10... | collective-permute-start | bytes 393224 | tf_op jit(solution)/shard_map/ppermute | solution.py:170
  27.5 0.0 collective-permute-done.10.refs_8_
  27.5 1.0 %shard_map.59.refs_0_ = f32[2,512,128]{2,1,0:T(8,128)S(1)} custom-call(f32[2,512,128]{2,1,0:T(8,128)S(1)} %get-tuple-element.15.refs_0_, f32[2,512,128]{2,1,0:T(8,128)S(1)} %get-tuple-element.22.refs_1_, f32[512,8]{1,0:T(8,128)S(1)} %get-tuple-element.16.refs_1_.refs_2_, bf16[512,2048]{1,0:T(8,128)(2,1)S(1)} %get-tuple-element.21.refs_3_, ...), custom_call_target="tpu_custom_call" | custom-call | flops 402653184 | bytes 4472832 | tf_op jit(solution)/shard_map/pallas_call | solution.py:20
  28.5 0.0 collective-permute-done.13.refs_5_
  28.5 0.0 collective-permute-done.12.refs_4_
  28.5 2.5 %collective-permute-done.14.refs_6_ = bf16[512,128]{1,0:T(8,128)(2,1)S(1)} collective-permute-done((bf16[512,128]{1,0:T(8,128)(2,1)S(1)}, bf16[512,128]{1,0:T(8,128)(2,1)S(1)}, u32[]{:S(2)}, u32[]{:S(2)}) %collective-permute-start.14) | collective-permute-done | bytes 131104 | tf_op jit(solution)/shard_map/ppermute | solution.py:170
  31.0 0.2 collective-permute-done.15.refs_7_
  31.2 1.1 %shard_map.61 = f32[1024,128]{1,0:T(8,128)} custom-call(f32[2,512,128]{2,1,0:T(8,128)S(1)} %shard_map.59.refs_0_, f32[2,128]{1,0:T(2,128)S(1)} %get-tuple-element.20.refs_1_, f32[512,8]{1,0:T(8,128)S(1)} %get-tuple-element.16.refs_1_.refs_2_, bf16[512,2048]{1,0:T(8,128)(2,1)S(1)} %get-tuple-element.21.refs_3_, ...), custom_call_target="tpu_custom_call" | custom-call | flops 134217728 | bytes 3687424 | tf_op jit(solution)/shard_map/pallas_call | solution.py:20
  (2 shorter events, 0.0 us)
Async XLA Ops:
  1.3 7.3 %collective-permute-start.1 = (bf16[512,128]{1,0:T(8,128)(2,1)S(1)}, bf16[512,128]{1,0:T(8,128)(2,1)S(1)}, u32[]{:S(2)}, u32[]{:S(2)}) collective-permute-start(bf16[512,128]{1,0:T(8,128)(2,1)S(1)} %get-tuple-element.18.refs_4_), channel_id=1, source_target_pairs={{0,8},{8,0},{16,24},{24,16},{1,9},{9,1},{17,25},{25,17},{2,10},{10... | collective-permute-start | bytes 393224 | tf_op jit(solution)/shard_map/ppermute | solution.py:170
  4.3 6.3 %collective-permute-start = (bf16[512,128]{1,0:T(8,128)(2,1)S(1)}, bf16[512,128]{1,0:T(8,128)(2,1)S(1)}, u32[]{:S(2)}, u32[]{:S(2)}) collective-permute-start(bf16[512,128]{1,0:T(8,128)(2,1)S(1)} %get-tuple-element.17.refs_3_.row_ref), channel_id=1, source_target_pairs={{0,8},{8,0},{16,24},{24,16},{1,9},{9,1},{17,25},{25,17},{2,10},{10... | collective-permute-start | bytes 393224 | tf_op jit(solution)/shard_map/ppermute | solution.py:170
  4.4 8.0 %collective-permute-start.3 = (bf16[512,128]{1,0:T(8,128)(2,1)S(1)}, bf16[512,128]{1,0:T(8,128)(2,1)S(1)}, u32[]{:S(2)}, u32[]{:S(2)}) collective-permute-start(bf16[512,128]{1,0:T(8,128)(2,1)S(1)} %get-tuple-element.18.refs_4_), channel_id=1, source_target_pairs={{0,16},{8,24},{16,0},{24,8},{1,17},{9,25},{17,1},{25,9},{2,18},{10... | collective-permute-start | bytes 393224 | tf_op jit(solution)/shard_map/ppermute | solution.py:170
  6.4 7.5 %collective-permute-start.2 = (bf16[512,128]{1,0:T(8,128)(2,1)S(1)}, bf16[512,128]{1,0:T(8,128)(2,1)S(1)}, u32[]{:S(2)}, u32[]{:S(2)}) collective-permute-start(bf16[512,128]{1,0:T(8,128)(2,1)S(1)} %get-tuple-element.17.refs_3_.row_ref), channel_id=1, source_target_pairs={{0,16},{8,24},{16,0},{24,8},{1,17},{9,25},{17,1},{25,9},{2,18},{10... | collective-permute-start | bytes 393224 | tf_op jit(solution)/shard_map/ppermute | solution.py:170
  6.4 10.0 %collective-permute-start.5 = (bf16[512,128]{1,0:T(8,128)(2,1)S(1)}, bf16[512,128]{1,0:T(8,128)(2,1)S(1)}, u32[]{:S(2)}, u32[]{:S(2)}) collective-permute-start(bf16[512,128]{1,0:T(8,128)(2,1)S(1)} %get-tuple-element.18.refs_4_), channel_id=1, source_target_pairs={{1,2},{3,4},{5,6},{2,1},{4,3},{6,5},{9,10},{11,12},{13,14},{10,9},... | collective-permute-start | bytes 393224 | tf_op jit(solution)/shard_map/ppermute | solution.py:179
  8.7 7.8 %collective-permute-start.4 = (bf16[512,128]{1,0:T(8,128)(2,1)S(1)}, bf16[512,128]{1,0:T(8,128)(2,1)S(1)}, u32[]{:S(2)}, u32[]{:S(2)}) collective-permute-start(bf16[512,128]{1,0:T(8,128)(2,1)S(1)} %shard_map.57), channel_id=1, source_target_pairs={{0,1},{1,0},{2,3},{3,2},{4,5},{5,4},{6,7},{7,6},{8,9},{9,8},{10,11... | collective-permute-start | bytes 393224 | tf_op jit(solution)/shard_map/ppermute | solution.py:179
  10.6 5.8 %collective-permute-start.6 = (bf16[512,128]{1,0:T(8,128)(2,1)S(1)}, bf16[512,128]{1,0:T(8,128)(2,1)S(1)}, u32[]{:S(2)}, u32[]{:S(2)}) collective-permute-start(bf16[512,128]{1,0:T(8,128)(2,1)S(1)} %collective-permute-done.refs_5_), channel_id=1, source_target_pairs={{0,16},{8,24},{16,0},{24,8},{1,17},{9,25},{17,1},{25,9},{2,18},{10... | collective-permute-start | bytes 393224 | tf_op jit(solution)/shard_map/ppermute | solution.py:170
  12.4 5.0 %collective-permute-start.7 = (bf16[512,128]{1,0:T(8,128)(2,1)S(1)}, bf16[512,128]{1,0:T(8,128)(2,1)S(1)}, u32[]{:S(2)}, u32[]{:S(2)}) collective-permute-start(bf16[512,128]{1,0:T(8,128)(2,1)S(1)} %collective-permute-done.3.refs_8_), channel_id=1, source_target_pairs={{0,8},{8,0},{16,24},{24,16},{1,9},{9,1},{17,25},{25,17},{2,10},{10... | collective-permute-start | bytes 393224 | tf_op jit(solution)/shard_map/ppermute | solution.py:170
  17.7 5.5 %collective-permute-start.9 = (bf16[512,128]{1,0:T(8,128)(2,1)S(1)}, bf16[512,128]{1,0:T(8,128)(2,1)S(1)}, u32[]{:S(2)}, u32[]{:S(2)}) collective-permute-start(bf16[512,128]{1,0:T(8,128)(2,1)S(1)} %get-tuple-element.24.refs_5_), channel_id=1, source_target_pairs={{0,8},{8,0},{16,24},{24,16},{1,9},{9,1},{17,25},{25,17},{2,10},{10... | collective-permute-start | bytes 393224 | tf_op jit(solution)/shard_map/ppermute | solution.py:170
  19.3 6.3 %collective-permute-start.8 = (bf16[512,128]{1,0:T(8,128)(2,1)S(1)}, bf16[512,128]{1,0:T(8,128)(2,1)S(1)}, u32[]{:S(2)}, u32[]{:S(2)}) collective-permute-start(bf16[512,128]{1,0:T(8,128)(2,1)S(1)} %get-tuple-element.23.refs_4_.row_ref), channel_id=1, source_target_pairs={{0,8},{8,0},{16,24},{24,16},{1,9},{9,1},{17,25},{25,17},{2,10},{10... | collective-permute-start | bytes 393224 | tf_op jit(solution)/shard_map/ppermute | solution.py:170
  19.8 6.2 %collective-permute-start.11 = (bf16[512,128]{1,0:T(8,128)(2,1)S(1)}, bf16[512,128]{1,0:T(8,128)(2,1)S(1)}, u32[]{:S(2)}, u32[]{:S(2)}) collective-permute-start(bf16[512,128]{1,0:T(8,128)(2,1)S(1)} %get-tuple-element.24.refs_5_), channel_id=1, source_target_pairs={{0,16},{8,24},{16,0},{24,8},{1,17},{9,25},{17,1},{25,9},{2,18},{10... | collective-permute-start | bytes 393224 | tf_op jit(solution)/shard_map/ppermute | solution.py:170
  20.2 7.3 %collective-permute-start.10 = (bf16[512,128]{1,0:T(8,128)(2,1)S(1)}, bf16[512,128]{1,0:T(8,128)(2,1)S(1)}, u32[]{:S(2)}, u32[]{:S(2)}) collective-permute-start(bf16[512,128]{1,0:T(8,128)(2,1)S(1)} %get-tuple-element.23.refs_4_.row_ref), channel_id=1, source_target_pairs={{0,16},{8,24},{16,0},{24,8},{1,17},{9,25},{17,1},{25,9},{2,18},{10... | collective-permute-start | bytes 393224 | tf_op jit(solution)/shard_map/ppermute | solution.py:170
  21.8 6.7 %collective-permute-start.13 = (bf16[512,128]{1,0:T(8,128)(2,1)S(1)}, bf16[512,128]{1,0:T(8,128)(2,1)S(1)}, u32[]{:S(2)}, u32[]{:S(2)}) collective-permute-start(bf16[512,128]{1,0:T(8,128)(2,1)S(1)} %get-tuple-element.24.refs_5_), channel_id=1, source_target_pairs={{1,2},{3,4},{5,6},{2,1},{4,3},{6,5},{9,10},{11,12},{13,14},{10,9},... | collective-permute-start | bytes 393224 | tf_op jit(solution)/shard_map/ppermute | solution.py:179
  23.2 5.3 %collective-permute-start.12 = (bf16[512,128]{1,0:T(8,128)(2,1)S(1)}, bf16[512,128]{1,0:T(8,128)(2,1)S(1)}, u32[]{:S(2)}, u32[]{:S(2)}) collective-permute-start(bf16[512,128]{1,0:T(8,128)(2,1)S(1)} %shard_map.60), channel_id=1, source_target_pairs={{0,1},{1,0},{2,3},{3,2},{4,5},{5,4},{6,7},{7,6},{8,9},{9,8},{10,11... | collective-permute-start | bytes 393224 | tf_op jit(solution)/shard_map/ppermute | solution.py:179
  25.5 5.5 %collective-permute-start.14 = (bf16[512,128]{1,0:T(8,128)(2,1)S(1)}, bf16[512,128]{1,0:T(8,128)(2,1)S(1)}, u32[]{:S(2)}, u32[]{:S(2)}) collective-permute-start(bf16[512,128]{1,0:T(8,128)(2,1)S(1)} %collective-permute-done.8.refs_6_), channel_id=1, source_target_pairs={{0,16},{8,24},{16,0},{24,8},{1,17},{9,25},{17,1},{25,9},{2,18},{10... | collective-permute-start | bytes 393224 | tf_op jit(solution)/shard_map/ppermute | solution.py:170
  26.0 5.2 %collective-permute-start.15 = (bf16[512,128]{1,0:T(8,128)(2,1)S(1)}, bf16[512,128]{1,0:T(8,128)(2,1)S(1)}, u32[]{:S(2)}, u32[]{:S(2)}) collective-permute-start(bf16[512,128]{1,0:T(8,128)(2,1)S(1)} %collective-permute-done.11.refs_9_), channel_id=1, source_target_pairs={{0,8},{8,0},{16,24},{24,16},{1,9},{9,1},{17,25},{25,17},{2,10},{10... | collective-permute-start | bytes 393224 | tf_op jit(solution)/shard_map/ppermute | solution.py:170

commit v4 on v3

v4 whole, which is shorter than its diff:
```python
import functools

import jax
import jax.numpy as jnp
from jax import lax
from jax.experimental import pallas as pl
from jax.experimental.pallas import tpu as pltpu
from jax.sharding import PartitionSpec as P

F32 = jnp.float32
BF16 = jnp.bfloat16
VMEM = pl.BlockSpec(memory_space=pltpu.VMEM)
HBM = pl.BlockSpec(memory_space=pltpu.HBM)


def call(body, outs, args, in_specs=None, out_specs=None, scratch=(), flops=0):
    total = sum(a.size * a.dtype.itemsize for a in (*outs, *args))
    if in_specs:
        args = [pltpu.with_memory_space_constraint(a, pltpu.HBM) if s is HBM else a for a, s in zip(args, in_specs)]
    return pl.pallas_call(
        body,
        out_shape=outs,
        in_specs=in_specs or [VMEM] * len(args),
        out_specs=out_specs or [VMEM] * len(outs),
        scratch_shapes=list(scratch),
        compiler_params=pltpu.CompilerParams(vmem_limit_bytes=24 * 2**20),
        cost_estimate=pl.CostEstimate(flops=flops, bytes_accessed=total, transcendentals=0),
    )(*args)


def shape(dims, dtype):
    return jax.ShapeDtypeStruct(dims, dtype)


def is_first():
    return 1 - lax.axis_index("cell") % 2


def source_row(r, rows):
    return r + is_first() * (rows - 1 - 2 * r)


def prepare(rows, pop_hbm, mask_hbm, octant_hbm, courant_hbm, c_hbm, *refs):
    q_refs, (p0_ref, keep_ref, coef_ref, c_ref) = refs[:rows], refs[rows : rows + 4]
    pop_ref, mask_ref, octant_ref, courant_ref, sems = refs[rows + 4 :]
    pairs = (mask_hbm, mask_ref), (pop_hbm, pop_ref), (octant_hbm, octant_ref), (courant_hbm, courant_ref), (c_hbm, c_ref)
    copies = [pltpu.make_async_copy(*pair, sems.at[i]) for i, pair in enumerate(pairs)]
    for copy in copies:
        copy.start()
    modes = p0_ref.shape[1]
    copies[0].wait()
    copies[1].wait()
    for r in range(rows):
        source = source_row(r, rows)
        keep = (1 - mask_ref[pl.ds(source, 1), :]).astype(F32)
        row = keep * pop_ref[pl.ds(source, modes, stride=rows), :]
        keep_ref[r : r + 1, :] = keep
        p0_ref[r] = row
        q_refs[r][...] = row.astype(BF16)
    copies[2].wait()
    copies[3].wait()
    octant = octant_ref[...]
    speeds = [(1.0 - 2.0 * ((octant >> d) & 1).astype(F32)) * courant_ref[d : d + 1] for d in range(3)]
    flags = [(v < 0).astype(F32) for v in speeds]
    table = jnp.concatenate([jnp.abs(v) for v in speeds] + flags + flags[:2], axis=0)
    coef_ref[...] = table.T
    copies[4].wait()


def columns(offset, modes):
    position = lax.axis_index("mode") ^ offset
    return pl.ds(pl.multiple_of(position * modes, modes), modes)


def product(c_ref, offset, blocks):
    cols = columns(offset, blocks[0].shape[0])
    return jnp.dot(c_ref[:, cols], jnp.concatenate(blocks, axis=1), preferred_element_type=F32)


def backward_y(coef_ref):
    return (coef_ref[:, 4:5] > 0) == (is_first() == 0)


def drift(fields, coef_ref):
    rows = len(fields)
    width = fields[0].shape[1]
    ax, ay, az = (coef_ref[:, d : d + 1] for d in range(3))
    neg_x = coef_ref[:, 3:4] > 0
    after = backward_y(coef_ref)
    stay = 1.0 - (ax + ay + az)
    results = []
    for r, p in enumerate(fields):
        beside = jnp.where(neg_x, pltpu.roll(p, width - 1, 1), pltpu.roll(p, 1, 1))
        prior = fields[r - 1] if r > 0 else jnp.zeros_like(p)
        later = fields[r + 1] if r < rows - 1 else jnp.zeros_like(p)
        results.append(stay * p + ax * beside + ay * jnp.where(after, later, prior))
    return results


def near_products(q_refs, early, blocks, c_ref):
    rows = len(q_refs)
    total = product(c_ref, 0, [q[...] for q in q_refs])
    for i, offset in enumerate(early):
        total = total + product(c_ref, offset, [b[...] for b in blocks[i * rows : (i + 1) * rows]])
    width = total.shape[1] // rows
    return [total[:, r * width : (r + 1) * width] for r in range(rows)]


def far_terms(group, rows, late, refs, coef_ref, c_ref):
    ay = coef_ref[:, 1:2]
    after = backward_y(coef_ref)
    refs = list(refs)
    inner = refs.pop(0) if 0 in group else None
    outer = refs.pop(0) if rows - 1 in group else None
    count = len(group)
    blocks = [[b[...] for b in refs[i * count : (i + 1) * count]] for i in range(len(late))]
    total = sum(product(c_ref, offset, block) for offset, block in zip(late, blocks))
    results = []
    for i, r in enumerate(group):
        width = c_ref.shape[1] if not late else total.shape[1] // count
        value = -total[:, i * width : (i + 1) * width] if late else 0.0
        if r == 0:
            value = value + jnp.where(after, 0.0, ay * inner[...].astype(F32))
        if r == rows - 1:
            value = value + jnp.where(after, ay * outer[...].astype(F32), 0.0)
        results.append(value)
    return results


def first_near(rows, early, *refs):
    p0_ref, coef_ref, c_ref, *rest = refs
    q_refs, blocks, base_ref = rest[:rows], rest[rows:-1], rest[-1]
    moved = drift([p0_ref[r] for r in range(rows)], coef_ref)
    for r, value in enumerate(near_products(q_refs, early, blocks, c_ref)):
        base_ref[r] = moved[r] - value


def first_end(group, rows, late, *refs):
    base_ref, keep_ref, coef_ref, c_ref, *rest = refs
    inputs, outputs = rest[: -2 * len(group)], rest[-2 * len(group) :]
    for i, (r, term) in enumerate(zip(group, far_terms(group, rows, late, inputs, coef_ref, c_ref))):
        value = keep_ref[r : r + 1] * (base_ref[r] + term)
        outputs[2 * i][...] = value.astype(BF16)
        outputs[2 * i + 1][...] = value


def second_near(rows, early, *refs):
    p0_ref, coef_ref, c_ref, *rest = refs
    p1_refs, q_refs, blocks, base_ref = rest[:rows], rest[rows : 2 * rows], rest[2 * rows : -1], rest[-1]
    moved = drift([p[...] for p in p1_refs], coef_ref)
    for r, value in enumerate(near_products(q_refs, early, blocks, c_ref)):
        base_ref[r] = 0.5 * p0_ref[r] + 0.5 * (moved[r] - value)


def second_end(rows, late, *refs):
    base_ref, keep_ref, coef_ref, c_ref, *inputs, out_ref = refs
    modes = out_ref.shape[0] // rows
    for r, term in enumerate(far_terms(range(rows), rows, late, inputs, coef_ref, c_ref)):
        out_ref[pl.ds(source_row(r, rows), modes, stride=rows), :] = keep_ref[r : r + 1] * (base_ref[r] + 0.5 * term)


def later(row, other):
    def body(row_ref, _, out_ref):
        out_ref[...] = row_ref[...]

    (copied,) = call(body, [shape(row.shape, row.dtype)], [row, other], in_specs=[VMEM, pl.BlockSpec(memory_space=pl.ANY)])
    return copied


def exchange(row, r, count):
    bits = [1 << b for b in range(count.bit_length() - 1)]
    held = {0: row}
    for bit in bits if r % 2 == 0 else bits[::-1]:
        pairs = [(i, i ^ bit) for i in range(count)]
        held |= {o ^ bit: lax.ppermute(b, "mode", pairs) for o, b in held.items()}
    return held


def within_pair(row):
    return lax.ppermute(row, "cell", [(i, i ^ 1) for i in range(lax.axis_size("cell"))])


def between_pairs(row):
    steps = [(i, i + 1) for i in range(1, lax.axis_size("cell") - 1, 2)]
    return lax.ppermute(row, "cell", steps + [(target, source) for source, target in steps])


def on_device(populations, contact_mask, octant, courant, collision):
    modes, planes, rows, width = populations.shape
    count = lax.axis_size("mode")
    assert planes == 1 and lax.axis_size("cell") % 2 == 0 and count & (count - 1) == 0
    early = [1 << b for b in range(count.bit_length() - 1)]
    late = [o for o in range(1, count) if o not in early]
    pop = populations.reshape(modes * rows, width)
    mask = contact_mask.reshape(rows, width)
    octant = octant.reshape(1, modes)
    row_bf16 = shape((modes, width), BF16)
    all_rows = shape((rows, modes, width), F32)
    flops = 2 * modes * modes * rows * width
    near = flops * (1 + len(early))
    far = flops * len(late)

    *q, p0, keep, coef, c = call(
        functools.partial(prepare, rows),
        [row_bf16] * rows + [all_rows, shape((rows, width), F32), shape((modes, 8), F32), shape(collision.shape, BF16)],
        [pop, mask, octant, courant, collision],
        in_specs=[HBM] * 5,
        scratch=[pltpu.VMEM(a.shape, a.dtype) for a in (pop, mask, octant, courant)] + [pltpu.SemaphoreType.DMA((5,))],
    )
    last = rows - 1
    groups = [g for g in (range(last), range(last, rows)) if len(g)]
    inner = within_pair(q[0])
    gathered = [exchange(row, r, count) for r, row in enumerate(q)]
    outer = between_pairs(later(q[last], inner))
    (base,) = call(
        functools.partial(first_near, rows, early),
        [all_rows],
        [p0, coef, c, *q, *(g[o] for o in early for g in gathered)],
        flops=near,
    )
    q, p1, held = [], [], []
    for group in groups:
        halo = [inner] * (0 in group) + [outer] * (last in group)
        results = call(
            functools.partial(first_end, group, rows, late),
            [row_bf16, shape((modes, width), F32)] * len(group),
            [base, keep, coef, c, *halo, *(gathered[r][o] for o in late for r in group)],
            flops=far,
        )
        q += results[::2]
        p1 += results[1::2]
        if 0 in group:
            second_inner = within_pair(q[0])
        held += [exchange(q[r], r, count) for r in group]
    inner, gathered = second_inner, held
    outer = between_pairs(later(q[last], inner))
    (base,) = call(
        functools.partial(second_near, rows, early),
        [all_rows],
        [p0, coef, c, *p1, *q, *(g[o] for o in early for g in gathered)],
        flops=near,
    )
    (out,) = call(
        functools.partial(second_end, rows, late),
        [shape((modes * rows, width), F32)],
        [base, keep, coef, c, inner, outer, *(g[o] for o in late for g in gathered)],
        flops=far,
    )
    return out.reshape(populations.shape)


def solution(mesh):
    placed = (
        P("mode", None, "cell", None),
        P(None, "cell", None),
        P("mode"),
        P(None, "mode"),
        P("mode", None),
    )
    return jax.shard_map(
        on_device,
        mesh=mesh,
        in_specs=placed,
        out_specs=P("mode", None, "cell", None),
        check_vma=False,
    )
```

time: 32.5 us -> 31.9 us (0.982)
  the two profiles are of different devices: /device:TPU:0 before, /device:TPU:1 now
where the time goes in v4:
time: 31.9 us; the launch traced here: 31.3 us
  starting transfers between devices  21 us (66%)
  Pallas kernels  5.65 us (18%)
  waiting for transfers between devices  4.53 us (14%)
    ppermute x12, starting transfers between devices, exchange(): held |= {o ^ bit: lax.ppermute(b, 'mode', pairs) for o, b in held.items()}  10.1 us
    ppermute x2, starting transfers between devices, between_pairs(): lax.ppermute(row, 'cell', steps + [(target, source) for source, target in...  9.94 us
    pallas_call x8, Pallas kernels, call(): pl.pallas_call(body, out_shape=outs, in_specs=in_specs or [VMEM] * len(ar...  5.65 us
    ppermute x12, waiting for transfers between devices, exchange(): held |= {o ^ bit: lax.ppermute(b, 'mode', pairs) for o, b in held.items()}  3.23 us
    ppermute x2, waiting for transfers between devices, between_pairs(): lax.ppermute(row, 'cell', steps + [(target, source) for source, target in...  1.29 us
    ppermute x2, starting transfers between devices, within_pair(): lax.ppermute(row, 'cell', [(i, i ^ 1) for i in range(lax.axis_size('cell'...  0.99 us
  transfers between devices with their start and end apart: 16, of which 6 were waited for; matrix products, arithmetic and copies ran while one was open for 0% of the time, Pallas kernels for 8%

profile of v4, /device:TPU:1, one launch (start us, length us, event | category | flops | bytes accessed | tf_op | source)
XLA Modules:
  0.0 31.3 jit_solution(5910745260258420724)
XLA Ops:
  0.0 1.9 %shard_map.55 = (bf16[512,128]{1,0:T(8,128)(2,1)S(1)}, bf16[512,128]{1,0:T(8,128)(2,1)S(1)}, f32[2,512,128]{2,1,0:T(8,128)S(1)}, f32[2,128]{1,0:T(2,128)S(1)}, f...) custom-call(f32[1024,128]{1,0:T(8,128)} %bitcast.6, s32[2,128]{1,0:T(2,128)} %bitcast.8, s32[1,512]{1,0:T(1,128)} %bitcast.7, ...), custom_call_target="tpu_custom_call" | custom-call | bytes 5531648 | tf_op jit(solution)/shard_map/pallas_call | solution.py:20
  1.9 2.1 %collective-permute-start = (bf16[512,128]{1,0:T(8,128)(2,1)S(1)}, bf16[512,128]{1,0:T(8,128)(2,1)S(1)}, u32[]{:S(2)}, u32[]{:S(2)}) collective-permute-start(bf16[512,128]{1,0:T(8,128)(2,1)S(1)} %get-tuple-element.18.refs_3_), channel_id=1, source_target_pairs={{0,8},{8,0},{16,24},{24,16},{1,9},{9,1},{17,25},{25,17},{2,10},{10... | collective-permute-start | bytes 393224 | tf_op jit(solution)/shard_map/ppermute | solution.py:175
  4.0 1.0 %collective-permute-start.4 = (bf16[512,128]{1,0:T(8,128)(2,1)S(1)}, bf16[512,128]{1,0:T(8,128)(2,1)S(1)}, u32[]{:S(2)}, u32[]{:S(2)}) collective-permute-start(bf16[512,128]{1,0:T(8,128)(2,1)S(1)} %get-tuple-element.18.refs_3_), channel_id=1, source_target_pairs={{0,1},{1,0},{2,3},{3,2},{4,5},{5,4},{6,7},{7,6},{8,9},{9,8},{10,11... | collective-permute-start | bytes 393224 | tf_op jit(solution)/shard_map/ppermute | solution.py:180
  4.9 1.2 %collective-permute-start.3 = (bf16[512,128]{1,0:T(8,128)(2,1)S(1)}, bf16[512,128]{1,0:T(8,128)(2,1)S(1)}, u32[]{:S(2)}, u32[]{:S(2)}) collective-permute-start(bf16[512,128]{1,0:T(8,128)(2,1)S(1)} %get-tuple-element.19.refs_4_.row_ref), channel_id=1, source_target_pairs={{0,16},{8,24},{16,0},{24,8},{1,17},{9,25},{17,1},{25,9},{2,18},{10... | collective-permute-start | bytes 393224 | tf_op jit(solution)/shard_map/ppermute | solution.py:175
  6.2 0.3 collective-permute-start.1
  6.4 0.0 collective-permute-start.2
  6.4 0.8 %collective-permute-done.refs_5_ = bf16[512,128]{1,0:T(8,128)(2,1)S(1)} collective-permute-done((bf16[512,128]{1,0:T(8,128)(2,1)S(1)}, bf16[512,128]{1,0:T(8,128)(2,1)S(1)}, u32[]{:S(2)}, u32[]{:S(2)}) %collective-permute-start) | collective-permute-done | bytes 131104 | tf_op jit(solution)/shard_map/ppermute | solution.py:175
  7.2 1.2 %collective-permute-start.5 = (bf16[512,128]{1,0:T(8,128)(2,1)S(1)}, bf16[512,128]{1,0:T(8,128)(2,1)S(1)}, u32[]{:S(2)}, u32[]{:S(2)}) collective-permute-start(bf16[512,128]{1,0:T(8,128)(2,1)S(1)} %collective-permute-done.refs_5_), channel_id=1, source_target_pairs={{0,16},{8,24},{16,0},{24,8},{1,17},{9,25},{17,1},{25,9},{2,18},{10... | collective-permute-start | bytes 393224 | tf_op jit(solution)/shard_map/ppermute | solution.py:175
  8.4 0.0 collective-permute-done.4.refs_4_._
  8.4 5.3 %collective-permute-start.6 = (bf16[512,128]{1,0:T(8,128)(2,1)S(1)}, bf16[512,128]{1,0:T(8,128)(2,1)S(1)}, u32[]{:S(2)}, u32[]{:S(2)}) collective-permute-start(bf16[512,128]{1,0:T(8,128)(2,1)S(1)} %shard_map.58), channel_id=1, source_target_pairs={{1,2},{3,4},{5,6},{2,1},{4,3},{6,5},{9,10},{11,12},{13,14},{10,9},... | collective-permute-start | bytes 393224 | tf_op jit(solution)/shard_map/ppermute | solution.py:185
  13.7 0.0 collective-permute-done.3.refs_8_
  13.7 2.0 %collective-permute-start.7 = (bf16[512,128]{1,0:T(8,128)(2,1)S(1)}, bf16[512,128]{1,0:T(8,128)(2,1)S(1)}, u32[]{:S(2)}, u32[]{:S(2)}) collective-permute-start(bf16[512,128]{1,0:T(8,128)(2,1)S(1)} %collective-permute-done.3.refs_8_), channel_id=1, source_target_pairs={{0,8},{8,0},{16,24},{24,16},{1,9},{9,1},{17,25},{25,17},{2,10},{10... | collective-permute-start | bytes 393224 | tf_op jit(solution)/shard_map/ppermute | solution.py:175
  15.7 0.0 collective-permute-done.1.refs_6_
  15.7 0.0 collective-permute-done.2.refs_7_
  15.7 1.0 %shard_map.56.refs_0_ = f32[2,512,128]{2,1,0:T(8,128)S(1)} custom-call(f32[2,512,128]{2,1,0:T(8,128)S(1)} %get-tuple-element.15.refs_0_, f32[512,8]{1,0:T(8,128)S(1)} %get-tuple-element.16.refs_1_.refs_2_, bf16[512,2048]{1,0:T(8,128)(2,1)S(1)} %get-tuple-element.17.refs_2_.refs_3_, bf16[512,128]{1,0:T(8,128)(2,1)S(1)} %get-tuple-element.18.refs_3_, ...), custom_call_target="tpu_custom_call" | custom-call | flops 402653184 | bytes 3948544 | tf_op jit(solution)/shard_map/pallas_call | solution.py:20
  16.7 0.0 collective-permute-done.5.refs_5_
  16.7 0.3 %shard_map.57 = (bf16[512,128]{1,0:T(8,128)(2,1)S(1)}, f32[512,128]{1,0:T(8,128)S(1)}) custom-call(f32[2,512,128]{2,1,0:T(8,128)S(1)} %shard_map.56.refs_0_, f32[2,128]{1,0:T(2,128)S(1)} %get-tuple-element.20.refs_1_, f32[512,8]{1,0:T(8,128)S(1)} %get-tuple-element.16.refs_1_.refs_2_, bf16[512,2048]{1,0:T(8,128)(2,1)S(1)} %get-tuple-element.17.refs_2_.refs_3_, ...), custom_call_target="tpu_custom_call" | custom-call | flops 134217728 | bytes 3294208 | tf_op jit(solution)/shard_map/pallas_call | solution.py:20
  17.1 0.1 collective-permute-start.8
  17.2 0.0 collective-permute-start.12
  17.2 0.0 collective-permute-done.6.refs_4_
  17.2 0.9 %collective-permute-done.7.refs_5_ = bf16[512,128]{1,0:T(8,128)(2,1)S(1)} collective-permute-done((bf16[512,128]{1,0:T(8,128)(2,1)S(1)}, bf16[512,128]{1,0:T(8,128)(2,1)S(1)}, u32[]{:S(2)}, u32[]{:S(2)}) %collective-permute-start.7) | collective-permute-done | bytes 131104 | tf_op jit(solution)/shard_map/ppermute | solution.py:175
  18.1 0.3 %shard_map.59 = (bf16[512,128]{1,0:T(8,128)(2,1)S(1)}, f32[512,128]{1,0:T(8,128)S(1)}) custom-call(f32[2,512,128]{2,1,0:T(8,128)S(1)} %shard_map.56.refs_0_, f32[2,128]{1,0:T(2,128)S(1)} %get-tuple-element.20.refs_1_, f32[512,8]{1,0:T(8,128)S(1)} %get-tuple-element.16.refs_1_.refs_2_, bf16[512,2048]{1,0:T(8,128)(2,1)S(1)} %get-tuple-element.17.refs_2_.refs_3_, ...), custom_call_target="tpu_custom_call" | custom-call | flops 134217728 | bytes 3294208 | tf_op jit(solution)/shard_map/pallas_call | solution.py:20
  18.4 0.6 %collective-permute-start.11 = (bf16[512,128]{1,0:T(8,128)(2,1)S(1)}, bf16[512,128]{1,0:T(8,128)(2,1)S(1)}, u32[]{:S(2)}, u32[]{:S(2)}) collective-permute-start(bf16[512,128]{1,0:T(8,128)(2,1)S(1)} %get-tuple-element.24.refs_6_.row_ref), channel_id=1, source_target_pairs={{0,16},{8,24},{16,0},{24,8},{1,17},{9,25},{17,1},{25,9},{2,18},{10... | collective-permute-start | bytes 393224 | tf_op jit(solution)/shard_map/ppermute | solution.py:175
  19.0 1.2 %collective-permute-start.9 = (bf16[512,128]{1,0:T(8,128)(2,1)S(1)}, bf16[512,128]{1,0:T(8,128)(2,1)S(1)}, u32[]{:S(2)}, u32[]{:S(2)}) collective-permute-start(bf16[512,128]{1,0:T(8,128)(2,1)S(1)} %get-tuple-element.24.refs_6_.row_ref), channel_id=1, source_target_pairs={{0,8},{8,0},{16,24},{24,16},{1,9},{9,1},{17,25},{25,17},{2,10},{10... | collective-permute-start | bytes 393224 | tf_op jit(solution)/shard_map/ppermute | solution.py:175
  20.2 1.2 %collective-permute-start.10 = (bf16[512,128]{1,0:T(8,128)(2,1)S(1)}, bf16[512,128]{1,0:T(8,128)(2,1)S(1)}, u32[]{:S(2)}, u32[]{:S(2)}) collective-permute-start(bf16[512,128]{1,0:T(8,128)(2,1)S(1)} %get-tuple-element.23.refs_5_), channel_id=1, source_target_pairs={{0,16},{8,24},{16,0},{24,8},{1,17},{9,25},{17,1},{25,9},{2,18},{10... | collective-permute-start | bytes 393224 | tf_op jit(solution)/shard_map/ppermute | solution.py:175
  21.4 0.0 collective-permute-done.12._.refs_4_
  21.4 4.6 %collective-permute-start.13 = (bf16[512,128]{1,0:T(8,128)(2,1)S(1)}, bf16[512,128]{1,0:T(8,128)(2,1)S(1)}, u32[]{:S(2)}, u32[]{:S(2)}) collective-permute-start(bf16[512,128]{1,0:T(8,128)(2,1)S(1)} %shard_map.61), channel_id=1, source_target_pairs={{1,2},{3,4},{5,6},{2,1},{4,3},{6,5},{9,10},{11,12},{13,14},{10,9},... | collective-permute-start | bytes 393224 | tf_op jit(solution)/shard_map/ppermute | solution.py:185
  26.1 0.0 collective-permute-done.8.refs_7_
  26.1 0.1 collective-permute-start.14
  26.2 0.0 collective-permute-done.11.refs_10_
  26.2 0.1 collective-permute-start.15
  26.3 0.0 collective-permute-done.9.refs_8_
  26.3 0.4 %collective-permute-done.10.refs_9_ = bf16[512,128]{1,0:T(8,128)(2,1)S(1)} collective-permute-done((bf16[512,128]{1,0:T(8,128)(2,1)S(1)}, bf16[512,128]{1,0:T(8,128)(2,1)S(1)}, u32[]{:S(2)}, u32[]{:S(2)}) %collective-permute-start.10) | collective-permute-done | bytes 131104 | tf_op jit(solution)/shard_map/ppermute | solution.py:175
  26.7 1.0 %shard_map.60.refs_0_ = f32[2,512,128]{2,1,0:T(8,128)S(1)} custom-call(f32[2,512,128]{2,1,0:T(8,128)S(1)} %get-tuple-element.15.refs_0_, f32[512,8]{1,0:T(8,128)S(1)} %get-tuple-element.16.refs_1_.refs_2_, bf16[512,2048]{1,0:T(8,128)(2,1)S(1)} %get-tuple-element.17.refs_2_.refs_3_, f32[512,128]{1,0:T(8,128)S(1)} %get-tuple-element.21.refs_3_, ...), custom_call_target="tpu_custom_call" | custom-call | flops 402653184 | bytes 4472832 | tf_op jit(solution)/shard_map/pallas_call | solution.py:20
  27.7 1.3 %collective-permute-done.13.refs_5_ = bf16[512,128]{1,0:T(8,128)(2,1)S(1)} collective-permute-done((bf16[512,128]{1,0:T(8,128)(2,1)S(1)}, bf16[512,128]{1,0:T(8,128)(2,1)S(1)}, u32[]{:S(2)}, u32[]{:S(2)}) %collective-permute-start.13) | collective-permute-done | bytes 131104 | tf_op jit(solution)/shard_map/ppermute | solution.py:185
  29.0 1.0 %collective-permute-done.14.refs_6_ = bf16[512,128]{1,0:T(8,128)(2,1)S(1)} collective-permute-done((bf16[512,128]{1,0:T(8,128)(2,1)S(1)}, bf16[512,128]{1,0:T(8,128)(2,1)S(1)}, u32[]{:S(2)}, u32[]{:S(2)}) %collective-permute-start.14) | collective-permute-done | bytes 131104 | tf_op jit(solution)/shard_map/ppermute | solution.py:175
  30.0 0.2 collective-permute-done.15.refs_7_
  30.2 1.1 %shard_map.62 = f32[1024,128]{1,0:T(8,128)} custom-call(f32[2,512,128]{2,1,0:T(8,128)S(1)} %shard_map.60.refs_0_, f32[2,128]{1,0:T(2,128)S(1)} %get-tuple-element.20.refs_1_, f32[512,8]{1,0:T(8,128)S(1)} %get-tuple-element.16.refs_1_.refs_2_, bf16[512,2048]{1,0:T(8,128)(2,1)S(1)} %get-tuple-element.17.refs_2_.refs_3_, ...), custom_call_target="tpu_custom_call" | custom-call | flops 134217728 | bytes 3687424 | tf_op jit(solution)/shard_map/pallas_call | solution.py:20
  (2 shorter events, 0.0 us)
Async XLA Ops:
  1.9 5.3 %collective-permute-start = (bf16[512,128]{1,0:T(8,128)(2,1)S(1)}, bf16[512,128]{1,0:T(8,128)(2,1)S(1)}, u32[]{:S(2)}, u32[]{:S(2)}) collective-permute-start(bf16[512,128]{1,0:T(8,128)(2,1)S(1)} %get-tuple-element.18.refs_3_), channel_id=1, source_target_pairs={{0,8},{8,0},{16,24},{24,16},{1,9},{9,1},{17,25},{25,17},{2,10},{10... | collective-permute-start | bytes 393224 | tf_op jit(solution)/shard_map/ppermute | solution.py:175
  4.0 4.4 %collective-permute-start.4 = (bf16[512,128]{1,0:T(8,128)(2,1)S(1)}, bf16[512,128]{1,0:T(8,128)(2,1)S(1)}, u32[]{:S(2)}, u32[]{:S(2)}) collective-permute-start(bf16[512,128]{1,0:T(8,128)(2,1)S(1)} %get-tuple-element.18.refs_3_), channel_id=1, source_target_pairs={{0,1},{1,0},{2,3},{3,2},{4,5},{5,4},{6,7},{7,6},{8,9},{9,8},{10,11... | collective-permute-start | bytes 393224 | tf_op jit(solution)/shard_map/ppermute | solution.py:180
  4.9 8.8 %collective-permute-start.3 = (bf16[512,128]{1,0:T(8,128)(2,1)S(1)}, bf16[512,128]{1,0:T(8,128)(2,1)S(1)}, u32[]{:S(2)}, u32[]{:S(2)}) collective-permute-start(bf16[512,128]{1,0:T(8,128)(2,1)S(1)} %get-tuple-element.19.refs_4_.row_ref), channel_id=1, source_target_pairs={{0,16},{8,24},{16,0},{24,8},{1,17},{9,25},{17,1},{25,9},{2,18},{10... | collective-permute-start | bytes 393224 | tf_op jit(solution)/shard_map/ppermute | solution.py:175
  6.2 9.6 %collective-permute-start.1 = (bf16[512,128]{1,0:T(8,128)(2,1)S(1)}, bf16[512,128]{1,0:T(8,128)(2,1)S(1)}, u32[]{:S(2)}, u32[]{:S(2)}) collective-permute-start(bf16[512,128]{1,0:T(8,128)(2,1)S(1)} %get-tuple-element.19.refs_4_.row_ref), channel_id=1, source_target_pairs={{0,8},{8,0},{16,24},{24,16},{1,9},{9,1},{17,25},{25,17},{2,10},{10... | collective-permute-start | bytes 393224 | tf_op jit(solution)/shard_map/ppermute | solution.py:175
  6.4 9.3 %collective-permute-start.2 = (bf16[512,128]{1,0:T(8,128)(2,1)S(1)}, bf16[512,128]{1,0:T(8,128)(2,1)S(1)}, u32[]{:S(2)}, u32[]{:S(2)}) collective-permute-start(bf16[512,128]{1,0:T(8,128)(2,1)S(1)} %get-tuple-element.18.refs_3_), channel_id=1, source_target_pairs={{0,16},{8,24},{16,0},{24,8},{1,17},{9,25},{17,1},{25,9},{2,18},{10... | collective-permute-start | bytes 393224 | tf_op jit(solution)/shard_map/ppermute | solution.py:175
  7.2 9.5 %collective-permute-start.5 = (bf16[512,128]{1,0:T(8,128)(2,1)S(1)}, bf16[512,128]{1,0:T(8,128)(2,1)S(1)}, u32[]{:S(2)}, u32[]{:S(2)}) collective-permute-start(bf16[512,128]{1,0:T(8,128)(2,1)S(1)} %collective-permute-done.refs_5_), channel_id=1, source_target_pairs={{0,16},{8,24},{16,0},{24,8},{1,17},{9,25},{17,1},{25,9},{2,18},{10... | collective-permute-start | bytes 393224 | tf_op jit(solution)/shard_map/ppermute | solution.py:175
  8.4 8.9 %collective-permute-start.6 = (bf16[512,128]{1,0:T(8,128)(2,1)S(1)}, bf16[512,128]{1,0:T(8,128)(2,1)S(1)}, u32[]{:S(2)}, u32[]{:S(2)}) collective-permute-start(bf16[512,128]{1,0:T(8,128)(2,1)S(1)} %shard_map.58), channel_id=1, source_target_pairs={{1,2},{3,4},{5,6},{2,1},{4,3},{6,5},{9,10},{11,12},{13,14},{10,9},... | collective-permute-start | bytes 393224 | tf_op jit(solution)/shard_map/ppermute | solution.py:185
  13.7 4.4 %collective-permute-start.7 = (bf16[512,128]{1,0:T(8,128)(2,1)S(1)}, bf16[512,128]{1,0:T(8,128)(2,1)S(1)}, u32[]{:S(2)}, u32[]{:S(2)}) collective-permute-start(bf16[512,128]{1,0:T(8,128)(2,1)S(1)} %collective-permute-done.3.refs_8_), channel_id=1, source_target_pairs={{0,8},{8,0},{16,24},{24,16},{1,9},{9,1},{17,25},{25,17},{2,10},{10... | collective-permute-start | bytes 393224 | tf_op jit(solution)/shard_map/ppermute | solution.py:175
  17.1 9.0 %collective-permute-start.8 = (bf16[512,128]{1,0:T(8,128)(2,1)S(1)}, bf16[512,128]{1,0:T(8,128)(2,1)S(1)}, u32[]{:S(2)}, u32[]{:S(2)}) collective-permute-start(bf16[512,128]{1,0:T(8,128)(2,1)S(1)} %get-tuple-element.23.refs_5_), channel_id=1, source_target_pairs={{0,8},{8,0},{16,24},{24,16},{1,9},{9,1},{17,25},{25,17},{2,10},{10... | collective-permute-start | bytes 393224 | tf_op jit(solution)/shard_map/ppermute | solution.py:175
  17.2 4.2 %collective-permute-start.12 = (bf16[512,128]{1,0:T(8,128)(2,1)S(1)}, bf16[512,128]{1,0:T(8,128)(2,1)S(1)}, u32[]{:S(2)}, u32[]{:S(2)}) collective-permute-start(bf16[512,128]{1,0:T(8,128)(2,1)S(1)} %get-tuple-element.23.refs_5_), channel_id=1, source_target_pairs={{0,1},{1,0},{2,3},{3,2},{4,5},{5,4},{6,7},{7,6},{8,9},{9,8},{10,11... | collective-permute-start | bytes 393224 | tf_op jit(solution)/shard_map/ppermute | solution.py:180
  18.4 7.8 %collective-permute-start.11 = (bf16[512,128]{1,0:T(8,128)(2,1)S(1)}, bf16[512,128]{1,0:T(8,128)(2,1)S(1)}, u32[]{:S(2)}, u32[]{:S(2)}) collective-permute-start(bf16[512,128]{1,0:T(8,128)(2,1)S(1)} %get-tuple-element.24.refs_6_.row_ref), channel_id=1, source_target_pairs={{0,16},{8,24},{16,0},{24,8},{1,17},{9,25},{17,1},{25,9},{2,18},{10... | collective-permute-start | bytes 393224 | tf_op jit(solution)/shard_map/ppermute | solution.py:175
  19.0 7.3 %collective-permute-start.9 = (bf16[512,128]{1,0:T(8,128)(2,1)S(1)}, bf16[512,128]{1,0:T(8,128)(2,1)S(1)}, u32[]{:S(2)}, u32[]{:S(2)}) collective-permute-start(bf16[512,128]{1,0:T(8,128)(2,1)S(1)} %get-tuple-element.24.refs_6_.row_ref), channel_id=1, source_target_pairs={{0,8},{8,0},{16,24},{24,16},{1,9},{9,1},{17,25},{25,17},{2,10},{10... | collective-permute-start | bytes 393224 | tf_op jit(solution)/shard_map/ppermute | solution.py:175
  20.2 6.5 %collective-permute-start.10 = (bf16[512,128]{1,0:T(8,128)(2,1)S(1)}, bf16[512,128]{1,0:T(8,128)(2,1)S(1)}, u32[]{:S(2)}, u32[]{:S(2)}) collective-permute-start(bf16[512,128]{1,0:T(8,128)(2,1)S(1)} %get-tuple-element.23.refs_5_), channel_id=1, source_target_pairs={{0,16},{8,24},{16,0},{24,8},{1,17},{9,25},{17,1},{25,9},{2,18},{10... | collective-permute-start | bytes 393224 | tf_op jit(solution)/shard_map/ppermute | solution.py:175
  21.4 7.6 %collective-permute-start.13 = (bf16[512,128]{1,0:T(8,128)(2,1)S(1)}, bf16[512,128]{1,0:T(8,128)(2,1)S(1)}, u32[]{:S(2)}, u32[]{:S(2)}) collective-permute-start(bf16[512,128]{1,0:T(8,128)(2,1)S(1)} %shard_map.61), channel_id=1, source_target_pairs={{1,2},{3,4},{5,6},{2,1},{4,3},{6,5},{9,10},{11,12},{13,14},{10,9},... | collective-permute-start | bytes 393224 | tf_op jit(solution)/shard_map/ppermute | solution.py:185
  26.1 3.9 %collective-permute-start.14 = (bf16[512,128]{1,0:T(8,128)(2,1)S(1)}, bf16[512,128]{1,0:T(8,128)(2,1)S(1)}, u32[]{:S(2)}, u32[]{:S(2)}) collective-permute-start(bf16[512,128]{1,0:T(8,128)(2,1)S(1)} %collective-permute-done.8.refs_7_), channel_id=1, source_target_pairs={{0,16},{8,24},{16,0},{24,8},{1,17},{9,25},{17,1},{25,9},{2,18},{10... | collective-permute-start | bytes 393224 | tf_op jit(solution)/shard_map/ppermute | solution.py:175
  26.2 4.0 %collective-permute-start.15 = (bf16[512,128]{1,0:T(8,128)(2,1)S(1)}, bf16[512,128]{1,0:T(8,128)(2,1)S(1)}, u32[]{:S(2)}, u32[]{:S(2)}) collective-permute-start(bf16[512,128]{1,0:T(8,128)(2,1)S(1)} %collective-permute-done.11.refs_10_), channel_id=1, source_target_pairs={{0,8},{8,0},{16,24},{24,16},{1,9},{9,1},{17,25},{25,17},{2,10},{10... | collective-permute-start | bytes 393224 | tf_op jit(solution)/shard_map/ppermute | solution.py:175

commit v5 on v0

v5 whole, which is shorter than its diff:
```python
import functools

import jax
import jax.numpy as jnp
from jax import lax
from jax.experimental import pallas as pl
from jax.experimental.pallas import tpu as pltpu
from jax.sharding import PartitionSpec as P

F32 = jnp.float32
BF16 = jnp.bfloat16
ANY = pl.BlockSpec(memory_space=pl.ANY)
HBM = pl.BlockSpec(memory_space=pltpu.HBM)
VMEM = pl.BlockSpec(memory_space=pltpu.VMEM)


def shape(dims, dtype):
    return jax.ShapeDtypeStruct(dims, dtype)


def call(body, ins, outs, hbm=(), after=(), scratch=(), flops=0):
    names, out_names = list(ins), list(outs)
    args = [pltpu.with_memory_space_constraint(ins[n], pltpu.HBM) if n in hbm else ins[n] for n in names]
    args += list(after)
    total = sum(a.size * a.dtype.itemsize for a in (*outs.values(), *args))

    def kernel(*refs):
        a, b = len(args), len(args) + len(outs)
        body(dict(zip(names, refs)), dict(zip(out_names, refs[a:b])), *refs[b:])

    results = pl.pallas_call(
        kernel,
        out_shape=list(outs.values()),
        in_specs=[HBM if n in hbm else VMEM for n in names] + [ANY] * len(after),
        out_specs=[VMEM] * len(outs),
        scratch_shapes=list(scratch),
        compiler_params=pltpu.CompilerParams(vmem_limit_bytes=24 * 2**20),
        cost_estimate=pl.CostEstimate(flops=flops, bytes_accessed=total, transcendentals=0),
    )(*args)
    return dict(zip(out_names, results))


def is_first():
    return 1 - lax.axis_index("cell") % 2


def source_row(r, rows):
    return r + is_first() * (rows - 1 - 2 * r)


def prepare(rows, ins, outs, pop, mask, sems):
    copies = [
        pltpu.make_async_copy(ins["mask"], mask, sems.at[0]),
        pltpu.make_async_copy(ins["pop"], pop, sems.at[1]),
    ]
    for copy in copies:
        copy.start()
    for copy in copies:
        copy.wait()
    modes = outs["p0"].shape[0]
    for r in range(rows):
        source = source_row(r, rows)
        keep = (1 - mask[pl.ds(source, 1), :]).astype(F32)
        row = keep * pop[pl.ds(source, modes, stride=rows), :]
        outs["keep"][r : r + 1, :] = keep
        outs[f"p{r}"][...] = row
        outs[f"q{r}"][...] = row.astype(BF16)


def coefficients(octant, courant):
    speeds = [(1.0 - 2.0 * ((octant >> d) & 1).astype(F32)) * courant[d : d + 1] for d in range(3)]
    flags = [(v < 0).astype(F32) for v in speeds]
    return jnp.concatenate([jnp.abs(v) for v in speeds] + flags + flags[:2], axis=0).T


def backward_y(coef):
    return (coef[:, 4:5] > 0) == (is_first() == 0)


def drift(fields, r, coef):
    p = fields[r]
    width = p.shape[1]
    ax, ay, az = (coef[:, d : d + 1] for d in range(3))
    beside = jnp.where(coef[:, 3:4] > 0, pltpu.roll(p, width - 1, 1), pltpu.roll(p, 1, 1))
    prior = fields[r - 1] if r > 0 else jnp.zeros_like(p)
    later = fields[r + 1] if r < len(fields) - 1 else jnp.zeros_like(p)
    return (1.0 - (ax + ay + az)) * p + ax * beside + ay * jnp.where(backward_y(coef), later, prior)


def product(c, offset, blocks):
    modes = blocks[0].shape[0]
    position = lax.axis_index("mode") ^ offset
    cols = pl.ds(pl.multiple_of(position * modes, modes), modes)
    return jnp.dot(c[:, cols], jnp.concatenate(blocks, axis=1), preferred_element_type=F32)


def begin(rows, ins, outs, octant, courant, sems):
    copies = [
        pltpu.make_async_copy(ins["octant"], octant, sems.at[0]),
        pltpu.make_async_copy(ins["courant"], courant, sems.at[1]),
        pltpu.make_async_copy(ins["collision"], outs["c"], sems.at[2]),
    ]
    for copy in copies:
        copy.start()
    copies[0].wait()
    copies[1].wait()
    coef = coefficients(octant[...], courant[...])
    outs["coef"][...] = coef
    fields = [ins[f"p{r}"][...] for r in range(rows)]
    for r in range(rows):
        outs[f"sum{r}"][...] = drift(fields, r, coef)
    copies[2].wait()


def step(rows, which, moves, keys, halos, ends, second, ins, outs):
    values = {r: 0.0 if moves else ins[f"sum{r}"][...] for r in which}
    if moves:
        fields = [ins[f"p{r}"][...] for r in range(rows)]
        values = {r: drift(fields, r, ins["coef"]) for r in which}
    if "inner" in halos:
        values[0] += jnp.where(backward_y(ins["coef"]), 0.0, ins["coef"][:, 1:2] * ins["inner"][...].astype(F32))
    if "outer" in halos:
        values[rows - 1] += jnp.where(backward_y(ins["coef"]), ins["coef"][:, 1:2] * ins["outer"][...].astype(F32), 0.0)
    for offset in sorted({o for o, _ in keys}):
        having = [r for r in which if (offset, r) in keys]
        result = product(ins["c"], offset, [ins[f"b{offset}_{r}"][...] for r in having])
        width = result.shape[1] // len(having)
        for i, r in enumerate(having):
            values[r] = values[r] - result[:, i * width : (i + 1) * width]
    for r, value in values.items():
        if not ends:
            outs[f"sum{r}"][...] = value
        elif not second:
            value = ins["keep"][r : r + 1] * value
            outs[f"p{r}"][...] = value
            outs[f"q{r}"][...] = value.astype(BF16)
        else:
            modes = outs["out"].shape[0] // rows
            value = ins["keep"][r : r + 1] * (0.5 * ins[f"first{r}"][...] + 0.5 * value)
            outs["out"][pl.ds(source_row(r, rows), modes, stride=rows), :] = value


def held(row, other):
    def body(ins, outs):
        outs["row"][...] = ins["row"][...]

    return call(body, {"row": row}, {"row": shape(row.shape, row.dtype)}, after=[other])["row"]


def exchange(row, bits, count, other=None):
    blocks = {0: row}
    for i, bit in enumerate(bits):
        pairs = [(j, j ^ bit) for j in range(count)]
        for offset, block in list(blocks.items()):
            if i and offset and other is not None:
                block = held(block, other)
            blocks[offset ^ bit] = lax.ppermute(block, "mode", pairs)
    return blocks


def within_pair(row):
    return lax.ppermute(row, "cell", [(i, i ^ 1) for i in range(lax.axis_size("cell"))])


def between_pairs(row):
    steps = [(i, i + 1) for i in range(1, lax.axis_size("cell") - 1, 2)]
    return lax.ppermute(row, "cell", steps + [(target, source) for source, target in steps])


def on_device(populations, contact_mask, octant, courant, collision):
    modes, planes, rows, width = populations.shape
    count = lax.axis_size("mode")
    assert planes == 1 and lax.axis_size("cell") % 2 == 0 and count & (count - 1) == 0
    last = rows - 1
    bits = [1 << b for b in range(count.bit_length() - 1)]
    orders = [bits if r % 2 == 0 else bits[::-1] for r in range(rows)]
    row_f32, row_bf16 = shape((modes, width), F32), shape((modes, width), BF16)
    keys = [(o, r) for r in range(rows) for o in range(count)]
    near = [(o, r) for o, r in keys if o == 0 or o in bits]
    far = [key for key in keys if key not in near]

    pop, mask = populations.reshape(modes * rows, width), contact_mask.reshape(rows, width)
    outs = {"keep": shape((rows, width), F32)}
    for r in range(rows):
        outs |= {f"p{r}": row_f32, f"q{r}": row_bf16}
    env = call(
        functools.partial(prepare, rows),
        {"pop": pop, "mask": mask},
        outs,
        hbm=("pop", "mask"),
        scratch=[pltpu.VMEM(pop.shape, F32), pltpu.VMEM(mask.shape, jnp.int32), pltpu.SemaphoreType.DMA((2,))],
    )
    first = {f"first{r}": env[f"p{r}"] for r in range(rows)}

    def run(blocks, which, moves, keys, halos, ends, second):
        names = [f"p{r}" for r in range(rows)] if moves else [f"sum{r}" for r in which]
        names += [*halos] + ["coef"] * (moves or len(halos) > 0) + ["c"] * (len(keys) > 0) + ["keep"] * ends
        ins = {n: env[n] for n in names} | {f"b{o}_{r}": blocks[r][o] for o, r in keys}
        if not ends:
            outs = {f"sum{r}": row_f32 for r in which}
        elif not second:
            outs = {f"p{r}": row_f32 for r in which} | {f"q{r}": row_bf16 for r in which}
        else:
            ins |= first
            outs = {"out": shape((modes * rows, width), F32)}
        body = functools.partial(step, rows, which, moves, keys, halos, ends, second)
        env.update(call(body, ins, outs, flops=2 * modes * modes * width * len(keys)))

    env["inner"] = within_pair(env["q0"])
    env |= call(
        functools.partial(begin, rows),
        {"octant": octant.reshape(1, modes), "courant": courant, "collision": collision}
        | {f"p{r}": env[f"p{r}"] for r in range(rows)},
        {"c": shape(collision.shape, BF16), "coef": shape((modes, 8), F32)} | {f"sum{r}": row_f32 for r in range(rows)},
        hbm=("octant", "courant", "collision"),
        scratch=[pltpu.VMEM((1, modes), jnp.int32), pltpu.VMEM(courant.shape, F32), pltpu.SemaphoreType.DMA((3,))],
    )
    blocks = [exchange(env[f"q{r}"], orders[r], count, env["c"] if r == 0 else None) for r in range(rows)]
    env["outer"] = between_pairs(held(env[f"q{last}"], env["inner"]))
    run(blocks, range(rows), False, near, ["inner"], False, False)
    if last:
        run(blocks, range(last), False, [k for k in far if k[1] < last], [], True, False)
    run(blocks, range(last, rows), False, [k for k in far if k[1] == last], [], False, False)
    run(blocks, range(last, rows), False, [], ["outer"], True, False)

    env["inner"] = within_pair(env["q0"])
    blocks = [exchange(env[f"q{r}"], orders[r], count) for r in range(rows)]
    env["outer"] = between_pairs(held(env[f"q{last}"], env["inner"]))
    run(blocks, range(rows), True, near, ["inner"], False, True)
    run(blocks, range(rows), False, far, ["outer"], True, True)
    return env["out"].reshape(populations.shape)


def solution(mesh):
    placed = (
        P("mode", None, "cell", None),
        P(None, "cell", None),
        P("mode"),
        P(None, "mode"),
        P("mode", None),
    )
    return jax.shard_map(
        on_device,
        mesh=mesh,
        in_specs=placed,
        out_specs=P("mode", None, "cell", None),
        check_vma=False,
    )
```

time: 99 us -> 30.9 us (0.31); the launches traced: 97.6 us -> 30.6 us
  waiting for transfers between devices: 32.9 us -> 3.41 us
  other arithmetic: 22.9 us -> 0 us
  between operations: 13.5 us -> 0.14 us
  local copies, waits for them, and re-layouts: 11.4 us -> 0 us
  starting transfers between devices: 12.2 us -> 20.5 us
  Pallas kernels: 0 us -> 6.5 us
  matrix products: 4.74 us -> 0 us
    all_gather x2 -> x0, waiting for transfers between devices: 32.5 us -> none  [collide(): lax.all_gather(rounded, 'mode', axis=0, tiled=True)]
    convert_element_type x4 -> x0, other arithmetic: 13.2 us -> none  [the longest x2 9.65 us: advect(): field.astype(jnp.bfloat16)]
    mul x3 -> x0, other arithmetic: 9.65 us -> none  [on_device(): return keep * (0.5 * first + 0.5 * final)]
    ppermute x4 -> x16, starting transfers between devices: 12.1 us -> 20.5 us  [the longest x12 10.6 us: exchange(): blocks[offset ^ bit] = lax.ppermute(block, 'mode', pairs)]
    slice x7 -> x0, local copies, waits for them, and re-layouts: 6.85 us -> none  [the longest x4 6.11 us: advect(): back_x = jnp.roll(field, 1, axis=3)]
    pallas_call x0 -> x11, Pallas kernels: none -> 6.5 us  [call(): pl.pallas_call(kernel, out_shape=list(outs.values()), in_specs=[HBM if n...]
    dot_general x2 -> x0, matrix products: 4.74 us -> none  [collide(): jnp.dot(collision, lax.all_gather(rounded, 'mode', axis=0, tiled=True), p...]
    reshape x2 -> x0, local copies, waits for them, and re-layouts: 3.03 us -> none  [collide(): return result.reshape(field.shape)]
  transfers between devices with their start and end apart: 6 -> 16, of which waited for: 4 -> 3; matrix products, arithmetic and copies ran while one was open for 11% -> 0% of each run, Pallas kernels for 0% -> 14%
where the time goes in v5:
time: 30.9 us; the launch traced here: 30.6 us
  starting transfers between devices  20.5 us (66%)
  Pallas kernels  6.5 us (21%)
  waiting for transfers between devices  3.41 us (11%)
    ppermute x12, starting transfers between devices, exchange(): blocks[offset ^ bit] = lax.ppermute(block, 'mode', pairs)  10.6 us
    ppermute x2, starting transfers between devices, between_pairs(): lax.ppermute(row, 'cell', steps + [(target, source) for source, target in...  8.58 us
    pallas_call x11, Pallas kernels, call(): pl.pallas_call(kernel, out_shape=list(outs.values()), in_specs=[HBM if n...  6.5 us
    ppermute x12, waiting for transfers between devices, exchange(): blocks[offset ^ bit] = lax.ppermute(block, 'mode', pairs)  2.41 us
    ppermute x2, starting transfers between devices, within_pair(): lax.ppermute(row, 'cell', [(i, i ^ 1) for i in range(lax.axis_size('cell'...  1.31 us
    ppermute x2, waiting for transfers between devices, between_pairs(): lax.ppermute(row, 'cell', steps + [(target, source) for source, target in...  0.99 us
  transfers between devices with their start and end apart: 16, of which 3 were waited for; matrix products, arithmetic and copies ran while one was open for 0% of the time, Pallas kernels for 14%

profile of v5, /device:TPU:1, one launch (start us, length us, event | category | flops | bytes accessed | tf_op | source)
XLA Modules:
  0.0 30.6 jit_solution(16983063191745964798)
XLA Ops:
  0.0 1.1 %shard_map.55 = (f32[2,128]{1,0:T(2,128)S(1)}, f32[512,128]{1,0:T(8,128)S(1)}, bf16[512,128]{1,0:T(8,128)(2,1)S(1)}, f32[512,128]{1,0:T(8,128)S(1)}, bf16[512,128]{1,0:T(8,128)(2,1)S(1)}) custom-call(f32[1024,128]{1,0:T(8,128)} %bitcast.6, s32[2,128]{1,0:T(2,128)} %bitcast.8), custom_call_target="tpu_custom_call" | custom-call | bytes 1312768 | tf_op jit(solution)/shard_map/pallas_call | solution.py:31
  1.1 2.1 %collective-permute-start.1 = (bf16[512,128]{1,0:T(8,128)(2,1)S(1)}, bf16[512,128]{1,0:T(8,128)(2,1)S(1)}, u32[]{:S(2)}, u32[]{:S(2)}) collective-permute-start(bf16[512,128]{1,0:T(8,128)(2,1)S(1)} %get-tuple-element.26.refs_5_), channel_id=1, source_target_pairs={{0,8},{8,0},{16,24},{24,16},{1,9},{9,1},{17,25},{25,17},{2,10},{10... | collective-permute-start | bytes 393224 | tf_op jit(solution)/shard_map/ppermute | solution.py:157
  3.2 1.2 %collective-permute-start.4 = (bf16[512,128]{1,0:T(8,128)(2,1)S(1)}, bf16[512,128]{1,0:T(8,128)(2,1)S(1)}, u32[]{:S(2)}, u32[]{:S(2)}) collective-permute-start(bf16[512,128]{1,0:T(8,128)(2,1)S(1)} %get-tuple-element.29.refs_8_.refs_0_), channel_id=1, source_target_pairs={{0,16},{8,24},{16,0},{24,8},{1,17},{9,25},{17,1},{25,9},{2,18},{10... | collective-permute-start | bytes 393224 | tf_op jit(solution)/shard_map/ppermute | solution.py:157
  4.5 1.2 %collective-permute-start = (bf16[512,128]{1,0:T(8,128)(2,1)S(1)}, bf16[512,128]{1,0:T(8,128)(2,1)S(1)}, u32[]{:S(2)}, u32[]{:S(2)}) collective-permute-start(bf16[512,128]{1,0:T(8,128)(2,1)S(1)} %get-tuple-element.26.refs_5_), channel_id=1, source_target_pairs={{0,1},{1,0},{2,3},{3,2},{4,5},{5,4},{6,7},{7,6},{8,9},{9,8},{10,11... | collective-permute-start | bytes 393224 | tf_op jit(solution)/shard_map/ppermute | solution.py:162
  5.7 0.2 collective-permute-start.2
  6.0 0.0 collective-permute-start.3
  6.0 1.7 %shard_map.56 = (bf16[512,2048]{1,0:T(8,128)(2,1)S(1)}, f32[512,8]{1,0:T(8,128)S(1)}, f32[512,128]{1,0:T(8,128)S(1)}, f32[512,128]{1,0:T(8,128)S(1)}) custom-call(s32[1,512]{1,0:T(1,128)} %bitcast.7, f32[3,512]{1,0:T(4,128)} %refs_1_.1, bf16[512,2048]{1,0:T(8,128)(2,1)} %refs_2_.1, f32[512,128]{1,0:T(8,128)S(1)} %get-tuple-element.22.refs_3_.refs_8_, ...), custom_call_target="tpu_custom_call" | custom-call | bytes 5267456 | tf_op jit(solution)/shard_map/pallas_call | solution.py:31
  7.7 0.0 collective-permute-done.1.refs_6_.refs_0_
  7.8 1.5 %collective-permute-start.5 = (bf16[512,128]{1,0:T(8,128)(2,1)S(1)}, bf16[512,128]{1,0:T(8,128)(2,1)S(1)}, u32[]{:S(2)}, u32[]{:S(2)}) collective-permute-start(bf16[512,128]{1,0:T(8,128)(2,1)S(1)} %shard_map.58), channel_id=1, source_target_pairs={{0,16},{8,24},{16,0},{24,8},{1,17},{9,25},{17,1},{25,9},{2,18},{10... | collective-permute-start | bytes 393224 | tf_op jit(solution)/shard_map/ppermute | solution.py:157
  9.3 0.0 collective-permute-done.4.refs_10_
  9.3 1.2 %collective-permute-start.6 = (bf16[512,128]{1,0:T(8,128)(2,1)S(1)}, bf16[512,128]{1,0:T(8,128)(2,1)S(1)}, u32[]{:S(2)}, u32[]{:S(2)}) collective-permute-start(bf16[512,128]{1,0:T(8,128)(2,1)S(1)} %collective-permute-done.4.refs_10_), channel_id=1, source_target_pairs={{0,8},{8,0},{16,24},{24,16},{1,9},{9,1},{17,25},{25,17},{2,10},{10... | collective-permute-start | bytes 393224 | tf_op jit(solution)/shard_map/ppermute | solution.py:157
  10.5 0.0 collective-permute-done.refs_2_.refs_1_
  10.5 4.2 %collective-permute-start.7 = (bf16[512,128]{1,0:T(8,128)(2,1)S(1)}, bf16[512,128]{1,0:T(8,128)(2,1)S(1)}, u32[]{:S(2)}, u32[]{:S(2)}) collective-permute-start(bf16[512,128]{1,0:T(8,128)(2,1)S(1)} %shard_map.61), channel_id=1, source_target_pairs={{1,2},{3,4},{5,6},{2,1},{4,3},{6,5},{9,10},{11,12},{13,14},{10,9},... | collective-permute-start | bytes 393224 | tf_op jit(solution)/shard_map/ppermute | solution.py:167
  14.7 0.0 collective-permute-done.2.refs_7_
  14.8 0.0 collective-permute-done.3.refs_9_
  14.8 0.6 %shard_map.57 = (f32[512,128]{1,0:T(8,128)S(1)}, f32[512,128]{1,0:T(8,128)S(1)}) custom-call(f32[512,128]{1,0:T(8,128)S(1)} %get-tuple-element.24.refs_0_, f32[512,128]{1,0:T(8,128)S(1)} %get-tuple-element.25.refs_1_, bf16[512,128]{1,0:T(8,128)(2,1)S(1)} %collective-permute-done.refs_2_.refs_1_, f32[512,8]{1,0:T(8,128)S(1)} %get-tuple-element.27.refs_3_.refs_2_, ...), custom_call_target="tpu_custom_call" | custom-call | flops 402653184 | bytes 4079616 | tf_op jit(solution)/shard_map/pallas_call | solution.py:31
  15.4 0.0 collective-permute-done.5.refs_3_
  15.4 0.3 shard_map.59
  15.7 0.1 collective-permute-start.8
  15.8 0.3 %collective-permute-start.9 = (bf16[512,128]{1,0:T(8,128)(2,1)S(1)}, bf16[512,128]{1,0:T(8,128)(2,1)S(1)}, u32[]{:S(2)}, u32[]{:S(2)}) collective-permute-start(bf16[512,128]{1,0:T(8,128)(2,1)S(1)} %get-tuple-element.35.refs_5_), channel_id=1, source_target_pairs={{0,8},{8,0},{16,24},{24,16},{1,9},{9,1},{17,25},{25,17},{2,10},{10... | collective-permute-start | bytes 393224 | tf_op jit(solution)/shard_map/ppermute | solution.py:157
  16.1 0.0 collective-permute-done.6.refs_2_
  16.1 0.3 shard_map.60.refs_0_
  16.4 1.0 %collective-permute-done.7.refs_1_ = bf16[512,128]{1,0:T(8,128)(2,1)S(1)} collective-permute-done((bf16[512,128]{1,0:T(8,128)(2,1)S(1)}, bf16[512,128]{1,0:T(8,128)(2,1)S(1)}, u32[]{:S(2)}, u32[]{:S(2)}) %collective-permute-start.7) | collective-permute-done | bytes 131104 | tf_op jit(solution)/shard_map/ppermute | solution.py:167
  17.4 0.2 shard_map.62
  17.6 0.7 %collective-permute-start.12 = (bf16[512,128]{1,0:T(8,128)(2,1)S(1)}, bf16[512,128]{1,0:T(8,128)(2,1)S(1)}, u32[]{:S(2)}, u32[]{:S(2)}) collective-permute-start(bf16[512,128]{1,0:T(8,128)(2,1)S(1)} %get-tuple-element.36.refs_8_.refs_0_), channel_id=1, source_target_pairs={{0,16},{8,24},{16,0},{24,8},{1,17},{9,25},{17,1},{25,9},{2,18},{10... | collective-permute-start | bytes 393224 | tf_op jit(solution)/shard_map/ppermute | solution.py:157
  18.3 0.8 %collective-permute-start.10 = (bf16[512,128]{1,0:T(8,128)(2,1)S(1)}, bf16[512,128]{1,0:T(8,128)(2,1)S(1)}, u32[]{:S(2)}, u32[]{:S(2)}) collective-permute-start(bf16[512,128]{1,0:T(8,128)(2,1)S(1)} %get-tuple-element.35.refs_5_), channel_id=1, source_target_pairs={{0,16},{8,24},{16,0},{24,8},{1,17},{9,25},{17,1},{25,9},{2,18},{10... | collective-permute-start | bytes 393224 | tf_op jit(solution)/shard_map/ppermute | solution.py:157
  19.1 0.5 %collective-permute-start.11 = (bf16[512,128]{1,0:T(8,128)(2,1)S(1)}, bf16[512,128]{1,0:T(8,128)(2,1)S(1)}, u32[]{:S(2)}, u32[]{:S(2)}) collective-permute-start(bf16[512,128]{1,0:T(8,128)(2,1)S(1)} %get-tuple-element.36.refs_8_.refs_0_), channel_id=1, source_target_pairs={{0,8},{8,0},{16,24},{24,16},{1,9},{9,1},{17,25},{25,17},{2,10},{10... | collective-permute-start | bytes 393224 | tf_op jit(solution)/shard_map/ppermute | solution.py:157
  19.6 0.0 collective-permute-done.8.refs_2_.refs_1_
  19.6 4.4 %collective-permute-start.13 = (bf16[512,128]{1,0:T(8,128)(2,1)S(1)}, bf16[512,128]{1,0:T(8,128)(2,1)S(1)}, u32[]{:S(2)}, u32[]{:S(2)}) collective-permute-start(bf16[512,128]{1,0:T(8,128)(2,1)S(1)} %shard_map.64), channel_id=1, source_target_pairs={{1,2},{3,4},{5,6},{2,1},{4,3},{6,5},{9,10},{11,12},{13,14},{10,9},... | collective-permute-start | bytes 393224 | tf_op jit(solution)/shard_map/ppermute | solution.py:167
  24.0 0.0 collective-permute-done.9.refs_6_
  24.0 1.6 %collective-permute-start.14 = (bf16[512,128]{1,0:T(8,128)(2,1)S(1)}, bf16[512,128]{1,0:T(8,128)(2,1)S(1)}, u32[]{:S(2)}, u32[]{:S(2)}) collective-permute-start(bf16[512,128]{1,0:T(8,128)(2,1)S(1)} %collective-permute-done.9.refs_6_), channel_id=1, source_target_pairs={{0,16},{8,24},{16,0},{24,8},{1,17},{9,25},{17,1},{25,9},{2,18},{10... | collective-permute-start | bytes 393224 | tf_op jit(solution)/shard_map/ppermute | solution.py:157
  25.6 0.0 collective-permute-done.12.refs_10_
  25.6 0.4 %collective-permute-start.15 = (bf16[512,128]{1,0:T(8,128)(2,1)S(1)}, bf16[512,128]{1,0:T(8,128)(2,1)S(1)}, u32[]{:S(2)}, u32[]{:S(2)}) collective-permute-start(bf16[512,128]{1,0:T(8,128)(2,1)S(1)} %collective-permute-done.12.refs_10_), channel_id=1, source_target_pairs={{0,8},{8,0},{16,24},{24,16},{1,9},{9,1},{17,25},{25,17},{2,10},{10... | collective-permute-start | bytes 393224 | tf_op jit(solution)/shard_map/ppermute | solution.py:157
  26.0 0.0 collective-permute-done.10.refs_7_
  26.0 0.0 collective-permute-done.11.refs_9_
  26.0 1.1 %shard_map.63 = (f32[512,128]{1,0:T(8,128)S(1)}, f32[512,128]{1,0:T(8,128)S(1)}) custom-call(f32[512,128]{1,0:T(8,128)S(1)} %get-tuple-element.32.refs_0_, f32[512,128]{1,0:T(8,128)S(1)} %get-tuple-element.34.refs_1_, bf16[512,128]{1,0:T(8,128)(2,1)S(1)} %collective-permute-done.8.refs_2_.refs_1_, f32[512,8]{1,0:T(8,128)S(1)} %get-tuple-element.27.refs_3_.refs_2_, ...), custom_call_target="tpu_custom_call" | custom-call | flops 402653184 | bytes 4079616 | tf_op jit(solution)/shard_map/pallas_call | solution.py:31
  27.0 0.0 collective-permute-done.13.refs_2_
  27.1 1.4 %collective-permute-done.14.refs_6_ = bf16[512,128]{1,0:T(8,128)(2,1)S(1)} collective-permute-done((bf16[512,128]{1,0:T(8,128)(2,1)S(1)}, bf16[512,128]{1,0:T(8,128)(2,1)S(1)}, u32[]{:S(2)}, u32[]{:S(2)}) %collective-permute-start.14) | collective-permute-done | bytes 131104 | tf_op jit(solution)/shard_map/ppermute | solution.py:157
  28.5 0.9 %collective-permute-done.15.refs_7_ = bf16[512,128]{1,0:T(8,128)(2,1)S(1)} collective-permute-done((bf16[512,128]{1,0:T(8,128)(2,1)S(1)}, bf16[512,128]{1,0:T(8,128)(2,1)S(1)}, u32[]{:S(2)}, u32[]{:S(2)}) %collective-permute-start.15) | collective-permute-done | bytes 131104 | tf_op jit(solution)/shard_map/ppermute | solution.py:157
  29.4 1.1 %shard_map.65 = f32[1024,128]{1,0:T(8,128)} custom-call(f32[512,128]{1,0:T(8,128)S(1)} %get-tuple-element.37.refs_0_, f32[512,128]{1,0:T(8,128)S(1)} %get-tuple-element.38.refs_1_, bf16[512,128]{1,0:T(8,128)(2,1)S(1)} %collective-permute-done.13.refs_2_, f32[512,8]{1,0:T(8,128)S(1)} %get-tuple-element.27.refs_3_.refs_2_, ...), custom_call_target="tpu_custom_call" | custom-call | flops 134217728 | bytes 4080640 | tf_op jit(solution)/shard_map/pallas_call | solution.py:31
  (3 shorter events, 0.0 us)
Async XLA Ops:
  1.1 6.6 %collective-permute-start.1 = (bf16[512,128]{1,0:T(8,128)(2,1)S(1)}, bf16[512,128]{1,0:T(8,128)(2,1)S(1)}, u32[]{:S(2)}, u32[]{:S(2)}) collective-permute-start(bf16[512,128]{1,0:T(8,128)(2,1)S(1)} %get-tuple-element.26.refs_5_), channel_id=1, source_target_pairs={{0,8},{8,0},{16,24},{24,16},{1,9},{9,1},{17,25},{25,17},{2,10},{10... | collective-permute-start | bytes 393224 | tf_op jit(solution)/shard_map/ppermute | solution.py:157
  3.2 6.0 %collective-permute-start.4 = (bf16[512,128]{1,0:T(8,128)(2,1)S(1)}, bf16[512,128]{1,0:T(8,128)(2,1)S(1)}, u32[]{:S(2)}, u32[]{:S(2)}) collective-permute-start(bf16[512,128]{1,0:T(8,128)(2,1)S(1)} %get-tuple-element.29.refs_8_.refs_0_), channel_id=1, source_target_pairs={{0,16},{8,24},{16,0},{24,8},{1,17},{9,25},{17,1},{25,9},{2,18},{10... | collective-permute-start | bytes 393224 | tf_op jit(solution)/shard_map/ppermute | solution.py:157
  4.5 6.0 %collective-permute-start = (bf16[512,128]{1,0:T(8,128)(2,1)S(1)}, bf16[512,128]{1,0:T(8,128)(2,1)S(1)}, u32[]{:S(2)}, u32[]{:S(2)}) collective-permute-start(bf16[512,128]{1,0:T(8,128)(2,1)S(1)} %get-tuple-element.26.refs_5_), channel_id=1, source_target_pairs={{0,1},{1,0},{2,3},{3,2},{4,5},{5,4},{6,7},{7,6},{8,9},{9,8},{10,11... | collective-permute-start | bytes 393224 | tf_op jit(solution)/shard_map/ppermute | solution.py:162
  5.7 9.0 %collective-permute-start.2 = (bf16[512,128]{1,0:T(8,128)(2,1)S(1)}, bf16[512,128]{1,0:T(8,128)(2,1)S(1)}, u32[]{:S(2)}, u32[]{:S(2)}) collective-permute-start(bf16[512,128]{1,0:T(8,128)(2,1)S(1)} %get-tuple-element.26.refs_5_), channel_id=1, source_target_pairs={{0,16},{8,24},{16,0},{24,8},{1,17},{9,25},{17,1},{25,9},{2,18},{10... | collective-permute-start | bytes 393224 | tf_op jit(solution)/shard_map/ppermute | solution.py:157
  6.0 8.8 %collective-permute-start.3 = (bf16[512,128]{1,0:T(8,128)(2,1)S(1)}, bf16[512,128]{1,0:T(8,128)(2,1)S(1)}, u32[]{:S(2)}, u32[]{:S(2)}) collective-permute-start(bf16[512,128]{1,0:T(8,128)(2,1)S(1)} %get-tuple-element.29.refs_8_.refs_0_), channel_id=1, source_target_pairs={{0,8},{8,0},{16,24},{24,16},{1,9},{9,1},{17,25},{25,17},{2,10},{10... | collective-permute-start | bytes 393224 | tf_op jit(solution)/shard_map/ppermute | solution.py:157
  7.8 7.6 %collective-permute-start.5 = (bf16[512,128]{1,0:T(8,128)(2,1)S(1)}, bf16[512,128]{1,0:T(8,128)(2,1)S(1)}, u32[]{:S(2)}, u32[]{:S(2)}) collective-permute-start(bf16[512,128]{1,0:T(8,128)(2,1)S(1)} %shard_map.58), channel_id=1, source_target_pairs={{0,16},{8,24},{16,0},{24,8},{1,17},{9,25},{17,1},{25,9},{2,18},{10... | collective-permute-start | bytes 393224 | tf_op jit(solution)/shard_map/ppermute | solution.py:157
  9.3 6.8 %collective-permute-start.6 = (bf16[512,128]{1,0:T(8,128)(2,1)S(1)}, bf16[512,128]{1,0:T(8,128)(2,1)S(1)}, u32[]{:S(2)}, u32[]{:S(2)}) collective-permute-start(bf16[512,128]{1,0:T(8,128)(2,1)S(1)} %collective-permute-done.4.refs_10_), channel_id=1, source_target_pairs={{0,8},{8,0},{16,24},{24,16},{1,9},{9,1},{17,25},{25,17},{2,10},{10... | collective-permute-start | bytes 393224 | tf_op jit(solution)/shard_map/ppermute | solution.py:157
  10.5 6.9 %collective-permute-start.7 = (bf16[512,128]{1,0:T(8,128)(2,1)S(1)}, bf16[512,128]{1,0:T(8,128)(2,1)S(1)}, u32[]{:S(2)}, u32[]{:S(2)}) collective-permute-start(bf16[512,128]{1,0:T(8,128)(2,1)S(1)} %shard_map.61), channel_id=1, source_target_pairs={{1,2},{3,4},{5,6},{2,1},{4,3},{6,5},{9,10},{11,12},{13,14},{10,9},... | collective-permute-start | bytes 393224 | tf_op jit(solution)/shard_map/ppermute | solution.py:167
  15.7 3.9 %collective-permute-start.8 = (bf16[512,128]{1,0:T(8,128)(2,1)S(1)}, bf16[512,128]{1,0:T(8,128)(2,1)S(1)}, u32[]{:S(2)}, u32[]{:S(2)}) collective-permute-start(bf16[512,128]{1,0:T(8,128)(2,1)S(1)} %get-tuple-element.35.refs_5_), channel_id=1, source_target_pairs={{0,1},{1,0},{2,3},{3,2},{4,5},{5,4},{6,7},{7,6},{8,9},{9,8},{10,11... | collective-permute-start | bytes 393224 | tf_op jit(solution)/shard_map/ppermute | solution.py:162
  15.8 8.3 %collective-permute-start.9 = (bf16[512,128]{1,0:T(8,128)(2,1)S(1)}, bf16[512,128]{1,0:T(8,128)(2,1)S(1)}, u32[]{:S(2)}, u32[]{:S(2)}) collective-permute-start(bf16[512,128]{1,0:T(8,128)(2,1)S(1)} %get-tuple-element.35.refs_5_), channel_id=1, source_target_pairs={{0,8},{8,0},{16,24},{24,16},{1,9},{9,1},{17,25},{25,17},{2,10},{10... | collective-permute-start | bytes 393224 | tf_op jit(solution)/shard_map/ppermute | solution.py:157
  17.6 8.0 %collective-permute-start.12 = (bf16[512,128]{1,0:T(8,128)(2,1)S(1)}, bf16[512,128]{1,0:T(8,128)(2,1)S(1)}, u32[]{:S(2)}, u32[]{:S(2)}) collective-permute-start(bf16[512,128]{1,0:T(8,128)(2,1)S(1)} %get-tuple-element.36.refs_8_.refs_0_), channel_id=1, source_target_pairs={{0,16},{8,24},{16,0},{24,8},{1,17},{9,25},{17,1},{25,9},{2,18},{10... | collective-permute-start | bytes 393224 | tf_op jit(solution)/shard_map/ppermute | solution.py:157
  18.3 7.7 %collective-permute-start.10 = (bf16[512,128]{1,0:T(8,128)(2,1)S(1)}, bf16[512,128]{1,0:T(8,128)(2,1)S(1)}, u32[]{:S(2)}, u32[]{:S(2)}) collective-permute-start(bf16[512,128]{1,0:T(8,128)(2,1)S(1)} %get-tuple-element.35.refs_5_), channel_id=1, source_target_pairs={{0,16},{8,24},{16,0},{24,8},{1,17},{9,25},{17,1},{25,9},{2,18},{10... | collective-permute-start | bytes 393224 | tf_op jit(solution)/shard_map/ppermute | solution.py:157
  19.1 6.9 %collective-permute-start.11 = (bf16[512,128]{1,0:T(8,128)(2,1)S(1)}, bf16[512,128]{1,0:T(8,128)(2,1)S(1)}, u32[]{:S(2)}, u32[]{:S(2)}) collective-permute-start(bf16[512,128]{1,0:T(8,128)(2,1)S(1)} %get-tuple-element.36.refs_8_.refs_0_), channel_id=1, source_target_pairs={{0,8},{8,0},{16,24},{24,16},{1,9},{9,1},{17,25},{25,17},{2,10},{10... | collective-permute-start | bytes 393224 | tf_op jit(solution)/shard_map/ppermute | solution.py:157
  19.6 7.4 %collective-permute-start.13 = (bf16[512,128]{1,0:T(8,128)(2,1)S(1)}, bf16[512,128]{1,0:T(8,128)(2,1)S(1)}, u32[]{:S(2)}, u32[]{:S(2)}) collective-permute-start(bf16[512,128]{1,0:T(8,128)(2,1)S(1)} %shard_map.64), channel_id=1, source_target_pairs={{1,2},{3,4},{5,6},{2,1},{4,3},{6,5},{9,10},{11,12},{13,14},{10,9},... | collective-permute-start | bytes 393224 | tf_op jit(solution)/shard_map/ppermute | solution.py:167
  24.0 4.5 %collective-permute-start.14 = (bf16[512,128]{1,0:T(8,128)(2,1)S(1)}, bf16[512,128]{1,0:T(8,128)(2,1)S(1)}, u32[]{:S(2)}, u32[]{:S(2)}) collective-permute-start(bf16[512,128]{1,0:T(8,128)(2,1)S(1)} %collective-permute-done.9.refs_6_), channel_id=1, source_target_pairs={{0,16},{8,24},{16,0},{24,8},{1,17},{9,25},{17,1},{25,9},{2,18},{10... | collective-permute-start | bytes 393224 | tf_op jit(solution)/shard_map/ppermute | solution.py:157
  25.6 3.8 %collective-permute-start.15 = (bf16[512,128]{1,0:T(8,128)(2,1)S(1)}, bf16[512,128]{1,0:T(8,128)(2,1)S(1)}, u32[]{:S(2)}, u32[]{:S(2)}) collective-permute-start(bf16[512,128]{1,0:T(8,128)(2,1)S(1)} %collective-permute-done.12.refs_10_), channel_id=1, source_target_pairs={{0,8},{8,0},{16,24},{24,16},{1,9},{9,1},{17,25},{25,17},{2,10},{10... | collective-permute-start | bytes 393224 | tf_op jit(solution)/shard_map/ppermute | solution.py:157

commit v6 on v5

--- a/solution.py
+++ b/solution.py
@@ -87,9 +87,15 @@
     return (1.0 - (ax + ay + az)) * p + ax * beside + ay * jnp.where(backward_y(coef), later, prior)
 
 
+def mirrored(offset, count):
+    bits = count.bit_length() - 1
+    return sum((offset >> b & 1) << (bits - 1 - b) for b in range(bits))
+
+
 def product(c, offset, blocks):
     modes = blocks[0].shape[0]
-    position = lax.axis_index("mode") ^ offset
+    other = mirrored(offset, c.shape[1] // modes)
+    position = lax.axis_index("mode") ^ (is_first() * offset + (1 - is_first()) * other)
     cols = pl.ds(pl.multiple_of(position * modes, modes), modes)
     return jnp.dot(c[:, cols], jnp.concatenate(blocks, axis=1), preferred_element_type=F32)
 
@@ -148,13 +154,15 @@
 
 
 def exchange(row, bits, count, other=None):
+    cells = lax.axis_size("cell")
     blocks = {0: row}
     for i, bit in enumerate(bits):
-        pairs = [(j, j ^ bit) for j in range(count)]
+        both = bit, mirrored(bit, count)
+        pairs = [(m * cells + c, (m ^ both[c % 2]) * cells + c) for m in range(count) for c in range(cells)]
         for offset, block in list(blocks.items()):
             if i and offset and other is not None:
                 block = held(block, other)
-            blocks[offset ^ bit] = lax.ppermute(block, "mode", pairs)
+            blocks[offset ^ bit] = lax.ppermute(block, ("mode", "cell"), pairs)
     return blocks
 
 
@@ -174,6 +182,7 @@
     last = rows - 1
     bits = [1 << b for b in range(count.bit_length() - 1)]
     orders = [bits if r % 2 == 0 else bits[::-1] for r in range(rows)]
+    turned = [order[::-1] for order in orders]
     row_f32, row_bf16 = shape((modes, width), F32), shape((modes, width), BF16)
     keys = [(o, r) for r in range(rows) for o in range(count)]
     near = [(o, r) for o, r in keys if o == 0 or o in bits]
@@ -215,13 +224,12 @@
         hbm=("octant", "courant", "collision"),
         scratch=[pltpu.VMEM((1, modes), jnp.int32), pltpu.VMEM(courant.shape, F32), pltpu.SemaphoreType.DMA((3,))],
     )
-    blocks = [exchange(env[f"q{r}"], orders[r], count, env["c"] if r == 0 else None) for r in range(rows)]
+    blocks = [exchange(env[f"q{r}"], turned[r], count, env["c"] if r == 0 else None) for r in range(rows)]
     env["outer"] = between_pairs(held(env[f"q{last}"], env["inner"]))
     run(blocks, range(rows), False, near, ["inner"], False, False)
     if last:
         run(blocks, range(last), False, [k for k in far if k[1] < last], [], True, False)
-    run(blocks, range(last, rows), False, [k for k in far if k[1] == last], [], False, False)
-    run(blocks, range(last, rows), False, [], ["outer"], True, False)
+    run(blocks, range(last, rows), False, [k for k in far if k[1] == last], ["outer"], True, False)
 
     env["inner"] = within_pair(env["q0"])
     blocks = [exchange(env[f"q{r}"], orders[r], count) for r in range(rows)]

time: 30.9 us -> 29.9 us (0.968)
  waiting for transfers between devices: 3.41 us -> 2.09 us
  starting transfers between devices: 20.5 us -> 21.2 us
    ppermute x12, starting transfers between devices: 10.6 us -> 12.9 us  [exchange(): blocks[offset ^ bit] = lax.ppermute(block, ('mode', 'cell'), pairs)]
    ppermute x2, starting transfers between devices: 8.58 us -> 7.18 us  [between_pairs(): lax.ppermute(row, 'cell', steps + [(target, source) for source, target in...]
    ppermute x2, waiting for transfers between devices: 0.99 us -> 0.01 us  [between_pairs(): lax.ppermute(row, 'cell', steps + [(target, source) for source, target in...]
    ppermute x12, waiting for transfers between devices: 2.41 us -> 2.08 us  [exchange(): blocks[offset ^ bit] = lax.ppermute(block, ('mode', 'cell'), pairs)]
    pallas_call x11 -> x10, Pallas kernels: 6.5 us -> 6.33 us  [call(): pl.pallas_call(kernel, out_shape=list(outs.values()), in_specs=[HBM if n...]
where the time goes in v6:
time: 29.9 us; the launch traced here: 29.7 us
  starting transfers between devices  21.2 us (71%)
  Pallas kernels  6.33 us (21%)
  waiting for transfers between devices  2.09 us (7%)
    ppermute x12, starting transfers between devices, exchange(): blocks[offset ^ bit] = lax.ppermute(block, ('mode', 'cell'), pairs)  12.9 us
    ppermute x2, starting transfers between devices, between_pairs(): lax.ppermute(row, 'cell', steps + [(target, source) for source, target in...  7.18 us
    pallas_call x10, Pallas kernels, call(): pl.pallas_call(kernel, out_shape=list(outs.values()), in_specs=[HBM if n...  6.33 us
    ppermute x12, waiting for transfers between devices, exchange(): blocks[offset ^ bit] = lax.ppermute(block, ('mode', 'cell'), pairs)  2.08 us
    ppermute x2, starting transfers between devices, within_pair(): lax.ppermute(row, 'cell', [(i, i ^ 1) for i in range(lax.axis_size('cell'...  1.05 us
  transfers between devices with their start and end apart: 16, of which 3 were waited for; matrix products, arithmetic and copies ran while one was open for 0% of the time, Pallas kernels for 14%

profile of v6, /device:TPU:1, one launch (start us, length us, event | category | flops | bytes accessed | tf_op | source)
XLA Modules:
  0.0 29.7 jit_solution(12058041025345559137)
XLA Ops:
  0.0 1.1 %shard_map.55 = (f32[2,128]{1,0:T(2,128)S(1)}, f32[512,128]{1,0:T(8,128)S(1)}, bf16[512,128]{1,0:T(8,128)(2,1)S(1)}, f32[512,128]{1,0:T(8,128)S(1)}, bf16[512,128]{1,0:T(8,128)(2,1)S(1)}) custom-call(f32[1024,128]{1,0:T(8,128)} %bitcast.6, s32[2,128]{1,0:T(2,128)} %bitcast.8), custom_call_target="tpu_custom_call" | custom-call | bytes 1312768 | tf_op jit(solution)/shard_map/pallas_call | solution.py:31
  1.1 2.1 %collective-permute-start.2 = (bf16[512,128]{1,0:T(8,128)(2,1)S(1)}, bf16[512,128]{1,0:T(8,128)(2,1)S(1)}, u32[]{:S(2)}, u32[]{:S(2)}) collective-permute-start(bf16[512,128]{1,0:T(8,128)(2,1)S(1)} %get-tuple-element.26.refs_5_), channel_id=1, source_target_pairs={{0,16},{1,9},{2,18},{3,11},{4,20},{5,13},{6,22},{7,15},{8,24},{9,1... | collective-permute-start | bytes 393224 | tf_op jit(solution)/shard_map/ppermute | solution.py:165
  3.2 1.0 %collective-permute-start = (bf16[512,128]{1,0:T(8,128)(2,1)S(1)}, bf16[512,128]{1,0:T(8,128)(2,1)S(1)}, u32[]{:S(2)}, u32[]{:S(2)}) collective-permute-start(bf16[512,128]{1,0:T(8,128)(2,1)S(1)} %get-tuple-element.26.refs_5_), channel_id=1, source_target_pairs={{0,1},{1,0},{2,3},{3,2},{4,5},{5,4},{6,7},{7,6},{8,9},{9,8},{10,11... | collective-permute-start | bytes 393224 | tf_op jit(solution)/shard_map/ppermute | solution.py:170
  4.2 0.3 collective-permute-start.3
  4.5 1.2 %collective-permute-start.1 = (bf16[512,128]{1,0:T(8,128)(2,1)S(1)}, bf16[512,128]{1,0:T(8,128)(2,1)S(1)}, u32[]{:S(2)}, u32[]{:S(2)}) collective-permute-start(bf16[512,128]{1,0:T(8,128)(2,1)S(1)} %get-tuple-element.26.refs_5_), channel_id=1, source_target_pairs={{0,8},{1,17},{2,10},{3,19},{4,12},{5,21},{6,14},{7,23},{8,0},{9,25... | collective-permute-start | bytes 393224 | tf_op jit(solution)/shard_map/ppermute | solution.py:165
  5.7 1.2 %collective-permute-start.4 = (bf16[512,128]{1,0:T(8,128)(2,1)S(1)}, bf16[512,128]{1,0:T(8,128)(2,1)S(1)}, u32[]{:S(2)}, u32[]{:S(2)}) collective-permute-start(bf16[512,128]{1,0:T(8,128)(2,1)S(1)} %get-tuple-element.29.refs_8_.refs_0_), channel_id=1, source_target_pairs={{0,16},{1,9},{2,18},{3,11},{4,20},{5,13},{6,22},{7,15},{8,24},{9,1... | collective-permute-start | bytes 393224 | tf_op jit(solution)/shard_map/ppermute | solution.py:165
  6.9 1.7 %shard_map.56 = (bf16[512,2048]{1,0:T(8,128)(2,1)S(1)}, f32[512,8]{1,0:T(8,128)S(1)}, f32[512,128]{1,0:T(8,128)S(1)}, f32[512,128]{1,0:T(8,128)S(1)}) custom-call(s32[1,512]{1,0:T(1,128)} %bitcast.7, f32[3,512]{1,0:T(4,128)} %refs_1_.1, bf16[512,2048]{1,0:T(8,128)(2,1)} %refs_2_.1, f32[512,128]{1,0:T(8,128)S(1)} %get-tuple-element.22.refs_3_.refs_8_, ...), custom_call_target="tpu_custom_call" | custom-call | bytes 5267456 | tf_op jit(solution)/shard_map/pallas_call | solution.py:31
  8.7 0.0 collective-permute-done.2.refs_7_.refs_0_
  8.7 0.3 collective-permute-start.5
  9.0 0.0 collective-permute-done.refs_2_.refs_1_
  9.0 4.2 %collective-permute-start.6 = (bf16[512,128]{1,0:T(8,128)(2,1)S(1)}, bf16[512,128]{1,0:T(8,128)(2,1)S(1)}, u32[]{:S(2)}, u32[]{:S(2)}) collective-permute-start(bf16[512,128]{1,0:T(8,128)(2,1)S(1)} %shard_map.60), channel_id=1, source_target_pairs={{1,2},{3,4},{5,6},{2,1},{4,3},{6,5},{9,10},{11,12},{13,14},{10,9},... | collective-permute-start | bytes 393224 | tf_op jit(solution)/shard_map/ppermute | solution.py:175
  13.2 0.0 collective-permute-done.3.refs_9_
  13.2 0.9 %collective-permute-start.7 = (bf16[512,128]{1,0:T(8,128)(2,1)S(1)}, bf16[512,128]{1,0:T(8,128)(2,1)S(1)}, u32[]{:S(2)}, u32[]{:S(2)}) collective-permute-start(bf16[512,128]{1,0:T(8,128)(2,1)S(1)} %collective-permute-done.3.refs_9_), channel_id=1, source_target_pairs={{0,16},{1,9},{2,18},{3,11},{4,20},{5,13},{6,22},{7,15},{8,24},{9,1... | collective-permute-start | bytes 393224 | tf_op jit(solution)/shard_map/ppermute | solution.py:165
  14.1 0.0 collective-permute-done.1.refs_6_
  14.1 0.0 collective-permute-done.4.refs_10_
  14.1 0.6 %shard_map.57 = (f32[512,128]{1,0:T(8,128)S(1)}, f32[512,128]{1,0:T(8,128)S(1)}) custom-call(f32[512,128]{1,0:T(8,128)S(1)} %get-tuple-element.24.refs_0_, f32[512,128]{1,0:T(8,128)S(1)} %get-tuple-element.25.refs_1_, bf16[512,128]{1,0:T(8,128)(2,1)S(1)} %collective-permute-done.refs_2_.refs_1_, f32[512,8]{1,0:T(8,128)S(1)} %get-tuple-element.27.refs_3_.refs_2_, ...), custom_call_target="tpu_custom_call" | custom-call | flops 402653184 | bytes 4079616 | tf_op jit(solution)/shard_map/pallas_call | solution.py:31
  14.7 0.0 collective-permute-done.5.refs_3_
  14.7 0.3 shard_map.59
  15.0 0.1 collective-permute-start.8
  15.1 1.3 %collective-permute-start.9 = (bf16[512,128]{1,0:T(8,128)(2,1)S(1)}, bf16[512,128]{1,0:T(8,128)(2,1)S(1)}, u32[]{:S(2)}, u32[]{:S(2)}) collective-permute-start(bf16[512,128]{1,0:T(8,128)(2,1)S(1)} %get-tuple-element.35.refs_5_), channel_id=1, source_target_pairs={{0,8},{1,17},{2,10},{3,19},{4,12},{5,21},{6,14},{7,23},{8,0},{9,25... | collective-permute-start | bytes 393224 | tf_op jit(solution)/shard_map/ppermute | solution.py:165
  16.3 0.0 collective-permute-done.6.refs_1_
  16.3 0.8 %collective-permute-done.7.refs_5_ = bf16[512,128]{1,0:T(8,128)(2,1)S(1)} collective-permute-done((bf16[512,128]{1,0:T(8,128)(2,1)S(1)}, bf16[512,128]{1,0:T(8,128)(2,1)S(1)}, u32[]{:S(2)}, u32[]{:S(2)}) %collective-permute-start.7) | collective-permute-done | bytes 131104 | tf_op jit(solution)/shard_map/ppermute | solution.py:165
  17.1 0.3 %shard_map.61 = (f32[512,128]{1,0:T(8,128)S(1)}, bf16[512,128]{1,0:T(8,128)(2,1)S(1)}) custom-call(f32[512,128]{1,0:T(8,128)S(1)} %get-tuple-element.33.refs_0_, bf16[512,128]{1,0:T(8,128)(2,1)S(1)} %collective-permute-done.6.refs_1_, f32[512,8]{1,0:T(8,128)S(1)} %get-tuple-element.27.refs_3_.refs_2_, ...), custom_call_target="tpu_custom_call" | custom-call | flops 67108864 | bytes 3032064 | tf_op jit(solution)/shard_map/pallas_call | solution.py:31
  17.4 0.9 %collective-permute-start.12 = (bf16[512,128]{1,0:T(8,128)(2,1)S(1)}, bf16[512,128]{1,0:T(8,128)(2,1)S(1)}, u32[]{:S(2)}, u32[]{:S(2)}) collective-permute-start(bf16[512,128]{1,0:T(8,128)(2,1)S(1)} %get-tuple-element.36.refs_8_.refs_0_), channel_id=1, source_target_pairs={{0,16},{1,9},{2,18},{3,11},{4,20},{5,13},{6,22},{7,15},{8,24},{9,1... | collective-permute-start | bytes 393224 | tf_op jit(solution)/shard_map/ppermute | solution.py:165
  18.3 0.7 %collective-permute-start.10 = (bf16[512,128]{1,0:T(8,128)(2,1)S(1)}, bf16[512,128]{1,0:T(8,128)(2,1)S(1)}, u32[]{:S(2)}, u32[]{:S(2)}) collective-permute-start(bf16[512,128]{1,0:T(8,128)(2,1)S(1)} %get-tuple-element.35.refs_5_), channel_id=1, source_target_pairs={{0,16},{1,9},{2,18},{3,11},{4,20},{5,13},{6,22},{7,15},{8,24},{9,1... | collective-permute-start | bytes 393224 | tf_op jit(solution)/shard_map/ppermute | solution.py:165
  19.0 1.7 %collective-permute-start.11 = (bf16[512,128]{1,0:T(8,128)(2,1)S(1)}, bf16[512,128]{1,0:T(8,128)(2,1)S(1)}, u32[]{:S(2)}, u32[]{:S(2)}) collective-permute-start(bf16[512,128]{1,0:T(8,128)(2,1)S(1)} %get-tuple-element.36.refs_8_.refs_0_), channel_id=1, source_target_pairs={{0,8},{1,17},{2,10},{3,19},{4,12},{5,21},{6,14},{7,23},{8,0},{9,25... | collective-permute-start | bytes 393224 | tf_op jit(solution)/shard_map/ppermute | solution.py:165
  20.7 0.0 collective-permute-done.8.refs_2_.refs_1_
  20.7 3.0 %collective-permute-start.13 = (bf16[512,128]{1,0:T(8,128)(2,1)S(1)}, bf16[512,128]{1,0:T(8,128)(2,1)S(1)}, u32[]{:S(2)}, u32[]{:S(2)}) collective-permute-start(bf16[512,128]{1,0:T(8,128)(2,1)S(1)} %shard_map.63), channel_id=1, source_target_pairs={{1,2},{3,4},{5,6},{2,1},{4,3},{6,5},{9,10},{11,12},{13,14},{10,9},... | collective-permute-start | bytes 393224 | tf_op jit(solution)/shard_map/ppermute | solution.py:175
  23.7 0.0 collective-permute-done.9.refs_6_
  23.7 0.8 %collective-permute-start.14 = (bf16[512,128]{1,0:T(8,128)(2,1)S(1)}, bf16[512,128]{1,0:T(8,128)(2,1)S(1)}, u32[]{:S(2)}, u32[]{:S(2)}) collective-permute-start(bf16[512,128]{1,0:T(8,128)(2,1)S(1)} %collective-permute-done.9.refs_6_), channel_id=1, source_target_pairs={{0,16},{1,9},{2,18},{3,11},{4,20},{5,13},{6,22},{7,15},{8,24},{9,1... | collective-permute-start | bytes 393224 | tf_op jit(solution)/shard_map/ppermute | solution.py:165
  24.5 0.0 collective-permute-done.12.refs_10_
  24.5 1.7 %collective-permute-start.15 = (bf16[512,128]{1,0:T(8,128)(2,1)S(1)}, bf16[512,128]{1,0:T(8,128)(2,1)S(1)}, u32[]{:S(2)}, u32[]{:S(2)}) collective-permute-start(bf16[512,128]{1,0:T(8,128)(2,1)S(1)} %collective-permute-done.12.refs_10_), channel_id=1, source_target_pairs={{0,8},{1,17},{2,10},{3,19},{4,12},{5,21},{6,14},{7,23},{8,0},{9,25... | collective-permute-start | bytes 393224 | tf_op jit(solution)/shard_map/ppermute | solution.py:165
  26.2 0.0 collective-permute-done.10.refs_7_
  26.2 0.0 collective-permute-done.11.refs_9_
  26.2 1.1 %shard_map.62 = (f32[512,128]{1,0:T(8,128)S(1)}, f32[512,128]{1,0:T(8,128)S(1)}) custom-call(f32[512,128]{1,0:T(8,128)S(1)} %get-tuple-element.32.refs_0_, f32[512,128]{1,0:T(8,128)S(1)} %get-tuple-element.34.refs_1_, bf16[512,128]{1,0:T(8,128)(2,1)S(1)} %collective-permute-done.8.refs_2_.refs_1_, f32[512,8]{1,0:T(8,128)S(1)} %get-tuple-element.27.refs_3_.refs_2_, ...), custom_call_target="tpu_custom_call" | custom-call | flops 402653184 | bytes 4079616 | tf_op jit(solution)/shard_map/pallas_call | solution.py:31
  27.3 0.0 collective-permute-done.13.refs_2_
  27.3 0.7 %collective-permute-done.14.refs_6_ = bf16[512,128]{1,0:T(8,128)(2,1)S(1)} collective-permute-done((bf16[512,128]{1,0:T(8,128)(2,1)S(1)}, bf16[512,128]{1,0:T(8,128)(2,1)S(1)}, u32[]{:S(2)}, u32[]{:S(2)}) %collective-permute-start.14) | collective-permute-done | bytes 131104 | tf_op jit(solution)/shard_map/ppermute | solution.py:165
  28.0 0.6 %collective-permute-done.15.refs_7_ = bf16[512,128]{1,0:T(8,128)(2,1)S(1)} collective-permute-done((bf16[512,128]{1,0:T(8,128)(2,1)S(1)}, bf16[512,128]{1,0:T(8,128)(2,1)S(1)}, u32[]{:S(2)}, u32[]{:S(2)}) %collective-permute-start.15) | collective-permute-done | bytes 131104 | tf_op jit(solution)/shard_map/ppermute | solution.py:165
  28.5 1.2 %shard_map.64 = f32[1024,128]{1,0:T(8,128)} custom-call(f32[512,128]{1,0:T(8,128)S(1)} %get-tuple-element.37.refs_0_, f32[512,128]{1,0:T(8,128)S(1)} %get-tuple-element.38.refs_1_, bf16[512,128]{1,0:T(8,128)(2,1)S(1)} %collective-permute-done.13.refs_2_, f32[512,8]{1,0:T(8,128)S(1)} %get-tuple-element.27.refs_3_.refs_2_, ...), custom_call_target="tpu_custom_call" | custom-call | flops 134217728 | bytes 4080640 | tf_op jit(solution)/shard_map/pallas_call | solution.py:31
  (3 shorter events, 0.0 us)
Async XLA Ops:
  1.1 7.5 %collective-permute-start.2 = (bf16[512,128]{1,0:T(8,128)(2,1)S(1)}, bf16[512,128]{1,0:T(8,128)(2,1)S(1)}, u32[]{:S(2)}, u32[]{:S(2)}) collective-permute-start(bf16[512,128]{1,0:T(8,128)(2,1)S(1)} %get-tuple-element.26.refs_5_), channel_id=1, source_target_pairs={{0,16},{1,9},{2,18},{3,11},{4,20},{5,13},{6,22},{7,15},{8,24},{9,1... | collective-permute-start | bytes 393224 | tf_op jit(solution)/shard_map/ppermute | solution.py:165
  3.2 5.7 %collective-permute-start = (bf16[512,128]{1,0:T(8,128)(2,1)S(1)}, bf16[512,128]{1,0:T(8,128)(2,1)S(1)}, u32[]{:S(2)}, u32[]{:S(2)}) collective-permute-start(bf16[512,128]{1,0:T(8,128)(2,1)S(1)} %get-tuple-element.26.refs_5_), channel_id=1, source_target_pairs={{0,1},{1,0},{2,3},{3,2},{4,5},{5,4},{6,7},{7,6},{8,9},{9,8},{10,11... | collective-permute-start | bytes 393224 | tf_op jit(solution)/shard_map/ppermute | solution.py:170
  4.2 9.0 %collective-permute-start.3 = (bf16[512,128]{1,0:T(8,128)(2,1)S(1)}, bf16[512,128]{1,0:T(8,128)(2,1)S(1)}, u32[]{:S(2)}, u32[]{:S(2)}) collective-permute-start(bf16[512,128]{1,0:T(8,128)(2,1)S(1)} %get-tuple-element.29.refs_8_.refs_0_), channel_id=1, source_target_pairs={{0,8},{1,17},{2,10},{3,19},{4,12},{5,21},{6,14},{7,23},{8,0},{9,25... | collective-permute-start | bytes 393224 | tf_op jit(solution)/shard_map/ppermute | solution.py:165
  4.5 9.6 %collective-permute-start.1 = (bf16[512,128]{1,0:T(8,128)(2,1)S(1)}, bf16[512,128]{1,0:T(8,128)(2,1)S(1)}, u32[]{:S(2)}, u32[]{:S(2)}) collective-permute-start(bf16[512,128]{1,0:T(8,128)(2,1)S(1)} %get-tuple-element.26.refs_5_), channel_id=1, source_target_pairs={{0,8},{1,17},{2,10},{3,19},{4,12},{5,21},{6,14},{7,23},{8,0},{9,25... | collective-permute-start | bytes 393224 | tf_op jit(solution)/shard_map/ppermute | solution.py:165
  5.7 8.4 %collective-permute-start.4 = (bf16[512,128]{1,0:T(8,128)(2,1)S(1)}, bf16[512,128]{1,0:T(8,128)(2,1)S(1)}, u32[]{:S(2)}, u32[]{:S(2)}) collective-permute-start(bf16[512,128]{1,0:T(8,128)(2,1)S(1)} %get-tuple-element.29.refs_8_.refs_0_), channel_id=1, source_target_pairs={{0,16},{1,9},{2,18},{3,11},{4,20},{5,13},{6,22},{7,15},{8,24},{9,1... | collective-permute-start | bytes 393224 | tf_op jit(solution)/shard_map/ppermute | solution.py:165
  8.7 6.0 %collective-permute-start.5 = (bf16[512,128]{1,0:T(8,128)(2,1)S(1)}, bf16[512,128]{1,0:T(8,128)(2,1)S(1)}, u32[]{:S(2)}, u32[]{:S(2)}) collective-permute-start(bf16[512,128]{1,0:T(8,128)(2,1)S(1)} %shard_map.58), channel_id=1, source_target_pairs={{0,8},{1,17},{2,10},{3,19},{4,12},{5,21},{6,14},{7,23},{8,0},{9,25... | collective-permute-start | bytes 393224 | tf_op jit(solution)/shard_map/ppermute | solution.py:165
  9.0 7.3 %collective-permute-start.6 = (bf16[512,128]{1,0:T(8,128)(2,1)S(1)}, bf16[512,128]{1,0:T(8,128)(2,1)S(1)}, u32[]{:S(2)}, u32[]{:S(2)}) collective-permute-start(bf16[512,128]{1,0:T(8,128)(2,1)S(1)} %shard_map.60), channel_id=1, source_target_pairs={{1,2},{3,4},{5,6},{2,1},{4,3},{6,5},{9,10},{11,12},{13,14},{10,9},... | collective-permute-start | bytes 393224 | tf_op jit(solution)/shard_map/ppermute | solution.py:175
  13.2 3.9 %collective-permute-start.7 = (bf16[512,128]{1,0:T(8,128)(2,1)S(1)}, bf16[512,128]{1,0:T(8,128)(2,1)S(1)}, u32[]{:S(2)}, u32[]{:S(2)}) collective-permute-start(bf16[512,128]{1,0:T(8,128)(2,1)S(1)} %collective-permute-done.3.refs_9_), channel_id=1, source_target_pairs={{0,16},{1,9},{2,18},{3,11},{4,20},{5,13},{6,22},{7,15},{8,24},{9,1... | collective-permute-start | bytes 393224 | tf_op jit(solution)/shard_map/ppermute | solution.py:165
  15.0 5.7 %collective-permute-start.8 = (bf16[512,128]{1,0:T(8,128)(2,1)S(1)}, bf16[512,128]{1,0:T(8,128)(2,1)S(1)}, u32[]{:S(2)}, u32[]{:S(2)}) collective-permute-start(bf16[512,128]{1,0:T(8,128)(2,1)S(1)} %get-tuple-element.35.refs_5_), channel_id=1, source_target_pairs={{0,1},{1,0},{2,3},{3,2},{4,5},{5,4},{6,7},{7,6},{8,9},{9,8},{10,11... | collective-permute-start | bytes 393224 | tf_op jit(solution)/shard_map/ppermute | solution.py:170
  15.1 8.6 %collective-permute-start.9 = (bf16[512,128]{1,0:T(8,128)(2,1)S(1)}, bf16[512,128]{1,0:T(8,128)(2,1)S(1)}, u32[]{:S(2)}, u32[]{:S(2)}) collective-permute-start(bf16[512,128]{1,0:T(8,128)(2,1)S(1)} %get-tuple-element.35.refs_5_), channel_id=1, source_target_pairs={{0,8},{1,17},{2,10},{3,19},{4,12},{5,21},{6,14},{7,23},{8,0},{9,25... | collective-permute-start | bytes 393224 | tf_op jit(solution)/shard_map/ppermute | solution.py:165
  17.4 7.1 %collective-permute-start.12 = (bf16[512,128]{1,0:T(8,128)(2,1)S(1)}, bf16[512,128]{1,0:T(8,128)(2,1)S(1)}, u32[]{:S(2)}, u32[]{:S(2)}) collective-permute-start(bf16[512,128]{1,0:T(8,128)(2,1)S(1)} %get-tuple-element.36.refs_8_.refs_0_), channel_id=1, source_target_pairs={{0,16},{1,9},{2,18},{3,11},{4,20},{5,13},{6,22},{7,15},{8,24},{9,1... | collective-permute-start | bytes 393224 | tf_op jit(solution)/shard_map/ppermute | solution.py:165
  18.3 7.9 %collective-permute-start.10 = (bf16[512,128]{1,0:T(8,128)(2,1)S(1)}, bf16[512,128]{1,0:T(8,128)(2,1)S(1)}, u32[]{:S(2)}, u32[]{:S(2)}) collective-permute-start(bf16[512,128]{1,0:T(8,128)(2,1)S(1)} %get-tuple-element.35.refs_5_), channel_id=1, source_target_pairs={{0,16},{1,9},{2,18},{3,11},{4,20},{5,13},{6,22},{7,15},{8,24},{9,1... | collective-permute-start | bytes 393224 | tf_op jit(solution)/shard_map/ppermute | solution.py:165
  19.0 7.2 %collective-permute-start.11 = (bf16[512,128]{1,0:T(8,128)(2,1)S(1)}, bf16[512,128]{1,0:T(8,128)(2,1)S(1)}, u32[]{:S(2)}, u32[]{:S(2)}) collective-permute-start(bf16[512,128]{1,0:T(8,128)(2,1)S(1)} %get-tuple-element.36.refs_8_.refs_0_), channel_id=1, source_target_pairs={{0,8},{1,17},{2,10},{3,19},{4,12},{5,21},{6,14},{7,23},{8,0},{9,25... | collective-permute-start | bytes 393224 | tf_op jit(solution)/shard_map/ppermute | solution.py:165
  20.7 6.5 %collective-permute-start.13 = (bf16[512,128]{1,0:T(8,128)(2,1)S(1)}, bf16[512,128]{1,0:T(8,128)(2,1)S(1)}, u32[]{:S(2)}, u32[]{:S(2)}) collective-permute-start(bf16[512,128]{1,0:T(8,128)(2,1)S(1)} %shard_map.63), channel_id=1, source_target_pairs={{1,2},{3,4},{5,6},{2,1},{4,3},{6,5},{9,10},{11,12},{13,14},{10,9},... | collective-permute-start | bytes 393224 | tf_op jit(solution)/shard_map/ppermute | solution.py:175
  23.7 4.3 %collective-permute-start.14 = (bf16[512,128]{1,0:T(8,128)(2,1)S(1)}, bf16[512,128]{1,0:T(8,128)(2,1)S(1)}, u32[]{:S(2)}, u32[]{:S(2)}) collective-permute-start(bf16[512,128]{1,0:T(8,128)(2,1)S(1)} %collective-permute-done.9.refs_6_), channel_id=1, source_target_pairs={{0,16},{1,9},{2,18},{3,11},{4,20},{5,13},{6,22},{7,15},{8,24},{9,1... | collective-permute-start | bytes 393224 | tf_op jit(solution)/shard_map/ppermute | solution.py:165
  24.5 4.0 %collective-permute-start.15 = (bf16[512,128]{1,0:T(8,128)(2,1)S(1)}, bf16[512,128]{1,0:T(8,128)(2,1)S(1)}, u32[]{:S(2)}, u32[]{:S(2)}) collective-permute-start(bf16[512,128]{1,0:T(8,128)(2,1)S(1)} %collective-permute-done.12.refs_10_), channel_id=1, source_target_pairs={{0,8},{1,17},{2,10},{3,19},{4,12},{5,21},{6,14},{7,23},{8,0},{9,25... | collective-permute-start | bytes 393224 | tf_op jit(solution)/shard_map/ppermute | solution.py:165

commit v7 on v6

--- a/solution.py
+++ b/solution.py
@@ -44,8 +44,9 @@
     return 1 - lax.axis_index("cell") % 2
 
 
-def source_row(r, rows):
-    return r + is_first() * (rows - 1 - 2 * r)
+def turned(values):
+    first = is_first() == 1
+    return [jnp.where(first, other, value) for value, other in zip(values, values[::-1])]
 
 
 def prepare(rows, ins, outs, pop, mask, sems):
@@ -58,10 +59,10 @@
     for copy in copies:
         copy.wait()
     modes = outs["p0"].shape[0]
-    for r in range(rows):
-        source = source_row(r, rows)
-        keep = (1 - mask[pl.ds(source, 1), :]).astype(F32)
-        row = keep * pop[pl.ds(source, modes, stride=rows), :]
+    keeps = turned([(1 - mask[r : r + 1, :]).astype(F32) for r in range(rows)])
+    fields = turned([pop[pl.ds(r, modes, stride=rows), :] for r in range(rows)])
+    for r, (keep, field) in enumerate(zip(keeps, fields)):
+        row = keep * field
         outs["keep"][r : r + 1, :] = keep
         outs[f"p{r}"][...] = row
         outs[f"q{r}"][...] = row.astype(BF16)
@@ -133,17 +134,19 @@
         width = result.shape[1] // len(having)
         for i, r in enumerate(having):
             values[r] = values[r] - result[:, i * width : (i + 1) * width]
+    if ends and second:
+        modes = outs["out"].shape[0] // rows
+        last = [ins["keep"][r : r + 1] * (0.5 * ins[f"first{r}"][...] + 0.5 * values[r]) for r in range(rows)]
+        for r, value in enumerate(turned(last)):
+            outs["out"][pl.ds(r, modes, stride=rows), :] = value
+        return
     for r, value in values.items():
-        if not ends:
-            outs[f"sum{r}"][...] = value
-        elif not second:
+        if ends:
             value = ins["keep"][r : r + 1] * value
             outs[f"p{r}"][...] = value
             outs[f"q{r}"][...] = value.astype(BF16)
         else:
-            modes = outs["out"].shape[0] // rows
-            value = ins["keep"][r : r + 1] * (0.5 * ins[f"first{r}"][...] + 0.5 * value)
-            outs["out"][pl.ds(source_row(r, rows), modes, stride=rows), :] = value
+            outs[f"sum{r}"][...] = value
 
 
 def held(row, other):
@@ -182,7 +185,6 @@
     last = rows - 1
     bits = [1 << b for b in range(count.bit_length() - 1)]
     orders = [bits if r % 2 == 0 else bits[::-1] for r in range(rows)]
-    turned = [order[::-1] for order in orders]
     row_f32, row_bf16 = shape((modes, width), F32), shape((modes, width), BF16)
     keys = [(o, r) for r in range(rows) for o in range(count)]
     near = [(o, r) for o, r in keys if o == 0 or o in bits]
@@ -224,7 +226,7 @@
         hbm=("octant", "courant", "collision"),
         scratch=[pltpu.VMEM((1, modes), jnp.int32), pltpu.VMEM(courant.shape, F32), pltpu.SemaphoreType.DMA((3,))],
     )
-    blocks = [exchange(env[f"q{r}"], turned[r], count, env["c"] if r == 0 else None) for r in range(rows)]
+    blocks = [exchange(env[f"q{r}"], orders[r][::-1], count, env["c"] if r == 0 else None) for r in range(rows)]
     env["outer"] = between_pairs(held(env[f"q{last}"], env["inner"]))
     run(blocks, range(rows), False, near, ["inner"], False, False)
     if last:

time: 29.9 us -> 30 us (level)
  no operation moved by 1% of the time
where the time goes in v7:
time: 30 us; the launch traced here: 29.8 us
  starting transfers between devices  21.1 us (70%)
  Pallas kernels  6.39 us (21%)
  waiting for transfers between devices  2.11 us (7%)
    ppermute x12, starting transfers between devices, exchange(): blocks[offset ^ bit] = lax.ppermute(block, ('mode', 'cell'), pairs)  12.9 us
    ppermute x2, starting transfers between devices, between_pairs(): lax.ppermute(row, 'cell', steps + [(target, source) for source, target in...  7.18 us
    pallas_call x10, Pallas kernels, call(): pl.pallas_call(kernel, out_shape=list(outs.values()), in_specs=[HBM if n...  6.39 us
    ppermute x12, waiting for transfers between devices, exchange(): blocks[offset ^ bit] = lax.ppermute(block, ('mode', 'cell'), pairs)  2.1 us
    ppermute x2, starting transfers between devices, within_pair(): lax.ppermute(row, 'cell', [(i, i ^ 1) for i in range(lax.axis_size('cell'...  1.05 us
  transfers between devices with their start and end apart: 16, of which 3 were waited for; matrix products, arithmetic and copies ran while one was open for 0% of the time, Pallas kernels for 14%

profile of v7, /device:TPU:1, one launch (start us, length us, event | category | flops | bytes accessed | tf_op | source)
XLA Modules:
  0.0 29.8 jit_solution(6734284523074484341)
XLA Ops:
  0.0 1.2 %shard_map.55 = (f32[2,128]{1,0:T(2,128)S(1)}, f32[512,128]{1,0:T(8,128)S(1)}, bf16[512,128]{1,0:T(8,128)(2,1)S(1)}, f32[512,128]{1,0:T(8,128)S(1)}, bf16[512,128]{1,0:T(8,128)(2,1)S(1)}) custom-call(f32[1024,128]{1,0:T(8,128)} %bitcast.6, s32[2,128]{1,0:T(2,128)} %bitcast.8), custom_call_target="tpu_custom_call" | custom-call | bytes 1312768 | tf_op jit(solution)/shard_map/pallas_call | solution.py:31
  1.2 2.1 %collective-permute-start.2 = (bf16[512,128]{1,0:T(8,128)(2,1)S(1)}, bf16[512,128]{1,0:T(8,128)(2,1)S(1)}, u32[]{:S(2)}, u32[]{:S(2)}) collective-permute-start(bf16[512,128]{1,0:T(8,128)(2,1)S(1)} %get-tuple-element.26.refs_5_), channel_id=1, source_target_pairs={{0,16},{1,9},{2,18},{3,11},{4,20},{5,13},{6,22},{7,15},{8,24},{9,1... | collective-permute-start | bytes 393224 | tf_op jit(solution)/shard_map/ppermute | solution.py:168
  3.3 1.0 %collective-permute-start = (bf16[512,128]{1,0:T(8,128)(2,1)S(1)}, bf16[512,128]{1,0:T(8,128)(2,1)S(1)}, u32[]{:S(2)}, u32[]{:S(2)}) collective-permute-start(bf16[512,128]{1,0:T(8,128)(2,1)S(1)} %get-tuple-element.26.refs_5_), channel_id=1, source_target_pairs={{0,1},{1,0},{2,3},{3,2},{4,5},{5,4},{6,7},{7,6},{8,9},{9,8},{10,11... | collective-permute-start | bytes 393224 | tf_op jit(solution)/shard_map/ppermute | solution.py:173
  4.3 0.3 collective-permute-start.3
  4.5 1.2 %collective-permute-start.1 = (bf16[512,128]{1,0:T(8,128)(2,1)S(1)}, bf16[512,128]{1,0:T(8,128)(2,1)S(1)}, u32[]{:S(2)}, u32[]{:S(2)}) collective-permute-start(bf16[512,128]{1,0:T(8,128)(2,1)S(1)} %get-tuple-element.26.refs_5_), channel_id=1, source_target_pairs={{0,8},{1,17},{2,10},{3,19},{4,12},{5,21},{6,14},{7,23},{8,0},{9,25... | collective-permute-start | bytes 393224 | tf_op jit(solution)/shard_map/ppermute | solution.py:168
  5.7 1.2 %collective-permute-start.4 = (bf16[512,128]{1,0:T(8,128)(2,1)S(1)}, bf16[512,128]{1,0:T(8,128)(2,1)S(1)}, u32[]{:S(2)}, u32[]{:S(2)}) collective-permute-start(bf16[512,128]{1,0:T(8,128)(2,1)S(1)} %get-tuple-element.29.refs_8_.refs_0_), channel_id=1, source_target_pairs={{0,16},{1,9},{2,18},{3,11},{4,20},{5,13},{6,22},{7,15},{8,24},{9,1... | collective-permute-start | bytes 393224 | tf_op jit(solution)/shard_map/ppermute | solution.py:168
  6.9 1.7 %shard_map.56 = (bf16[512,2048]{1,0:T(8,128)(2,1)S(1)}, f32[512,8]{1,0:T(8,128)S(1)}, f32[512,128]{1,0:T(8,128)S(1)}, f32[512,128]{1,0:T(8,128)S(1)}) custom-call(s32[1,512]{1,0:T(1,128)} %bitcast.7, f32[3,512]{1,0:T(4,128)} %refs_1_.1, bf16[512,2048]{1,0:T(8,128)(2,1)} %refs_2_.1, f32[512,128]{1,0:T(8,128)S(1)} %get-tuple-element.22.refs_3_.refs_8_, ...), custom_call_target="tpu_custom_call" | custom-call | bytes 5267456 | tf_op jit(solution)/shard_map/pallas_call | solution.py:31
  8.7 0.0 collective-permute-done.2.refs_7_.refs_0_
  8.7 0.3 collective-permute-start.5
  9.0 0.0 collective-permute-done.refs_2_.refs_1_
  9.0 4.2 %collective-permute-start.6 = (bf16[512,128]{1,0:T(8,128)(2,1)S(1)}, bf16[512,128]{1,0:T(8,128)(2,1)S(1)}, u32[]{:S(2)}, u32[]{:S(2)}) collective-permute-start(bf16[512,128]{1,0:T(8,128)(2,1)S(1)} %shard_map.60), channel_id=1, source_target_pairs={{1,2},{3,4},{5,6},{2,1},{4,3},{6,5},{9,10},{11,12},{13,14},{10,9},... | collective-permute-start | bytes 393224 | tf_op jit(solution)/shard_map/ppermute | solution.py:178
  13.3 0.0 collective-permute-done.3.refs_9_
  13.3 0.9 %collective-permute-start.7 = (bf16[512,128]{1,0:T(8,128)(2,1)S(1)}, bf16[512,128]{1,0:T(8,128)(2,1)S(1)}, u32[]{:S(2)}, u32[]{:S(2)}) collective-permute-start(bf16[512,128]{1,0:T(8,128)(2,1)S(1)} %collective-permute-done.3.refs_9_), channel_id=1, source_target_pairs={{0,16},{1,9},{2,18},{3,11},{4,20},{5,13},{6,22},{7,15},{8,24},{9,1... | collective-permute-start | bytes 393224 | tf_op jit(solution)/shard_map/ppermute | solution.py:168
  14.1 0.0 collective-permute-done.1.refs_6_
  14.1 0.0 collective-permute-done.4.refs_10_
  14.1 0.6 %shard_map.57 = (f32[512,128]{1,0:T(8,128)S(1)}, f32[512,128]{1,0:T(8,128)S(1)}) custom-call(f32[512,128]{1,0:T(8,128)S(1)} %get-tuple-element.24.refs_0_, f32[512,128]{1,0:T(8,128)S(1)} %get-tuple-element.25.refs_1_, bf16[512,128]{1,0:T(8,128)(2,1)S(1)} %collective-permute-done.refs_2_.refs_1_, f32[512,8]{1,0:T(8,128)S(1)} %get-tuple-element.27.refs_3_.refs_2_, ...), custom_call_target="tpu_custom_call" | custom-call | flops 402653184 | bytes 4079616 | tf_op jit(solution)/shard_map/pallas_call | solution.py:31
  14.7 0.0 collective-permute-done.5.refs_3_
  14.8 0.3 shard_map.59
  15.1 0.1 collective-permute-start.8
  15.1 1.2 %collective-permute-start.9 = (bf16[512,128]{1,0:T(8,128)(2,1)S(1)}, bf16[512,128]{1,0:T(8,128)(2,1)S(1)}, u32[]{:S(2)}, u32[]{:S(2)}) collective-permute-start(bf16[512,128]{1,0:T(8,128)(2,1)S(1)} %get-tuple-element.35.refs_5_), channel_id=1, source_target_pairs={{0,8},{1,17},{2,10},{3,19},{4,12},{5,21},{6,14},{7,23},{8,0},{9,25... | collective-permute-start | bytes 393224 | tf_op jit(solution)/shard_map/ppermute | solution.py:168
  16.4 0.0 collective-permute-done.6.refs_1_
  16.4 0.8 %collective-permute-done.7.refs_5_ = bf16[512,128]{1,0:T(8,128)(2,1)S(1)} collective-permute-done((bf16[512,128]{1,0:T(8,128)(2,1)S(1)}, bf16[512,128]{1,0:T(8,128)(2,1)S(1)}, u32[]{:S(2)}, u32[]{:S(2)}) %collective-permute-start.7) | collective-permute-done | bytes 131104 | tf_op jit(solution)/shard_map/ppermute | solution.py:168
  17.2 0.3 %shard_map.61 = (f32[512,128]{1,0:T(8,128)S(1)}, bf16[512,128]{1,0:T(8,128)(2,1)S(1)}) custom-call(f32[512,128]{1,0:T(8,128)S(1)} %get-tuple-element.33.refs_0_, bf16[512,128]{1,0:T(8,128)(2,1)S(1)} %collective-permute-done.6.refs_1_, f32[512,8]{1,0:T(8,128)S(1)} %get-tuple-element.27.refs_3_.refs_2_, ...), custom_call_target="tpu_custom_call" | custom-call | flops 67108864 | bytes 3032064 | tf_op jit(solution)/shard_map/pallas_call | solution.py:31
  17.5 0.9 %collective-permute-start.12 = (bf16[512,128]{1,0:T(8,128)(2,1)S(1)}, bf16[512,128]{1,0:T(8,128)(2,1)S(1)}, u32[]{:S(2)}, u32[]{:S(2)}) collective-permute-start(bf16[512,128]{1,0:T(8,128)(2,1)S(1)} %get-tuple-element.36.refs_8_.refs_0_), channel_id=1, source_target_pairs={{0,16},{1,9},{2,18},{3,11},{4,20},{5,13},{6,22},{7,15},{8,24},{9,1... | collective-permute-start | bytes 393224 | tf_op jit(solution)/shard_map/ppermute | solution.py:168
  18.3 0.7 %collective-permute-start.10 = (bf16[512,128]{1,0:T(8,128)(2,1)S(1)}, bf16[512,128]{1,0:T(8,128)(2,1)S(1)}, u32[]{:S(2)}, u32[]{:S(2)}) collective-permute-start(bf16[512,128]{1,0:T(8,128)(2,1)S(1)} %get-tuple-element.35.refs_5_), channel_id=1, source_target_pairs={{0,16},{1,9},{2,18},{3,11},{4,20},{5,13},{6,22},{7,15},{8,24},{9,1... | collective-permute-start | bytes 393224 | tf_op jit(solution)/shard_map/ppermute | solution.py:168
  19.0 1.7 %collective-permute-start.11 = (bf16[512,128]{1,0:T(8,128)(2,1)S(1)}, bf16[512,128]{1,0:T(8,128)(2,1)S(1)}, u32[]{:S(2)}, u32[]{:S(2)}) collective-permute-start(bf16[512,128]{1,0:T(8,128)(2,1)S(1)} %get-tuple-element.36.refs_8_.refs_0_), channel_id=1, source_target_pairs={{0,8},{1,17},{2,10},{3,19},{4,12},{5,21},{6,14},{7,23},{8,0},{9,25... | collective-permute-start | bytes 393224 | tf_op jit(solution)/shard_map/ppermute | solution.py:168
  20.7 0.0 collective-permute-done.8.refs_2_.refs_1_
  20.8 3.0 %collective-permute-start.13 = (bf16[512,128]{1,0:T(8,128)(2,1)S(1)}, bf16[512,128]{1,0:T(8,128)(2,1)S(1)}, u32[]{:S(2)}, u32[]{:S(2)}) collective-permute-start(bf16[512,128]{1,0:T(8,128)(2,1)S(1)} %shard_map.63), channel_id=1, source_target_pairs={{1,2},{3,4},{5,6},{2,1},{4,3},{6,5},{9,10},{11,12},{13,14},{10,9},... | collective-permute-start | bytes 393224 | tf_op jit(solution)/shard_map/ppermute | solution.py:178
  23.7 0.0 collective-permute-done.9.refs_6_
  23.7 0.8 %collective-permute-start.14 = (bf16[512,128]{1,0:T(8,128)(2,1)S(1)}, bf16[512,128]{1,0:T(8,128)(2,1)S(1)}, u32[]{:S(2)}, u32[]{:S(2)}) collective-permute-start(bf16[512,128]{1,0:T(8,128)(2,1)S(1)} %collective-permute-done.9.refs_6_), channel_id=1, source_target_pairs={{0,16},{1,9},{2,18},{3,11},{4,20},{5,13},{6,22},{7,15},{8,24},{9,1... | collective-permute-start | bytes 393224 | tf_op jit(solution)/shard_map/ppermute | solution.py:168
  24.6 0.0 collective-permute-done.12.refs_10_
  24.6 1.7 %collective-permute-start.15 = (bf16[512,128]{1,0:T(8,128)(2,1)S(1)}, bf16[512,128]{1,0:T(8,128)(2,1)S(1)}, u32[]{:S(2)}, u32[]{:S(2)}) collective-permute-start(bf16[512,128]{1,0:T(8,128)(2,1)S(1)} %collective-permute-done.12.refs_10_), channel_id=1, source_target_pairs={{0,8},{1,17},{2,10},{3,19},{4,12},{5,21},{6,14},{7,23},{8,0},{9,25... | collective-permute-start | bytes 393224 | tf_op jit(solution)/shard_map/ppermute | solution.py:168
  26.2 0.0 collective-permute-done.10.refs_7_
  26.2 0.0 collective-permute-done.11.refs_9_
  26.2 1.1 %shard_map.62 = (f32[512,128]{1,0:T(8,128)S(1)}, f32[512,128]{1,0:T(8,128)S(1)}) custom-call(f32[512,128]{1,0:T(8,128)S(1)} %get-tuple-element.32.refs_0_, f32[512,128]{1,0:T(8,128)S(1)} %get-tuple-element.34.refs_1_, bf16[512,128]{1,0:T(8,128)(2,1)S(1)} %collective-permute-done.8.refs_2_.refs_1_, f32[512,8]{1,0:T(8,128)S(1)} %get-tuple-element.27.refs_3_.refs_2_, ...), custom_call_target="tpu_custom_call" | custom-call | flops 402653184 | bytes 4079616 | tf_op jit(solution)/shard_map/pallas_call | solution.py:31
  27.3 0.0 collective-permute-done.13.refs_2_
  27.3 0.7 %collective-permute-done.14.refs_6_ = bf16[512,128]{1,0:T(8,128)(2,1)S(1)} collective-permute-done((bf16[512,128]{1,0:T(8,128)(2,1)S(1)}, bf16[512,128]{1,0:T(8,128)(2,1)S(1)}, u32[]{:S(2)}, u32[]{:S(2)}) %collective-permute-start.14) | collective-permute-done | bytes 131104 | tf_op jit(solution)/shard_map/ppermute | solution.py:168
  28.0 0.6 %collective-permute-done.15.refs_7_ = bf16[512,128]{1,0:T(8,128)(2,1)S(1)} collective-permute-done((bf16[512,128]{1,0:T(8,128)(2,1)S(1)}, bf16[512,128]{1,0:T(8,128)(2,1)S(1)}, u32[]{:S(2)}, u32[]{:S(2)}) %collective-permute-start.15) | collective-permute-done | bytes 131104 | tf_op jit(solution)/shard_map/ppermute | solution.py:168
  28.6 1.2 %shard_map.64 = f32[1024,128]{1,0:T(8,128)} custom-call(f32[512,128]{1,0:T(8,128)S(1)} %get-tuple-element.37.refs_0_, f32[512,128]{1,0:T(8,128)S(1)} %get-tuple-element.38.refs_1_, bf16[512,128]{1,0:T(8,128)(2,1)S(1)} %collective-permute-done.13.refs_2_, f32[512,8]{1,0:T(8,128)S(1)} %get-tuple-element.27.refs_3_.refs_2_, ...), custom_call_target="tpu_custom_call" | custom-call | flops 134217728 | bytes 4080640 | tf_op jit(solution)/shard_map/pallas_call | solution.py:31
  (3 shorter events, 0.0 us)
Async XLA Ops:
  1.2 7.5 %collective-permute-start.2 = (bf16[512,128]{1,0:T(8,128)(2,1)S(1)}, bf16[512,128]{1,0:T(8,128)(2,1)S(1)}, u32[]{:S(2)}, u32[]{:S(2)}) collective-permute-start(bf16[512,128]{1,0:T(8,128)(2,1)S(1)} %get-tuple-element.26.refs_5_), channel_id=1, source_target_pairs={{0,16},{1,9},{2,18},{3,11},{4,20},{5,13},{6,22},{7,15},{8,24},{9,1... | collective-permute-start | bytes 393224 | tf_op jit(solution)/shard_map/ppermute | solution.py:168
  3.3 5.7 %collective-permute-start = (bf16[512,128]{1,0:T(8,128)(2,1)S(1)}, bf16[512,128]{1,0:T(8,128)(2,1)S(1)}, u32[]{:S(2)}, u32[]{:S(2)}) collective-permute-start(bf16[512,128]{1,0:T(8,128)(2,1)S(1)} %get-tuple-element.26.refs_5_), channel_id=1, source_target_pairs={{0,1},{1,0},{2,3},{3,2},{4,5},{5,4},{6,7},{7,6},{8,9},{9,8},{10,11... | collective-permute-start | bytes 393224 | tf_op jit(solution)/shard_map/ppermute | solution.py:173
  4.3 9.0 %collective-permute-start.3 = (bf16[512,128]{1,0:T(8,128)(2,1)S(1)}, bf16[512,128]{1,0:T(8,128)(2,1)S(1)}, u32[]{:S(2)}, u32[]{:S(2)}) collective-permute-start(bf16[512,128]{1,0:T(8,128)(2,1)S(1)} %get-tuple-element.29.refs_8_.refs_0_), channel_id=1, source_target_pairs={{0,8},{1,17},{2,10},{3,19},{4,12},{5,21},{6,14},{7,23},{8,0},{9,25... | collective-permute-start | bytes 393224 | tf_op jit(solution)/shard_map/ppermute | solution.py:168
  4.5 9.6 %collective-permute-start.1 = (bf16[512,128]{1,0:T(8,128)(2,1)S(1)}, bf16[512,128]{1,0:T(8,128)(2,1)S(1)}, u32[]{:S(2)}, u32[]{:S(2)}) collective-permute-start(bf16[512,128]{1,0:T(8,128)(2,1)S(1)} %get-tuple-element.26.refs_5_), channel_id=1, source_target_pairs={{0,8},{1,17},{2,10},{3,19},{4,12},{5,21},{6,14},{7,23},{8,0},{9,25... | collective-permute-start | bytes 393224 | tf_op jit(solution)/shard_map/ppermute | solution.py:168
  5.7 8.4 %collective-permute-start.4 = (bf16[512,128]{1,0:T(8,128)(2,1)S(1)}, bf16[512,128]{1,0:T(8,128)(2,1)S(1)}, u32[]{:S(2)}, u32[]{:S(2)}) collective-permute-start(bf16[512,128]{1,0:T(8,128)(2,1)S(1)} %get-tuple-element.29.refs_8_.refs_0_), channel_id=1, source_target_pairs={{0,16},{1,9},{2,18},{3,11},{4,20},{5,13},{6,22},{7,15},{8,24},{9,1... | collective-permute-start | bytes 393224 | tf_op jit(solution)/shard_map/ppermute | solution.py:168
  8.7 6.0 %collective-permute-start.5 = (bf16[512,128]{1,0:T(8,128)(2,1)S(1)}, bf16[512,128]{1,0:T(8,128)(2,1)S(1)}, u32[]{:S(2)}, u32[]{:S(2)}) collective-permute-start(bf16[512,128]{1,0:T(8,128)(2,1)S(1)} %shard_map.58), channel_id=1, source_target_pairs={{0,8},{1,17},{2,10},{3,19},{4,12},{5,21},{6,14},{7,23},{8,0},{9,25... | collective-permute-start | bytes 393224 | tf_op jit(solution)/shard_map/ppermute | solution.py:168
  9.0 7.3 %collective-permute-start.6 = (bf16[512,128]{1,0:T(8,128)(2,1)S(1)}, bf16[512,128]{1,0:T(8,128)(2,1)S(1)}, u32[]{:S(2)}, u32[]{:S(2)}) collective-permute-start(bf16[512,128]{1,0:T(8,128)(2,1)S(1)} %shard_map.60), channel_id=1, source_target_pairs={{1,2},{3,4},{5,6},{2,1},{4,3},{6,5},{9,10},{11,12},{13,14},{10,9},... | collective-permute-start | bytes 393224 | tf_op jit(solution)/shard_map/ppermute | solution.py:178
  13.3 3.9 %collective-permute-start.7 = (bf16[512,128]{1,0:T(8,128)(2,1)S(1)}, bf16[512,128]{1,0:T(8,128)(2,1)S(1)}, u32[]{:S(2)}, u32[]{:S(2)}) collective-permute-start(bf16[512,128]{1,0:T(8,128)(2,1)S(1)} %collective-permute-done.3.refs_9_), channel_id=1, source_target_pairs={{0,16},{1,9},{2,18},{3,11},{4,20},{5,13},{6,22},{7,15},{8,24},{9,1... | collective-permute-start | bytes 393224 | tf_op jit(solution)/shard_map/ppermute | solution.py:168
  15.1 5.7 %collective-permute-start.8 = (bf16[512,128]{1,0:T(8,128)(2,1)S(1)}, bf16[512,128]{1,0:T(8,128)(2,1)S(1)}, u32[]{:S(2)}, u32[]{:S(2)}) collective-permute-start(bf16[512,128]{1,0:T(8,128)(2,1)S(1)} %get-tuple-element.35.refs_5_), channel_id=1, source_target_pairs={{0,1},{1,0},{2,3},{3,2},{4,5},{5,4},{6,7},{7,6},{8,9},{9,8},{10,11... | collective-permute-start | bytes 393224 | tf_op jit(solution)/shard_map/ppermute | solution.py:173
  15.1 8.6 %collective-permute-start.9 = (bf16[512,128]{1,0:T(8,128)(2,1)S(1)}, bf16[512,128]{1,0:T(8,128)(2,1)S(1)}, u32[]{:S(2)}, u32[]{:S(2)}) collective-permute-start(bf16[512,128]{1,0:T(8,128)(2,1)S(1)} %get-tuple-element.35.refs_5_), channel_id=1, source_target_pairs={{0,8},{1,17},{2,10},{3,19},{4,12},{5,21},{6,14},{7,23},{8,0},{9,25... | collective-permute-start | bytes 393224 | tf_op jit(solution)/shard_map/ppermute | solution.py:168
  17.5 7.1 %collective-permute-start.12 = (bf16[512,128]{1,0:T(8,128)(2,1)S(1)}, bf16[512,128]{1,0:T(8,128)(2,1)S(1)}, u32[]{:S(2)}, u32[]{:S(2)}) collective-permute-start(bf16[512,128]{1,0:T(8,128)(2,1)S(1)} %get-tuple-element.36.refs_8_.refs_0_), channel_id=1, source_target_pairs={{0,16},{1,9},{2,18},{3,11},{4,20},{5,13},{6,22},{7,15},{8,24},{9,1... | collective-permute-start | bytes 393224 | tf_op jit(solution)/shard_map/ppermute | solution.py:168
  18.3 7.9 %collective-permute-start.10 = (bf16[512,128]{1,0:T(8,128)(2,1)S(1)}, bf16[512,128]{1,0:T(8,128)(2,1)S(1)}, u32[]{:S(2)}, u32[]{:S(2)}) collective-permute-start(bf16[512,128]{1,0:T(8,128)(2,1)S(1)} %get-tuple-element.35.refs_5_), channel_id=1, source_target_pairs={{0,16},{1,9},{2,18},{3,11},{4,20},{5,13},{6,22},{7,15},{8,24},{9,1... | collective-permute-start | bytes 393224 | tf_op jit(solution)/shard_map/ppermute | solution.py:168
  19.0 7.2 %collective-permute-start.11 = (bf16[512,128]{1,0:T(8,128)(2,1)S(1)}, bf16[512,128]{1,0:T(8,128)(2,1)S(1)}, u32[]{:S(2)}, u32[]{:S(2)}) collective-permute-start(bf16[512,128]{1,0:T(8,128)(2,1)S(1)} %get-tuple-element.36.refs_8_.refs_0_), channel_id=1, source_target_pairs={{0,8},{1,17},{2,10},{3,19},{4,12},{5,21},{6,14},{7,23},{8,0},{9,25... | collective-permute-start | bytes 393224 | tf_op jit(solution)/shard_map/ppermute | solution.py:168
  20.8 6.5 %collective-permute-start.13 = (bf16[512,128]{1,0:T(8,128)(2,1)S(1)}, bf16[512,128]{1,0:T(8,128)(2,1)S(1)}, u32[]{:S(2)}, u32[]{:S(2)}) collective-permute-start(bf16[512,128]{1,0:T(8,128)(2,1)S(1)} %shard_map.63), channel_id=1, source_target_pairs={{1,2},{3,4},{5,6},{2,1},{4,3},{6,5},{9,10},{11,12},{13,14},{10,9},... | collective-permute-start | bytes 393224 | tf_op jit(solution)/shard_map/ppermute | solution.py:178
  23.7 4.2 %collective-permute-start.14 = (bf16[512,128]{1,0:T(8,128)(2,1)S(1)}, bf16[512,128]{1,0:T(8,128)(2,1)S(1)}, u32[]{:S(2)}, u32[]{:S(2)}) collective-permute-start(bf16[512,128]{1,0:T(8,128)(2,1)S(1)} %collective-permute-done.9.refs_6_), channel_id=1, source_target_pairs={{0,16},{1,9},{2,18},{3,11},{4,20},{5,13},{6,22},{7,15},{8,24},{9,1... | collective-permute-start | bytes 393224 | tf_op jit(solution)/shard_map/ppermute | solution.py:168
  24.6 4.0 %collective-permute-start.15 = (bf16[512,128]{1,0:T(8,128)(2,1)S(1)}, bf16[512,128]{1,0:T(8,128)(2,1)S(1)}, u32[]{:S(2)}, u32[]{:S(2)}) collective-permute-start(bf16[512,128]{1,0:T(8,128)(2,1)S(1)} %collective-permute-done.12.refs_10_), channel_id=1, source_target_pairs={{0,8},{1,17},{2,10},{3,19},{4,12},{5,21},{6,14},{7,23},{8,0},{9,25... | collective-permute-start | bytes 393224 | tf_op jit(solution)/shard_map/ppermute | solution.py:168

commit v8 on v7

--- a/solution.py
+++ b/solution.py
@@ -114,9 +114,12 @@
     coef = coefficients(octant[...], courant[...])
     outs["coef"][...] = coef
     fields = [ins[f"p{r}"][...] for r in range(rows)]
+    moved = [drift(fields, r, coef) for r in range(rows)]
+    copies[2].wait()
+    own = product(outs["c"], 0, [ins[f"q{r}"][...] for r in range(rows)])
+    width = own.shape[1] // rows
     for r in range(rows):
-        outs[f"sum{r}"][...] = drift(fields, r, coef)
-    copies[2].wait()
+        outs[f"sum{r}"][...] = moved[r] - own[:, r * width : (r + 1) * width]
 
 
 def step(rows, which, moves, keys, halos, ends, second, ins, outs):
@@ -221,14 +224,14 @@
     env |= call(
         functools.partial(begin, rows),
         {"octant": octant.reshape(1, modes), "courant": courant, "collision": collision}
-        | {f"p{r}": env[f"p{r}"] for r in range(rows)},
+        | {f"{n}{r}": env[f"{n}{r}"] for n in "pq" for r in range(rows)},
         {"c": shape(collision.shape, BF16), "coef": shape((modes, 8), F32)} | {f"sum{r}": row_f32 for r in range(rows)},
         hbm=("octant", "courant", "collision"),
         scratch=[pltpu.VMEM((1, modes), jnp.int32), pltpu.VMEM(courant.shape, F32), pltpu.SemaphoreType.DMA((3,))],
     )
     blocks = [exchange(env[f"q{r}"], orders[r][::-1], count, env["c"] if r == 0 else None) for r in range(rows)]
     env["outer"] = between_pairs(held(env[f"q{last}"], env["inner"]))
-    run(blocks, range(rows), False, near, ["inner"], False, False)
+    run(blocks, range(rows), False, [key for key in near if key[0]], ["inner"], False, False)
     if last:
         run(blocks, range(last), False, [k for k in far if k[1] < last], [], True, False)
     run(blocks, range(last, rows), False, [k for k in far if k[1] == last], ["outer"], True, False)

time: 30 us -> 30 us (level)
  starting transfers between devices: 21.1 us -> 20.6 us
  waiting for transfers between devices: 2.11 us -> 2.57 us
    ppermute x12, starting transfers between devices: 12.9 us -> 12.1 us  [exchange(): blocks[offset ^ bit] = lax.ppermute(block, ('mode', 'cell'), pairs)]
    ppermute x12, waiting for transfers between devices: 2.1 us -> 2.56 us  [exchange(): blocks[offset ^ bit] = lax.ppermute(block, ('mode', 'cell'), pairs)]
where the time goes in v8:
time: 30 us; the launch traced here: 29.7 us
  starting transfers between devices  20.6 us (69%)
  Pallas kernels  6.43 us (21%)
  waiting for transfers between devices  2.57 us (9%)
    ppermute x12, starting transfers between devices, exchange(): blocks[offset ^ bit] = lax.ppermute(block, ('mode', 'cell'), pairs)  12.1 us
    ppermute x2, starting transfers between devices, between_pairs(): lax.ppermute(row, 'cell', steps + [(target, source) for source, target in...  7.44 us
    pallas_call x10, Pallas kernels, call(): pl.pallas_call(kernel, out_shape=list(outs.values()), in_specs=[HBM if n...  6.43 us
    ppermute x12, waiting for transfers between devices, exchange(): blocks[offset ^ bit] = lax.ppermute(block, ('mode', 'cell'), pairs)  2.56 us
    ppermute x2, starting transfers between devices, within_pair(): lax.ppermute(row, 'cell', [(i, i ^ 1) for i in range(lax.axis_size('cell'...  1.05 us
  transfers between devices with their start and end apart: 16, of which 3 were waited for; matrix products, arithmetic and copies ran while one was open for 0% of the time, Pallas kernels for 14%

profile of v8, /device:TPU:1, one launch (start us, length us, event | category | flops | bytes accessed | tf_op | source)
XLA Modules:
  0.0 29.7 jit_solution(452131264364643554)
XLA Ops:
  0.0 1.2 %shard_map.55 = (f32[2,128]{1,0:T(2,128)S(1)}, f32[512,128]{1,0:T(8,128)S(1)}, bf16[512,128]{1,0:T(8,128)(2,1)S(1)}, f32[512,128]{1,0:T(8,128)S(1)}, bf16[512,128]{1,0:T(8,128)(2,1)S(1)}) custom-call(f32[1024,128]{1,0:T(8,128)} %bitcast.6, s32[2,128]{1,0:T(2,128)} %bitcast.8), custom_call_target="tpu_custom_call" | custom-call | bytes 1312768 | tf_op jit(solution)/shard_map/pallas_call | solution.py:31
  1.2 2.1 %collective-permute-start.2 = (bf16[512,128]{1,0:T(8,128)(2,1)S(1)}, bf16[512,128]{1,0:T(8,128)(2,1)S(1)}, u32[]{:S(2)}, u32[]{:S(2)}) collective-permute-start(bf16[512,128]{1,0:T(8,128)(2,1)S(1)} %get-tuple-element.24.refs_5_), channel_id=1, source_target_pairs={{0,16},{1,9},{2,18},{3,11},{4,20},{5,13},{6,22},{7,15},{8,24},{9,1... | collective-permute-start | bytes 393224 | tf_op jit(solution)/shard_map/ppermute | solution.py:171
  3.3 1.0 %collective-permute-start = (bf16[512,128]{1,0:T(8,128)(2,1)S(1)}, bf16[512,128]{1,0:T(8,128)(2,1)S(1)}, u32[]{:S(2)}, u32[]{:S(2)}) collective-permute-start(bf16[512,128]{1,0:T(8,128)(2,1)S(1)} %get-tuple-element.24.refs_5_), channel_id=1, source_target_pairs={{0,1},{1,0},{2,3},{3,2},{4,5},{5,4},{6,7},{7,6},{8,9},{9,8},{10,11... | collective-permute-start | bytes 393224 | tf_op jit(solution)/shard_map/ppermute | solution.py:176
  4.3 0.3 collective-permute-start.3
  4.5 1.2 %collective-permute-start.1 = (bf16[512,128]{1,0:T(8,128)(2,1)S(1)}, bf16[512,128]{1,0:T(8,128)(2,1)S(1)}, u32[]{:S(2)}, u32[]{:S(2)}) collective-permute-start(bf16[512,128]{1,0:T(8,128)(2,1)S(1)} %get-tuple-element.24.refs_5_), channel_id=1, source_target_pairs={{0,8},{1,17},{2,10},{3,19},{4,12},{5,21},{6,14},{7,23},{8,0},{9,25... | collective-permute-start | bytes 393224 | tf_op jit(solution)/shard_map/ppermute | solution.py:171
  5.7 1.2 %collective-permute-start.4 = (bf16[512,128]{1,0:T(8,128)(2,1)S(1)}, bf16[512,128]{1,0:T(8,128)(2,1)S(1)}, u32[]{:S(2)}, u32[]{:S(2)}) collective-permute-start(bf16[512,128]{1,0:T(8,128)(2,1)S(1)} %get-tuple-element.25.refs_6_.refs_0_), channel_id=1, source_target_pairs={{0,16},{1,9},{2,18},{3,11},{4,20},{5,13},{6,22},{7,15},{8,24},{9,1... | collective-permute-start | bytes 393224 | tf_op jit(solution)/shard_map/ppermute | solution.py:171
  6.9 2.0 %shard_map.56 = (bf16[512,2048]{1,0:T(8,128)(2,1)S(1)}, f32[512,8]{1,0:T(8,128)S(1)}, f32[512,128]{1,0:T(8,128)S(1)}, f32[512,128]{1,0:T(8,128)S(1)}) custom-call(s32[1,512]{1,0:T(1,128)} %bitcast.7, f32[3,512]{1,0:T(4,128)} %refs_1_.1, bf16[512,2048]{1,0:T(8,128)(2,1)} %refs_2_.1, f32[512,128]{1,0:T(8,128)S(1)} %get-tuple-element.22.refs_3_.refs_8_, ...), custom_call_target="tpu_custom_call" | custom-call | bytes 5529600 | tf_op jit(solution)/shard_map/pallas_call | solution.py:31
  9.0 0.0 collective-permute-done.2.refs_6_.refs_0_
  9.0 0.3 collective-permute-start.5
  9.3 0.0 collective-permute-done.refs_2_.refs_1_
  9.3 4.2 %collective-permute-start.6 = (bf16[512,128]{1,0:T(8,128)(2,1)S(1)}, bf16[512,128]{1,0:T(8,128)(2,1)S(1)}, u32[]{:S(2)}, u32[]{:S(2)}) collective-permute-start(bf16[512,128]{1,0:T(8,128)(2,1)S(1)} %shard_map.60), channel_id=1, source_target_pairs={{1,2},{3,4},{5,6},{2,1},{4,3},{6,5},{9,10},{11,12},{13,14},{10,9},... | collective-permute-start | bytes 393224 | tf_op jit(solution)/shard_map/ppermute | solution.py:181
  13.5 0.0 collective-permute-done.3.refs_7_
  13.5 0.9 %collective-permute-start.7 = (bf16[512,128]{1,0:T(8,128)(2,1)S(1)}, bf16[512,128]{1,0:T(8,128)(2,1)S(1)}, u32[]{:S(2)}, u32[]{:S(2)}) collective-permute-start(bf16[512,128]{1,0:T(8,128)(2,1)S(1)} %collective-permute-done.3.refs_7_), channel_id=1, source_target_pairs={{0,16},{1,9},{2,18},{3,11},{4,20},{5,13},{6,22},{7,15},{8,24},{9,1... | collective-permute-start | bytes 393224 | tf_op jit(solution)/shard_map/ppermute | solution.py:171
  14.4 0.0 collective-permute-done.1.refs_5_
  14.4 0.0 collective-permute-done.4.refs_8_
  14.4 0.5 %shard_map.57 = (f32[512,128]{1,0:T(8,128)S(1)}, f32[512,128]{1,0:T(8,128)S(1)}) custom-call(f32[512,128]{1,0:T(8,128)S(1)} %get-tuple-element.26.refs_0_, f32[512,128]{1,0:T(8,128)S(1)} %get-tuple-element.27.refs_1_, bf16[512,128]{1,0:T(8,128)(2,1)S(1)} %collective-permute-done.refs_2_.refs_1_, f32[512,8]{1,0:T(8,128)S(1)} %get-tuple-element.28.refs_3_.refs_2_, ...), custom_call_target="tpu_custom_call" | custom-call | flops 268435456 | bytes 3817472 | tf_op jit(solution)/shard_map/pallas_call | solution.py:31
  14.8 0.0 collective-permute-done.5.refs_3_
  14.9 0.3 %shard_map.59 = (f32[512,128]{1,0:T(8,128)S(1)}, bf16[512,128]{1,0:T(8,128)(2,1)S(1)}) custom-call(f32[512,128]{1,0:T(8,128)S(1)} %get-tuple-element.30.refs_0_, bf16[512,2048]{1,0:T(8,128)(2,1)S(1)} %get-tuple-element.29.refs_4_.refs_1_.refs_3_, f32[2,128]{1,0:T(2,128)S(1)} %get-tuple-element.31.refs_2_.refs_4_.refs_5_, ...), custom_call_target="tpu_custom_call" | custom-call | flops 67108864 | bytes 2884608 | tf_op jit(solution)/shard_map/pallas_call | solution.py:31
  15.2 0.1 collective-permute-start.8
  15.2 1.0 %collective-permute-start.9 = (bf16[512,128]{1,0:T(8,128)(2,1)S(1)}, bf16[512,128]{1,0:T(8,128)(2,1)S(1)}, u32[]{:S(2)}, u32[]{:S(2)}) collective-permute-start(bf16[512,128]{1,0:T(8,128)(2,1)S(1)} %get-tuple-element.35.refs_5_), channel_id=1, source_target_pairs={{0,8},{1,17},{2,10},{3,19},{4,12},{5,21},{6,14},{7,23},{8,0},{9,25... | collective-permute-start | bytes 393224 | tf_op jit(solution)/shard_map/ppermute | solution.py:171
  16.2 0.0 collective-permute-done.6.refs_1_
  16.2 1.2 %collective-permute-done.7.refs_5_ = bf16[512,128]{1,0:T(8,128)(2,1)S(1)} collective-permute-done((bf16[512,128]{1,0:T(8,128)(2,1)S(1)}, bf16[512,128]{1,0:T(8,128)(2,1)S(1)}, u32[]{:S(2)}, u32[]{:S(2)}) %collective-permute-start.7) | collective-permute-done | bytes 131104 | tf_op jit(solution)/shard_map/ppermute | solution.py:171
  17.4 0.3 %shard_map.61 = (f32[512,128]{1,0:T(8,128)S(1)}, bf16[512,128]{1,0:T(8,128)(2,1)S(1)}) custom-call(f32[512,128]{1,0:T(8,128)S(1)} %get-tuple-element.33.refs_0_, bf16[512,128]{1,0:T(8,128)(2,1)S(1)} %collective-permute-done.6.refs_1_, f32[512,8]{1,0:T(8,128)S(1)} %get-tuple-element.28.refs_3_.refs_2_, ...), custom_call_target="tpu_custom_call" | custom-call | flops 67108864 | bytes 3032064 | tf_op jit(solution)/shard_map/pallas_call | solution.py:31
  17.7 0.9 %collective-permute-start.12 = (bf16[512,128]{1,0:T(8,128)(2,1)S(1)}, bf16[512,128]{1,0:T(8,128)(2,1)S(1)}, u32[]{:S(2)}, u32[]{:S(2)}) collective-permute-start(bf16[512,128]{1,0:T(8,128)(2,1)S(1)} %get-tuple-element.36.refs_8_.refs_0_), channel_id=1, source_target_pairs={{0,16},{1,9},{2,18},{3,11},{4,20},{5,13},{6,22},{7,15},{8,24},{9,1... | collective-permute-start | bytes 393224 | tf_op jit(solution)/shard_map/ppermute | solution.py:171
  18.6 0.7 %collective-permute-start.10 = (bf16[512,128]{1,0:T(8,128)(2,1)S(1)}, bf16[512,128]{1,0:T(8,128)(2,1)S(1)}, u32[]{:S(2)}, u32[]{:S(2)}) collective-permute-start(bf16[512,128]{1,0:T(8,128)(2,1)S(1)} %get-tuple-element.35.refs_5_), channel_id=1, source_target_pairs={{0,16},{1,9},{2,18},{3,11},{4,20},{5,13},{6,22},{7,15},{8,24},{9,1... | collective-permute-start | bytes 393224 | tf_op jit(solution)/shard_map/ppermute | solution.py:171
  19.3 1.5 %collective-permute-start.11 = (bf16[512,128]{1,0:T(8,128)(2,1)S(1)}, bf16[512,128]{1,0:T(8,128)(2,1)S(1)}, u32[]{:S(2)}, u32[]{:S(2)}) collective-permute-start(bf16[512,128]{1,0:T(8,128)(2,1)S(1)} %get-tuple-element.36.refs_8_.refs_0_), channel_id=1, source_target_pairs={{0,8},{1,17},{2,10},{3,19},{4,12},{5,21},{6,14},{7,23},{8,0},{9,25... | collective-permute-start | bytes 393224 | tf_op jit(solution)/shard_map/ppermute | solution.py:171
  20.7 0.0 collective-permute-done.8.refs_2_.refs_1_
  20.8 3.2 %collective-permute-start.13 = (bf16[512,128]{1,0:T(8,128)(2,1)S(1)}, bf16[512,128]{1,0:T(8,128)(2,1)S(1)}, u32[]{:S(2)}, u32[]{:S(2)}) collective-permute-start(bf16[512,128]{1,0:T(8,128)(2,1)S(1)} %shard_map.63), channel_id=1, source_target_pairs={{1,2},{3,4},{5,6},{2,1},{4,3},{6,5},{9,10},{11,12},{13,14},{10,9},... | collective-permute-start | bytes 393224 | tf_op jit(solution)/shard_map/ppermute | solution.py:181
  24.0 0.0 collective-permute-done.9.refs_6_
  24.0 0.7 %collective-permute-start.14 = (bf16[512,128]{1,0:T(8,128)(2,1)S(1)}, bf16[512,128]{1,0:T(8,128)(2,1)S(1)}, u32[]{:S(2)}, u32[]{:S(2)}) collective-permute-start(bf16[512,128]{1,0:T(8,128)(2,1)S(1)} %collective-permute-done.9.refs_6_), channel_id=1, source_target_pairs={{0,16},{1,9},{2,18},{3,11},{4,20},{5,13},{6,22},{7,15},{8,24},{9,1... | collective-permute-start | bytes 393224 | tf_op jit(solution)/shard_map/ppermute | solution.py:171
  24.7 0.0 collective-permute-done.12.refs_10_
  24.7 1.5 %collective-permute-start.15 = (bf16[512,128]{1,0:T(8,128)(2,1)S(1)}, bf16[512,128]{1,0:T(8,128)(2,1)S(1)}, u32[]{:S(2)}, u32[]{:S(2)}) collective-permute-start(bf16[512,128]{1,0:T(8,128)(2,1)S(1)} %collective-permute-done.12.refs_10_), channel_id=1, source_target_pairs={{0,8},{1,17},{2,10},{3,19},{4,12},{5,21},{6,14},{7,23},{8,0},{9,25... | collective-permute-start | bytes 393224 | tf_op jit(solution)/shard_map/ppermute | solution.py:171
  26.2 0.0 collective-permute-done.10.refs_7_
  26.2 0.0 collective-permute-done.11.refs_9_
  26.2 1.0 %shard_map.62 = (f32[512,128]{1,0:T(8,128)S(1)}, f32[512,128]{1,0:T(8,128)S(1)}) custom-call(f32[512,128]{1,0:T(8,128)S(1)} %get-tuple-element.32.refs_0_, f32[512,128]{1,0:T(8,128)S(1)} %get-tuple-element.34.refs_1_, bf16[512,128]{1,0:T(8,128)(2,1)S(1)} %collective-permute-done.8.refs_2_.refs_1_, f32[512,8]{1,0:T(8,128)S(1)} %get-tuple-element.28.refs_3_.refs_2_, ...), custom_call_target="tpu_custom_call" | custom-call | flops 402653184 | bytes 4079616 | tf_op jit(solution)/shard_map/pallas_call | solution.py:31
  27.2 0.0 collective-permute-done.13.refs_2_
  27.2 0.6 %collective-permute-done.14.refs_6_ = bf16[512,128]{1,0:T(8,128)(2,1)S(1)} collective-permute-done((bf16[512,128]{1,0:T(8,128)(2,1)S(1)}, bf16[512,128]{1,0:T(8,128)(2,1)S(1)}, u32[]{:S(2)}, u32[]{:S(2)}) %collective-permute-start.14) | collective-permute-done | bytes 131104 | tf_op jit(solution)/shard_map/ppermute | solution.py:171
  27.9 0.7 %collective-permute-done.15.refs_7_ = bf16[512,128]{1,0:T(8,128)(2,1)S(1)} collective-permute-done((bf16[512,128]{1,0:T(8,128)(2,1)S(1)}, bf16[512,128]{1,0:T(8,128)(2,1)S(1)}, u32[]{:S(2)}, u32[]{:S(2)}) %collective-permute-start.15) | collective-permute-done | bytes 131104 | tf_op jit(solution)/shard_map/ppermute | solution.py:171
  28.6 1.2 %shard_map.64 = f32[1024,128]{1,0:T(8,128)} custom-call(f32[512,128]{1,0:T(8,128)S(1)} %get-tuple-element.37.refs_0_, f32[512,128]{1,0:T(8,128)S(1)} %get-tuple-element.38.refs_1_, bf16[512,128]{1,0:T(8,128)(2,1)S(1)} %collective-permute-done.13.refs_2_, f32[512,8]{1,0:T(8,128)S(1)} %get-tuple-element.28.refs_3_.refs_2_, ...), custom_call_target="tpu_custom_call" | custom-call | flops 134217728 | bytes 4080640 | tf_op jit(solution)/shard_map/pallas_call | solution.py:31
  (3 shorter events, 0.0 us)
Async XLA Ops:
  1.2 7.8 %collective-permute-start.2 = (bf16[512,128]{1,0:T(8,128)(2,1)S(1)}, bf16[512,128]{1,0:T(8,128)(2,1)S(1)}, u32[]{:S(2)}, u32[]{:S(2)}) collective-permute-start(bf16[512,128]{1,0:T(8,128)(2,1)S(1)} %get-tuple-element.24.refs_5_), channel_id=1, source_target_pairs={{0,16},{1,9},{2,18},{3,11},{4,20},{5,13},{6,22},{7,15},{8,24},{9,1... | collective-permute-start | bytes 393224 | tf_op jit(solution)/shard_map/ppermute | solution.py:171
  3.3 6.0 %collective-permute-start = (bf16[512,128]{1,0:T(8,128)(2,1)S(1)}, bf16[512,128]{1,0:T(8,128)(2,1)S(1)}, u32[]{:S(2)}, u32[]{:S(2)}) collective-permute-start(bf16[512,128]{1,0:T(8,128)(2,1)S(1)} %get-tuple-element.24.refs_5_), channel_id=1, source_target_pairs={{0,1},{1,0},{2,3},{3,2},{4,5},{5,4},{6,7},{7,6},{8,9},{9,8},{10,11... | collective-permute-start | bytes 393224 | tf_op jit(solution)/shard_map/ppermute | solution.py:176
  4.3 9.3 %collective-permute-start.3 = (bf16[512,128]{1,0:T(8,128)(2,1)S(1)}, bf16[512,128]{1,0:T(8,128)(2,1)S(1)}, u32[]{:S(2)}, u32[]{:S(2)}) collective-permute-start(bf16[512,128]{1,0:T(8,128)(2,1)S(1)} %get-tuple-element.25.refs_6_.refs_0_), channel_id=1, source_target_pairs={{0,8},{1,17},{2,10},{3,19},{4,12},{5,21},{6,14},{7,23},{8,0},{9,25... | collective-permute-start | bytes 393224 | tf_op jit(solution)/shard_map/ppermute | solution.py:171
  4.5 9.9 %collective-permute-start.1 = (bf16[512,128]{1,0:T(8,128)(2,1)S(1)}, bf16[512,128]{1,0:T(8,128)(2,1)S(1)}, u32[]{:S(2)}, u32[]{:S(2)}) collective-permute-start(bf16[512,128]{1,0:T(8,128)(2,1)S(1)} %get-tuple-element.24.refs_5_), channel_id=1, source_target_pairs={{0,8},{1,17},{2,10},{3,19},{4,12},{5,21},{6,14},{7,23},{8,0},{9,25... | collective-permute-start | bytes 393224 | tf_op jit(solution)/shard_map/ppermute | solution.py:171
  5.7 8.7 %collective-permute-start.4 = (bf16[512,128]{1,0:T(8,128)(2,1)S(1)}, bf16[512,128]{1,0:T(8,128)(2,1)S(1)}, u32[]{:S(2)}, u32[]{:S(2)}) collective-permute-start(bf16[512,128]{1,0:T(8,128)(2,1)S(1)} %get-tuple-element.25.refs_6_.refs_0_), channel_id=1, source_target_pairs={{0,16},{1,9},{2,18},{3,11},{4,20},{5,13},{6,22},{7,15},{8,24},{9,1... | collective-permute-start | bytes 393224 | tf_op jit(solution)/shard_map/ppermute | solution.py:171
  9.0 5.9 %collective-permute-start.5 = (bf16[512,128]{1,0:T(8,128)(2,1)S(1)}, bf16[512,128]{1,0:T(8,128)(2,1)S(1)}, u32[]{:S(2)}, u32[]{:S(2)}) collective-permute-start(bf16[512,128]{1,0:T(8,128)(2,1)S(1)} %shard_map.58), channel_id=1, source_target_pairs={{0,8},{1,17},{2,10},{3,19},{4,12},{5,21},{6,14},{7,23},{8,0},{9,25... | collective-permute-start | bytes 393224 | tf_op jit(solution)/shard_map/ppermute | solution.py:171
  9.3 6.9 %collective-permute-start.6 = (bf16[512,128]{1,0:T(8,128)(2,1)S(1)}, bf16[512,128]{1,0:T(8,128)(2,1)S(1)}, u32[]{:S(2)}, u32[]{:S(2)}) collective-permute-start(bf16[512,128]{1,0:T(8,128)(2,1)S(1)} %shard_map.60), channel_id=1, source_target_pairs={{1,2},{3,4},{5,6},{2,1},{4,3},{6,5},{9,10},{11,12},{13,14},{10,9},... | collective-permute-start | bytes 393224 | tf_op jit(solution)/shard_map/ppermute | solution.py:181
  13.5 3.9 %collective-permute-start.7 = (bf16[512,128]{1,0:T(8,128)(2,1)S(1)}, bf16[512,128]{1,0:T(8,128)(2,1)S(1)}, u32[]{:S(2)}, u32[]{:S(2)}) collective-permute-start(bf16[512,128]{1,0:T(8,128)(2,1)S(1)} %collective-permute-done.3.refs_7_), channel_id=1, source_target_pairs={{0,16},{1,9},{2,18},{3,11},{4,20},{5,13},{6,22},{7,15},{8,24},{9,1... | collective-permute-start | bytes 393224 | tf_op jit(solution)/shard_map/ppermute | solution.py:171
  15.2 5.6 %collective-permute-start.8 = (bf16[512,128]{1,0:T(8,128)(2,1)S(1)}, bf16[512,128]{1,0:T(8,128)(2,1)S(1)}, u32[]{:S(2)}, u32[]{:S(2)}) collective-permute-start(bf16[512,128]{1,0:T(8,128)(2,1)S(1)} %get-tuple-element.35.refs_5_), channel_id=1, source_target_pairs={{0,1},{1,0},{2,3},{3,2},{4,5},{5,4},{6,7},{7,6},{8,9},{9,8},{10,11... | collective-permute-start | bytes 393224 | tf_op jit(solution)/shard_map/ppermute | solution.py:176
  15.2 8.7 %collective-permute-start.9 = (bf16[512,128]{1,0:T(8,128)(2,1)S(1)}, bf16[512,128]{1,0:T(8,128)(2,1)S(1)}, u32[]{:S(2)}, u32[]{:S(2)}) collective-permute-start(bf16[512,128]{1,0:T(8,128)(2,1)S(1)} %get-tuple-element.35.refs_5_), channel_id=1, source_target_pairs={{0,8},{1,17},{2,10},{3,19},{4,12},{5,21},{6,14},{7,23},{8,0},{9,25... | collective-permute-start | bytes 393224 | tf_op jit(solution)/shard_map/ppermute | solution.py:171
  17.7 7.0 %collective-permute-start.12 = (bf16[512,128]{1,0:T(8,128)(2,1)S(1)}, bf16[512,128]{1,0:T(8,128)(2,1)S(1)}, u32[]{:S(2)}, u32[]{:S(2)}) collective-permute-start(bf16[512,128]{1,0:T(8,128)(2,1)S(1)} %get-tuple-element.36.refs_8_.refs_0_), channel_id=1, source_target_pairs={{0,16},{1,9},{2,18},{3,11},{4,20},{5,13},{6,22},{7,15},{8,24},{9,1... | collective-permute-start | bytes 393224 | tf_op jit(solution)/shard_map/ppermute | solution.py:171
  18.6 7.6 %collective-permute-start.10 = (bf16[512,128]{1,0:T(8,128)(2,1)S(1)}, bf16[512,128]{1,0:T(8,128)(2,1)S(1)}, u32[]{:S(2)}, u32[]{:S(2)}) collective-permute-start(bf16[512,128]{1,0:T(8,128)(2,1)S(1)} %get-tuple-element.35.refs_5_), channel_id=1, source_target_pairs={{0,16},{1,9},{2,18},{3,11},{4,20},{5,13},{6,22},{7,15},{8,24},{9,1... | collective-permute-start | bytes 393224 | tf_op jit(solution)/shard_map/ppermute | solution.py:171
  19.3 7.0 %collective-permute-start.11 = (bf16[512,128]{1,0:T(8,128)(2,1)S(1)}, bf16[512,128]{1,0:T(8,128)(2,1)S(1)}, u32[]{:S(2)}, u32[]{:S(2)}) collective-permute-start(bf16[512,128]{1,0:T(8,128)(2,1)S(1)} %get-tuple-element.36.refs_8_.refs_0_), channel_id=1, source_target_pairs={{0,8},{1,17},{2,10},{3,19},{4,12},{5,21},{6,14},{7,23},{8,0},{9,25... | collective-permute-start | bytes 393224 | tf_op jit(solution)/shard_map/ppermute | solution.py:171
  20.8 6.5 %collective-permute-start.13 = (bf16[512,128]{1,0:T(8,128)(2,1)S(1)}, bf16[512,128]{1,0:T(8,128)(2,1)S(1)}, u32[]{:S(2)}, u32[]{:S(2)}) collective-permute-start(bf16[512,128]{1,0:T(8,128)(2,1)S(1)} %shard_map.63), channel_id=1, source_target_pairs={{1,2},{3,4},{5,6},{2,1},{4,3},{6,5},{9,10},{11,12},{13,14},{10,9},... | collective-permute-start | bytes 393224 | tf_op jit(solution)/shard_map/ppermute | solution.py:181
  24.0 3.9 %collective-permute-start.14 = (bf16[512,128]{1,0:T(8,128)(2,1)S(1)}, bf16[512,128]{1,0:T(8,128)(2,1)S(1)}, u32[]{:S(2)}, u32[]{:S(2)}) collective-permute-start(bf16[512,128]{1,0:T(8,128)(2,1)S(1)} %collective-permute-done.9.refs_6_), channel_id=1, source_target_pairs={{0,16},{1,9},{2,18},{3,11},{4,20},{5,13},{6,22},{7,15},{8,24},{9,1... | collective-permute-start | bytes 393224 | tf_op jit(solution)/shard_map/ppermute | solution.py:171
  24.7 3.8 %collective-permute-start.15 = (bf16[512,128]{1,0:T(8,128)(2,1)S(1)}, bf16[512,128]{1,0:T(8,128)(2,1)S(1)}, u32[]{:S(2)}, u32[]{:S(2)}) collective-permute-start(bf16[512,128]{1,0:T(8,128)(2,1)S(1)} %collective-permute-done.12.refs_10_), channel_id=1, source_target_pairs={{0,8},{1,17},{2,10},{3,19},{4,12},{5,21},{6,14},{7,23},{8,0},{9,25... | collective-permute-start | bytes 393224 | tf_op jit(solution)/shard_map/ppermute | solution.py:171

commit v9 on v7

--- a/solution.py
+++ b/solution.py
@@ -234,7 +234,7 @@
     run(blocks, range(last, rows), False, [k for k in far if k[1] == last], ["outer"], True, False)
 
     env["inner"] = within_pair(env["q0"])
-    blocks = [exchange(env[f"q{r}"], orders[r], count) for r in range(rows)]
+    blocks = [exchange(env[f"q{r}"], orders[r], count, env["inner"] if r == last else None) for r in range(rows)]
     env["outer"] = between_pairs(held(env[f"q{last}"], env["inner"]))
     run(blocks, range(rows), True, near, ["inner"], False, True)
     run(blocks, range(rows), False, far, ["outer"], True, True)

time: 30 us -> 30 us (level)
    pallas_call x10 -> x11, Pallas kernels: 6.39 us -> 6.39 us  [call(): pl.pallas_call(kernel, out_shape=list(outs.values()), in_specs=[HBM if n...]
where the time goes in v9:
time: 30 us; the launch traced here: 29.8 us
  starting transfers between devices  21.2 us (71%)
  Pallas kernels  6.39 us (21%)
  waiting for transfers between devices  2.11 us (7%)
    ppermute x12, starting transfers between devices, exchange(): blocks[offset ^ bit] = lax.ppermute(block, ('mode', 'cell'), pairs)  13 us
    ppermute x2, starting transfers between devices, between_pairs(): lax.ppermute(row, 'cell', steps + [(target, source) for source, target in...  7.18 us
    pallas_call x11, Pallas kernels, call(): pl.pallas_call(kernel, out_shape=list(outs.values()), in_specs=[HBM if n...  6.39 us
    ppermute x12, waiting for transfers between devices, exchange(): blocks[offset ^ bit] = lax.ppermute(block, ('mode', 'cell'), pairs)  2.1 us
    ppermute x2, starting transfers between devices, within_pair(): lax.ppermute(row, 'cell', [(i, i ^ 1) for i in range(lax.axis_size('cell'...  1.05 us
  transfers between devices with their start and end apart: 16, of which 3 were waited for; matrix products, arithmetic and copies ran while one was open for 0% of the time, Pallas kernels for 14%

profile of v9, /device:TPU:1, one launch (start us, length us, event | category | flops | bytes accessed | tf_op | source)
XLA Modules:
  0.0 29.8 jit_solution(10802656339322816150)
XLA Ops:
  0.0 1.2 %shard_map.55 = (f32[2,128]{1,0:T(2,128)S(1)}, f32[512,128]{1,0:T(8,128)S(1)}, bf16[512,128]{1,0:T(8,128)(2,1)S(1)}, f32[512,128]{1,0:T(8,128)S(1)}, bf16[512,128]{1,0:T(8,128)(2,1)S(1)}) custom-call(f32[1024,128]{1,0:T(8,128)} %bitcast.6, s32[2,128]{1,0:T(2,128)} %bitcast.8), custom_call_target="tpu_custom_call" | custom-call | bytes 1312768 | tf_op jit(solution)/shard_map/pallas_call | solution.py:31
  1.2 2.1 %collective-permute-start.2 = (bf16[512,128]{1,0:T(8,128)(2,1)S(1)}, bf16[512,128]{1,0:T(8,128)(2,1)S(1)}, u32[]{:S(2)}, u32[]{:S(2)}) collective-permute-start(bf16[512,128]{1,0:T(8,128)(2,1)S(1)} %get-tuple-element.26.refs_5_), channel_id=1, source_target_pairs={{0,16},{1,9},{2,18},{3,11},{4,20},{5,13},{6,22},{7,15},{8,24},{9,1... | collective-permute-start | bytes 393224 | tf_op jit(solution)/shard_map/ppermute | solution.py:168
  3.3 1.0 %collective-permute-start = (bf16[512,128]{1,0:T(8,128)(2,1)S(1)}, bf16[512,128]{1,0:T(8,128)(2,1)S(1)}, u32[]{:S(2)}, u32[]{:S(2)}) collective-permute-start(bf16[512,128]{1,0:T(8,128)(2,1)S(1)} %get-tuple-element.26.refs_5_), channel_id=1, source_target_pairs={{0,1},{1,0},{2,3},{3,2},{4,5},{5,4},{6,7},{7,6},{8,9},{9,8},{10,11... | collective-permute-start | bytes 393224 | tf_op jit(solution)/shard_map/ppermute | solution.py:173
  4.3 0.3 collective-permute-start.3
  4.5 1.2 %collective-permute-start.1 = (bf16[512,128]{1,0:T(8,128)(2,1)S(1)}, bf16[512,128]{1,0:T(8,128)(2,1)S(1)}, u32[]{:S(2)}, u32[]{:S(2)}) collective-permute-start(bf16[512,128]{1,0:T(8,128)(2,1)S(1)} %get-tuple-element.26.refs_5_), channel_id=1, source_target_pairs={{0,8},{1,17},{2,10},{3,19},{4,12},{5,21},{6,14},{7,23},{8,0},{9,25... | collective-permute-start | bytes 393224 | tf_op jit(solution)/shard_map/ppermute | solution.py:168
  5.7 1.2 %collective-permute-start.4 = (bf16[512,128]{1,0:T(8,128)(2,1)S(1)}, bf16[512,128]{1,0:T(8,128)(2,1)S(1)}, u32[]{:S(2)}, u32[]{:S(2)}) collective-permute-start(bf16[512,128]{1,0:T(8,128)(2,1)S(1)} %get-tuple-element.29.refs_8_.refs_0_), channel_id=1, source_target_pairs={{0,16},{1,9},{2,18},{3,11},{4,20},{5,13},{6,22},{7,15},{8,24},{9,1... | collective-permute-start | bytes 393224 | tf_op jit(solution)/shard_map/ppermute | solution.py:168
  6.9 1.7 %shard_map.56 = (bf16[512,2048]{1,0:T(8,128)(2,1)S(1)}, f32[512,8]{1,0:T(8,128)S(1)}, f32[512,128]{1,0:T(8,128)S(1)}, f32[512,128]{1,0:T(8,128)S(1)}) custom-call(s32[1,512]{1,0:T(1,128)} %bitcast.7, f32[3,512]{1,0:T(4,128)} %refs_1_.1, bf16[512,2048]{1,0:T(8,128)(2,1)} %refs_2_.1, f32[512,128]{1,0:T(8,128)S(1)} %get-tuple-element.22.refs_3_.refs_8_, ...), custom_call_target="tpu_custom_call" | custom-call | bytes 5267456 | tf_op jit(solution)/shard_map/pallas_call | solution.py:31
  8.7 0.0 collective-permute-done.2.refs_7_.refs_0_
  8.7 0.3 collective-permute-start.5
  9.0 0.0 collective-permute-done.refs_2_.refs_1_
  9.0 4.2 %collective-permute-start.6 = (bf16[512,128]{1,0:T(8,128)(2,1)S(1)}, bf16[512,128]{1,0:T(8,128)(2,1)S(1)}, u32[]{:S(2)}, u32[]{:S(2)}) collective-permute-start(bf16[512,128]{1,0:T(8,128)(2,1)S(1)} %shard_map.60), channel_id=1, source_target_pairs={{1,2},{3,4},{5,6},{2,1},{4,3},{6,5},{9,10},{11,12},{13,14},{10,9},... | collective-permute-start | bytes 393224 | tf_op jit(solution)/shard_map/ppermute | solution.py:178
  13.3 0.0 collective-permute-done.3.refs_9_
  13.3 0.9 %collective-permute-start.7 = (bf16[512,128]{1,0:T(8,128)(2,1)S(1)}, bf16[512,128]{1,0:T(8,128)(2,1)S(1)}, u32[]{:S(2)}, u32[]{:S(2)}) collective-permute-start(bf16[512,128]{1,0:T(8,128)(2,1)S(1)} %collective-permute-done.3.refs_9_), channel_id=1, source_target_pairs={{0,16},{1,9},{2,18},{3,11},{4,20},{5,13},{6,22},{7,15},{8,24},{9,1... | collective-permute-start | bytes 393224 | tf_op jit(solution)/shard_map/ppermute | solution.py:168
  14.1 0.0 collective-permute-done.1.refs_6_
  14.1 0.0 collective-permute-done.4.refs_10_
  14.1 0.6 %shard_map.57 = (f32[512,128]{1,0:T(8,128)S(1)}, f32[512,128]{1,0:T(8,128)S(1)}) custom-call(f32[512,128]{1,0:T(8,128)S(1)} %get-tuple-element.24.refs_0_, f32[512,128]{1,0:T(8,128)S(1)} %get-tuple-element.25.refs_1_, bf16[512,128]{1,0:T(8,128)(2,1)S(1)} %collective-permute-done.refs_2_.refs_1_, f32[512,8]{1,0:T(8,128)S(1)} %get-tuple-element.27.refs_3_.refs_2_, ...), custom_call_target="tpu_custom_call" | custom-call | flops 402653184 | bytes 4079616 | tf_op jit(solution)/shard_map/pallas_call | solution.py:31
  14.7 0.0 collective-permute-done.5.refs_3_
  14.8 0.3 shard_map.59
  15.1 0.1 collective-permute-start.8
  15.1 1.2 %collective-permute-start.9 = (bf16[512,128]{1,0:T(8,128)(2,1)S(1)}, bf16[512,128]{1,0:T(8,128)(2,1)S(1)}, u32[]{:S(2)}, u32[]{:S(2)}) collective-permute-start(bf16[512,128]{1,0:T(8,128)(2,1)S(1)} %get-tuple-element.35.refs_5_), channel_id=1, source_target_pairs={{0,8},{1,17},{2,10},{3,19},{4,12},{5,21},{6,14},{7,23},{8,0},{9,25... | collective-permute-start | bytes 393224 | tf_op jit(solution)/shard_map/ppermute | solution.py:168
  16.4 0.0 collective-permute-done.6.refs_1_
  16.4 0.8 %collective-permute-done.7.refs_5_ = bf16[512,128]{1,0:T(8,128)(2,1)S(1)} collective-permute-done((bf16[512,128]{1,0:T(8,128)(2,1)S(1)}, bf16[512,128]{1,0:T(8,128)(2,1)S(1)}, u32[]{:S(2)}, u32[]{:S(2)}) %collective-permute-start.7) | collective-permute-done | bytes 131104 | tf_op jit(solution)/shard_map/ppermute | solution.py:168
  17.2 0.3 %shard_map.61 = (f32[512,128]{1,0:T(8,128)S(1)}, bf16[512,128]{1,0:T(8,128)(2,1)S(1)}) custom-call(f32[512,128]{1,0:T(8,128)S(1)} %get-tuple-element.33.refs_0_, bf16[512,128]{1,0:T(8,128)(2,1)S(1)} %collective-permute-done.6.refs_1_, f32[512,8]{1,0:T(8,128)S(1)} %get-tuple-element.27.refs_3_.refs_2_, ...), custom_call_target="tpu_custom_call" | custom-call | flops 67108864 | bytes 3032064 | tf_op jit(solution)/shard_map/pallas_call | solution.py:31
  17.5 0.9 %collective-permute-start.12 = (bf16[512,128]{1,0:T(8,128)(2,1)S(1)}, bf16[512,128]{1,0:T(8,128)(2,1)S(1)}, u32[]{:S(2)}, u32[]{:S(2)}) collective-permute-start(bf16[512,128]{1,0:T(8,128)(2,1)S(1)} %get-tuple-element.36.refs_8_.refs_0_), channel_id=1, source_target_pairs={{0,16},{1,9},{2,18},{3,11},{4,20},{5,13},{6,22},{7,15},{8,24},{9,1... | collective-permute-start | bytes 393224 | tf_op jit(solution)/shard_map/ppermute | solution.py:168
  18.3 0.7 %collective-permute-start.10 = (bf16[512,128]{1,0:T(8,128)(2,1)S(1)}, bf16[512,128]{1,0:T(8,128)(2,1)S(1)}, u32[]{:S(2)}, u32[]{:S(2)}) collective-permute-start(bf16[512,128]{1,0:T(8,128)(2,1)S(1)} %get-tuple-element.35.refs_5_), channel_id=1, source_target_pairs={{0,16},{1,9},{2,18},{3,11},{4,20},{5,13},{6,22},{7,15},{8,24},{9,1... | collective-permute-start | bytes 393224 | tf_op jit(solution)/shard_map/ppermute | solution.py:168
  19.0 1.7 %collective-permute-start.11 = (bf16[512,128]{1,0:T(8,128)(2,1)S(1)}, bf16[512,128]{1,0:T(8,128)(2,1)S(1)}, u32[]{:S(2)}, u32[]{:S(2)}) collective-permute-start(bf16[512,128]{1,0:T(8,128)(2,1)S(1)} %get-tuple-element.36.refs_8_.refs_0_), channel_id=1, source_target_pairs={{0,8},{1,17},{2,10},{3,19},{4,12},{5,21},{6,14},{7,23},{8,0},{9,25... | collective-permute-start | bytes 393224 | tf_op jit(solution)/shard_map/ppermute | solution.py:168
  20.8 0.0 collective-permute-done.8.refs_2_.refs_1_
  20.8 3.0 %collective-permute-start.13 = (bf16[512,128]{1,0:T(8,128)(2,1)S(1)}, bf16[512,128]{1,0:T(8,128)(2,1)S(1)}, u32[]{:S(2)}, u32[]{:S(2)}) collective-permute-start(bf16[512,128]{1,0:T(8,128)(2,1)S(1)} %shard_map.63), channel_id=1, source_target_pairs={{1,2},{3,4},{5,6},{2,1},{4,3},{6,5},{9,10},{11,12},{13,14},{10,9},... | collective-permute-start | bytes 393224 | tf_op jit(solution)/shard_map/ppermute | solution.py:178
  23.7 0.0 collective-permute-done.9.refs_6_
  23.7 0.8 %collective-permute-start.14 = (bf16[512,128]{1,0:T(8,128)(2,1)S(1)}, bf16[512,128]{1,0:T(8,128)(2,1)S(1)}, u32[]{:S(2)}, u32[]{:S(2)}) collective-permute-start(bf16[512,128]{1,0:T(8,128)(2,1)S(1)} %collective-permute-done.9.refs_6_), channel_id=1, source_target_pairs={{0,16},{1,9},{2,18},{3,11},{4,20},{5,13},{6,22},{7,15},{8,24},{9,1... | collective-permute-start | bytes 393224 | tf_op jit(solution)/shard_map/ppermute | solution.py:168
  24.6 0.0 collective-permute-done.12.refs_10_.refs_0_
  24.6 1.7 %collective-permute-start.15 = (bf16[512,128]{1,0:T(8,128)(2,1)S(1)}, bf16[512,128]{1,0:T(8,128)(2,1)S(1)}, u32[]{:S(2)}, u32[]{:S(2)}) collective-permute-start(bf16[512,128]{1,0:T(8,128)(2,1)S(1)} %shard_map.64), channel_id=1, source_target_pairs={{0,8},{1,17},{2,10},{3,19},{4,12},{5,21},{6,14},{7,23},{8,0},{9,25... | collective-permute-start | bytes 393224 | tf_op jit(solution)/shard_map/ppermute | solution.py:168
  26.3 0.0 collective-permute-done.10.refs_7_
  26.3 0.0 collective-permute-done.11.refs_9_
  26.3 1.0 %shard_map.62 = (f32[512,128]{1,0:T(8,128)S(1)}, f32[512,128]{1,0:T(8,128)S(1)}) custom-call(f32[512,128]{1,0:T(8,128)S(1)} %get-tuple-element.32.refs_0_, f32[512,128]{1,0:T(8,128)S(1)} %get-tuple-element.34.refs_1_, bf16[512,128]{1,0:T(8,128)(2,1)S(1)} %collective-permute-done.8.refs_2_.refs_1_, f32[512,8]{1,0:T(8,128)S(1)} %get-tuple-element.27.refs_3_.refs_2_, ...), custom_call_target="tpu_custom_call" | custom-call | flops 402653184 | bytes 4079616 | tf_op jit(solution)/shard_map/pallas_call | solution.py:31
  27.4 0.0 collective-permute-done.13.refs_2_
  27.4 0.7 %collective-permute-done.14.refs_6_ = bf16[512,128]{1,0:T(8,128)(2,1)S(1)} collective-permute-done((bf16[512,128]{1,0:T(8,128)(2,1)S(1)}, bf16[512,128]{1,0:T(8,128)(2,1)S(1)}, u32[]{:S(2)}, u32[]{:S(2)}) %collective-permute-start.14) | collective-permute-done | bytes 131104 | tf_op jit(solution)/shard_map/ppermute | solution.py:168
  28.1 0.6 %collective-permute-done.15.refs_7_ = bf16[512,128]{1,0:T(8,128)(2,1)S(1)} collective-permute-done((bf16[512,128]{1,0:T(8,128)(2,1)S(1)}, bf16[512,128]{1,0:T(8,128)(2,1)S(1)}, u32[]{:S(2)}, u32[]{:S(2)}) %collective-permute-start.15) | collective-permute-done | bytes 131104 | tf_op jit(solution)/shard_map/ppermute | solution.py:168
  28.7 1.2 %shard_map.65 = f32[1024,128]{1,0:T(8,128)} custom-call(f32[512,128]{1,0:T(8,128)S(1)} %get-tuple-element.37.refs_0_, f32[512,128]{1,0:T(8,128)S(1)} %get-tuple-element.38.refs_1_, bf16[512,128]{1,0:T(8,128)(2,1)S(1)} %collective-permute-done.13.refs_2_, f32[512,8]{1,0:T(8,128)S(1)} %get-tuple-element.27.refs_3_.refs_2_, ...), custom_call_target="tpu_custom_call" | custom-call | flops 134217728 | bytes 4080640 | tf_op jit(solution)/shard_map/pallas_call | solution.py:31
  (4 shorter events, 0.0 us)
Async XLA Ops:
  1.2 7.5 %collective-permute-start.2 = (bf16[512,128]{1,0:T(8,128)(2,1)S(1)}, bf16[512,128]{1,0:T(8,128)(2,1)S(1)}, u32[]{:S(2)}, u32[]{:S(2)}) collective-permute-start(bf16[512,128]{1,0:T(8,128)(2,1)S(1)} %get-tuple-element.26.refs_5_), channel_id=1, source_target_pairs={{0,16},{1,9},{2,18},{3,11},{4,20},{5,13},{6,22},{7,15},{8,24},{9,1... | collective-permute-start | bytes 393224 | tf_op jit(solution)/shard_map/ppermute | solution.py:168
  3.3 5.7 %collective-permute-start = (bf16[512,128]{1,0:T(8,128)(2,1)S(1)}, bf16[512,128]{1,0:T(8,128)(2,1)S(1)}, u32[]{:S(2)}, u32[]{:S(2)}) collective-permute-start(bf16[512,128]{1,0:T(8,128)(2,1)S(1)} %get-tuple-element.26.refs_5_), channel_id=1, source_target_pairs={{0,1},{1,0},{2,3},{3,2},{4,5},{5,4},{6,7},{7,6},{8,9},{9,8},{10,11... | collective-permute-start | bytes 393224 | tf_op jit(solution)/shard_map/ppermute | solution.py:173
  4.3 9.0 %collective-permute-start.3 = (bf16[512,128]{1,0:T(8,128)(2,1)S(1)}, bf16[512,128]{1,0:T(8,128)(2,1)S(1)}, u32[]{:S(2)}, u32[]{:S(2)}) collective-permute-start(bf16[512,128]{1,0:T(8,128)(2,1)S(1)} %get-tuple-element.29.refs_8_.refs_0_), channel_id=1, source_target_pairs={{0,8},{1,17},{2,10},{3,19},{4,12},{5,21},{6,14},{7,23},{8,0},{9,25... | collective-permute-start | bytes 393224 | tf_op jit(solution)/shard_map/ppermute | solution.py:168
  4.5 9.6 %collective-permute-start.1 = (bf16[512,128]{1,0:T(8,128)(2,1)S(1)}, bf16[512,128]{1,0:T(8,128)(2,1)S(1)}, u32[]{:S(2)}, u32[]{:S(2)}) collective-permute-start(bf16[512,128]{1,0:T(8,128)(2,1)S(1)} %get-tuple-element.26.refs_5_), channel_id=1, source_target_pairs={{0,8},{1,17},{2,10},{3,19},{4,12},{5,21},{6,14},{7,23},{8,0},{9,25... | collective-permute-start | bytes 393224 | tf_op jit(solution)/shard_map/ppermute | solution.py:168
  5.7 8.4 %collective-permute-start.4 = (bf16[512,128]{1,0:T(8,128)(2,1)S(1)}, bf16[512,128]{1,0:T(8,128)(2,1)S(1)}, u32[]{:S(2)}, u32[]{:S(2)}) collective-permute-start(bf16[512,128]{1,0:T(8,128)(2,1)S(1)} %get-tuple-element.29.refs_8_.refs_0_), channel_id=1, source_target_pairs={{0,16},{1,9},{2,18},{3,11},{4,20},{5,13},{6,22},{7,15},{8,24},{9,1... | collective-permute-start | bytes 393224 | tf_op jit(solution)/shard_map/ppermute | solution.py:168
  8.7 6.0 %collective-permute-start.5 = (bf16[512,128]{1,0:T(8,128)(2,1)S(1)}, bf16[512,128]{1,0:T(8,128)(2,1)S(1)}, u32[]{:S(2)}, u32[]{:S(2)}) collective-permute-start(bf16[512,128]{1,0:T(8,128)(2,1)S(1)} %shard_map.58), channel_id=1, source_target_pairs={{0,8},{1,17},{2,10},{3,19},{4,12},{5,21},{6,14},{7,23},{8,0},{9,25... | collective-permute-start | bytes 393224 | tf_op jit(solution)/shard_map/ppermute | solution.py:168
  9.0 7.3 %collective-permute-start.6 = (bf16[512,128]{1,0:T(8,128)(2,1)S(1)}, bf16[512,128]{1,0:T(8,128)(2,1)S(1)}, u32[]{:S(2)}, u32[]{:S(2)}) collective-permute-start(bf16[512,128]{1,0:T(8,128)(2,1)S(1)} %shard_map.60), channel_id=1, source_target_pairs={{1,2},{3,4},{5,6},{2,1},{4,3},{6,5},{9,10},{11,12},{13,14},{10,9},... | collective-permute-start | bytes 393224 | tf_op jit(solution)/shard_map/ppermute | solution.py:178
  13.3 3.9 %collective-permute-start.7 = (bf16[512,128]{1,0:T(8,128)(2,1)S(1)}, bf16[512,128]{1,0:T(8,128)(2,1)S(1)}, u32[]{:S(2)}, u32[]{:S(2)}) collective-permute-start(bf16[512,128]{1,0:T(8,128)(2,1)S(1)} %collective-permute-done.3.refs_9_), channel_id=1, source_target_pairs={{0,16},{1,9},{2,18},{3,11},{4,20},{5,13},{6,22},{7,15},{8,24},{9,1... | collective-permute-start | bytes 393224 | tf_op jit(solution)/shard_map/ppermute | solution.py:168
  15.1 5.7 %collective-permute-start.8 = (bf16[512,128]{1,0:T(8,128)(2,1)S(1)}, bf16[512,128]{1,0:T(8,128)(2,1)S(1)}, u32[]{:S(2)}, u32[]{:S(2)}) collective-permute-start(bf16[512,128]{1,0:T(8,128)(2,1)S(1)} %get-tuple-element.35.refs_5_), channel_id=1, source_target_pairs={{0,1},{1,0},{2,3},{3,2},{4,5},{5,4},{6,7},{7,6},{8,9},{9,8},{10,11... | collective-permute-start | bytes 393224 | tf_op jit(solution)/shard_map/ppermute | solution.py:173
  15.1 8.6 %collective-permute-start.9 = (bf16[512,128]{1,0:T(8,128)(2,1)S(1)}, bf16[512,128]{1,0:T(8,128)(2,1)S(1)}, u32[]{:S(2)}, u32[]{:S(2)}) collective-permute-start(bf16[512,128]{1,0:T(8,128)(2,1)S(1)} %get-tuple-element.35.refs_5_), channel_id=1, source_target_pairs={{0,8},{1,17},{2,10},{3,19},{4,12},{5,21},{6,14},{7,23},{8,0},{9,25... | collective-permute-start | bytes 393224 | tf_op jit(solution)/shard_map/ppermute | solution.py:168
  17.5 7.1 %collective-permute-start.12 = (bf16[512,128]{1,0:T(8,128)(2,1)S(1)}, bf16[512,128]{1,0:T(8,128)(2,1)S(1)}, u32[]{:S(2)}, u32[]{:S(2)}) collective-permute-start(bf16[512,128]{1,0:T(8,128)(2,1)S(1)} %get-tuple-element.36.refs_8_.refs_0_), channel_id=1, source_target_pairs={{0,16},{1,9},{2,18},{3,11},{4,20},{5,13},{6,22},{7,15},{8,24},{9,1... | collective-permute-start | bytes 393224 | tf_op jit(solution)/shard_map/ppermute | solution.py:168
  18.3 8.0 %collective-permute-start.10 = (bf16[512,128]{1,0:T(8,128)(2,1)S(1)}, bf16[512,128]{1,0:T(8,128)(2,1)S(1)}, u32[]{:S(2)}, u32[]{:S(2)}) collective-permute-start(bf16[512,128]{1,0:T(8,128)(2,1)S(1)} %get-tuple-element.35.refs_5_), channel_id=1, source_target_pairs={{0,16},{1,9},{2,18},{3,11},{4,20},{5,13},{6,22},{7,15},{8,24},{9,1... | collective-permute-start | bytes 393224 | tf_op jit(solution)/shard_map/ppermute | solution.py:168
  19.0 7.3 %collective-permute-start.11 = (bf16[512,128]{1,0:T(8,128)(2,1)S(1)}, bf16[512,128]{1,0:T(8,128)(2,1)S(1)}, u32[]{:S(2)}, u32[]{:S(2)}) collective-permute-start(bf16[512,128]{1,0:T(8,128)(2,1)S(1)} %get-tuple-element.36.refs_8_.refs_0_), channel_id=1, source_target_pairs={{0,8},{1,17},{2,10},{3,19},{4,12},{5,21},{6,14},{7,23},{8,0},{9,25... | collective-permute-start | bytes 393224 | tf_op jit(solution)/shard_map/ppermute | solution.py:168
  20.8 6.6 %collective-permute-start.13 = (bf16[512,128]{1,0:T(8,128)(2,1)S(1)}, bf16[512,128]{1,0:T(8,128)(2,1)S(1)}, u32[]{:S(2)}, u32[]{:S(2)}) collective-permute-start(bf16[512,128]{1,0:T(8,128)(2,1)S(1)} %shard_map.63), channel_id=1, source_target_pairs={{1,2},{3,4},{5,6},{2,1},{4,3},{6,5},{9,10},{11,12},{13,14},{10,9},... | collective-permute-start | bytes 393224 | tf_op jit(solution)/shard_map/ppermute | solution.py:178
  23.7 4.3 %collective-permute-start.14 = (bf16[512,128]{1,0:T(8,128)(2,1)S(1)}, bf16[512,128]{1,0:T(8,128)(2,1)S(1)}, u32[]{:S(2)}, u32[]{:S(2)}) collective-permute-start(bf16[512,128]{1,0:T(8,128)(2,1)S(1)} %collective-permute-done.9.refs_6_), channel_id=1, source_target_pairs={{0,16},{1,9},{2,18},{3,11},{4,20},{5,13},{6,22},{7,15},{8,24},{9,1... | collective-permute-start | bytes 393224 | tf_op jit(solution)/shard_map/ppermute | solution.py:168
  24.6 4.1 %collective-permute-start.15 = (bf16[512,128]{1,0:T(8,128)(2,1)S(1)}, bf16[512,128]{1,0:T(8,128)(2,1)S(1)}, u32[]{:S(2)}, u32[]{:S(2)}) collective-permute-start(bf16[512,128]{1,0:T(8,128)(2,1)S(1)} %shard_map.64), channel_id=1, source_target_pairs={{0,8},{1,17},{2,10},{3,19},{4,12},{5,21},{6,14},{7,23},{8,0},{9,25... | collective-permute-start | bytes 393224 | tf_op jit(solution)/shard_map/ppermute | solution.py:168
